TPU v7x, 256 devices: a whole 4x4x8 slice. The times are simulated.
256 devices in a mesh: sec: 2 (over x_lo), dom: 128 (over x_hi, y, z, core).
Axes of the slice: x: 4 (x_hi: 2, x_lo: 2; x = x_hi * 2 + x_lo), y: 4, z: 8, core: 2. Of those that a mesh axis runs over, the one named last changes fastest.
Arguments:
- velocity: float32 [256, 3, 32, 32, 128], P(('sec', 'dom')), may hold values from -6 to 6
- first_kernel: bfloat16 [3, 3, 3, 3, 64], replicated, may hold values from -0.625 to 0.625
- norm_gain: float32 [64], replicated, may hold values from 0.5 to 1.5
- second_kernel: bfloat16 [3, 3, 3, 64, 128], replicated, may hold values from -0.15625 to 0.15625
- head_weight: bfloat16 [128, 6], replicated, may hold values from -0.5 to 0.5
- selection: int32 [256, 1], P(('sec', 'dom')), may hold values from 0 to 3
- assignment: int32 [256, 1], replicated, may hold values from 0 to 255, as said below
- target_stress: bfloat16 [256, 1, 3072], P(('sec', 'dom')), may hold values from -6 to 6
Outputs:
- pressure: float32 [256, 32, 32, 128], P(('sec', 'dom'))
- predicted_stress: bfloat16 [256, 1, 3072], P(('sec', 'dom'))
- first_gradient: float32 [3, 3, 3, 3, 64], replicated
- gain_gradient: float32 [64], replicated
- second_gradient: float32 [3, 3, 3, 64, 128], replicated
- head_gradient: float32 [128, 6], replicated
Inputs may be any that keep to these rules, and one draw needn't show every extreme that they name: `selection`: local block numbers of one subdomain. `assignment`: every network device is named exactly 1 times in the whole table.
All inputs are finite; a program needn't handle non-finite values.
Results may differ from a plain program's by a relative error of at most 0.011.
Values may be sent and summed in bfloat16 or wider, within the bound.
A program may use at most 128 MiB of HBM per device.

v0:
```python
import jax
import jax.numpy as jnp
from jax import lax
from jax.sharding import PartitionSpec as P

BE = 32
OV = 2
SWEEPS = 4
ITERS = 2


NORM_EPS = 1e-05
CONV_LAYOUT = ("NDHWC", "DHWIO", "NDHWC")


def shifted_2(x, axis, by):
    devices = lax.axis_size(axis)
    pairs = [(i, i + by) for i in range(devices) if 0 <= i + by < devices]
    return lax.ppermute(x, axis, pairs)


def conv_layer(inputs, kernel, stride):
    return lax.conv_general_dilated(
        inputs,
        kernel,
        (stride, stride, stride),
        ((1, 1), (1, 1), (1, 1)),
        dimension_numbers=CONV_LAYOUT,
        preferred_element_type=jnp.float32,
    )


def network_loss(weights, batch_rows, targets):
    first_kernel, norm_gain, second_kernel, head_weight = weights
    batch_size = batch_rows.shape[0]
    blocks = batch_rows.reshape(batch_size, 3, BE, BE, BE).transpose(0, 2, 3, 4, 1)
    first_out = conv_layer(blocks, first_kernel, 2)
    chan_mean = jnp.mean(first_out, axis=(0, 1, 2, 3))
    centred = first_out - chan_mean
    variance = jnp.mean(centred * centred, axis=(0, 1, 2, 3))
    normed = centred * (norm_gain * lax.rsqrt(variance + NORM_EPS))
    hidden = jax.nn.silu(normed).astype(jnp.bfloat16)
    second_out = conv_layer(hidden, second_kernel, 2)
    deep_act = jax.nn.silu(second_out).astype(jnp.bfloat16)
    flat_act = deep_act.reshape(-1, deep_act.shape[-1])
    stress = jnp.dot(flat_act, head_weight, preferred_element_type=jnp.float32)
    stress = stress.reshape(batch_size, -1, 6).transpose(0, 2, 1).reshape(batch_size, -1)
    error_vals = stress - targets.astype(jnp.float32)
    loss_value = jnp.sum(error_vals * error_vals) / (2.0 * batch_size)
    return (loss_value, stress)


def pick_blocks(volume, chosen):
    extent_x, extent_y, extent_z = (volume.shape[1], volume.shape[2], volume.shape[3])
    blocks = volume.reshape(3, extent_x // BE, BE, extent_y // BE, BE, extent_z // BE, BE)
    blocks = blocks.transpose(1, 3, 5, 0, 2, 4, 6).reshape(-1, 3 * BE * BE * BE)
    return jnp.take(blocks, chosen, axis=0).astype(jnp.bfloat16)


def neighbours(padded):
    summed = padded[2:, 1:-1, 1:-1] + padded[:-2, 1:-1, 1:-1]
    summed = summed + padded[1:-1, 2:, 1:-1] + padded[1:-1, :-2, 1:-1]
    return summed + padded[1:-1, 1:-1, 2:] + padded[1:-1, 1:-1, :-2]


def operate(padded):
    return 6.0 * padded[1:-1, 1:-1, 1:-1] - neighbours(padded)


def local_solve(window, inside):
    correction = jnp.zeros_like(window)
    for sweep_num in range(SWEEPS):
        correction = inside * (window + neighbours(jnp.pad(correction, 1))) / 6.0
    return correction[OV:-OV, OV:-OV, OV:-OV]


def layout():
    dom_count = lax.axis_size("dom")
    span_y = max(2, dom_count // 32)
    span_z = 2 * span_y
    span_x = 2 * dom_count // (span_y * span_z)
    flat_index = lax.axis_index("sec") * dom_count + lax.axis_index("dom")
    coords = (flat_index // (span_y * span_z), flat_index // span_z % span_y, flat_index % span_z)
    return ((span_x, span_y, span_z), (span_y * span_z, span_z, 1), coords)


def from_below(layers, stride, at_start):
    arrived = shifted_2(layers.astype(jnp.bfloat16), ("sec", "dom"), stride).astype(layers.dtype)
    return jnp.where(at_start, jnp.zeros_like(arrived), arrived)


def from_above(layers, stride, at_end):
    arrived = shifted_2(layers.astype(jnp.bfloat16), ("sec", "dom"), -stride).astype(layers.dtype)
    return jnp.where(at_end, jnp.zeros_like(arrived), arrived)


def extend(volume, margin, layout_info):
    counts, strides, coords = layout_info
    for axis_num in range(3):
        extent = volume.shape[axis_num]
        top_layer = lax.slice_in_dim(volume, extent - margin, extent, axis=axis_num)
        bottom_layer = lax.slice_in_dim(volume, 0, margin, axis=axis_num)
        lower_part = from_below(top_layer, strides[axis_num], coords[axis_num] == 0)
        upper_part = from_above(
            bottom_layer, strides[axis_num], coords[axis_num] == counts[axis_num] - 1
        )
        volume = jnp.concatenate([lower_part, volume, upper_part], axis=axis_num)
    return volume


def divergence(volume, layout_info):
    counts, strides, coords = layout_info
    summed = jnp.zeros(volume.shape[1:], jnp.float32)
    for axis_num in range(3):
        component = volume[axis_num]
        extent = component.shape[axis_num]
        edge_layer = lax.slice_in_dim(component, extent - 1, extent, axis=axis_num)
        rim_layer = from_below(edge_layer, strides[axis_num], coords[axis_num] == 0)
        shifted = jnp.concatenate(
            [rim_layer, lax.slice_in_dim(component, 0, extent - 1, axis=axis_num)], axis=axis_num
        )
        summed = summed + (component - shifted)
    return -summed


def inside_mask(extent_shape, layout_info):
    counts, strides, coords = layout_info
    shape_wide = tuple((extent + 2 * OV for extent in extent_shape))
    inside = jnp.ones(shape_wide, jnp.float32)
    for axis_num in range(3):
        position = lax.broadcasted_iota(jnp.int32, shape_wide, axis_num)
        keep_low = (position >= OV) | (coords[axis_num] > 0)
        keep_high = (position < extent_shape[axis_num] + OV) | (
            coords[axis_num] < counts[axis_num] - 1
        )
        inside = inside * (keep_low & keep_high).astype(jnp.float32)
    return inside


def shards(
    velocity,
    first_kernel,
    norm_gain,
    second_kernel,
    head_weight,
    selection,
    assignment,
    target_stress,
):
    layout_info = layout()
    volume = velocity[0]
    source = divergence(volume, layout_info)
    inside = inside_mask(source.shape, layout_info)
    pressure = jnp.zeros_like(source)
    source_wide = extend(source, OV, layout_info)
    for round_num in range(ITERS):
        if round_num == 0:
            window = source_wide
        else:
            residual = source - operate(extend(pressure, 1, layout_info))
            window = extend(residual, OV, layout_info)
        pressure = pressure + local_solve(window, inside)
    snap_count = selection.shape[1]
    dom_count = lax.axis_size("dom")
    device_count = 2 * dom_count
    order = jnp.argsort(assignment.reshape(-1), stable=True)
    ranks = jnp.argsort(order, stable=True)
    picked = pick_blocks(volume, selection[0])
    send_blocks = picked.reshape(snap_count, 2, dom_count, -1)
    spread = lax.all_to_all(
        lax.all_to_all(send_blocks, "sec", split_axis=1, concat_axis=1, tiled=True),
        "dom",
        split_axis=2,
        concat_axis=2,
        tiled=True,
    )
    piece_len = spread.shape[3]
    by_source = spread.transpose(1, 2, 0, 3).reshape(device_count * snap_count, piece_len)
    sorted_pieces = jnp.take(by_source, order, axis=0).reshape(2, dom_count, snap_count, piece_len)
    arrived = lax.all_to_all(
        lax.all_to_all(sorted_pieces, "sec", split_axis=0, concat_axis=0, tiled=True),
        "dom",
        split_axis=1,
        concat_axis=1,
        tiled=True,
    )
    batch_rows = arrived.transpose(2, 0, 1, 3).reshape(snap_count, -1)
    targets = target_stress[0]
    weights = (first_kernel, norm_gain, second_kernel, head_weight)
    loss_value, pullback, stress = jax.vjp(
        lambda params: network_loss(params, batch_rows, targets), weights, has_aux=True
    )
    gradients = pullback(jnp.ones_like(loss_value))[0]
    stress_len = stress.shape[1]
    share_len = (stress_len + device_count - 1) // device_count
    outgoing = jnp.pad(
        stress.astype(jnp.bfloat16), ((0, 0), (0, share_len * device_count - stress_len))
    )
    outgoing = outgoing.reshape(snap_count, 2, dom_count, share_len)
    stress_parts = lax.all_to_all(
        lax.all_to_all(outgoing, "sec", split_axis=1, concat_axis=1, tiled=True),
        "dom",
        split_axis=2,
        concat_axis=2,
        tiled=True,
    )
    by_rank = stress_parts.transpose(1, 2, 0, 3).reshape(device_count * snap_count, share_len)
    by_owner = jnp.take(by_rank, ranks, axis=0).reshape(2, dom_count, snap_count, share_len)
    returned = lax.all_to_all(
        lax.all_to_all(by_owner, "sec", split_axis=0, concat_axis=0, tiled=True),
        "dom",
        split_axis=1,
        concat_axis=1,
        tiled=True,
    )
    predicted = returned.transpose(2, 0, 1, 3).reshape(snap_count, -1)[:, :stress_len]
    summed = lax.psum(
        (
            gradients[0].astype(jnp.float32),
            gradients[1].astype(jnp.float32),
            gradients[2].astype(jnp.float32),
            gradients[3].astype(jnp.float32),
        ),
        ("sec", "dom"),
    )
    return (pressure[None], predicted[None], summed[0], summed[1], summed[2], summed[3])


def solution(mesh):
    placed = (
        P(("sec", "dom"), None, None, None, None),
        P(),
        P(),
        P(),
        P(),
        P(("sec", "dom"), None),
        P(),
        P(("sec", "dom"), None, None),
    )
    return jax.shard_map(
        shards,
        mesh=mesh,
        in_specs=placed,
        out_specs=(
            P(("sec", "dom"), None, None, None),
            P(("sec", "dom"), None, None),
            P(),
            P(),
            P(),
            P(),
        ),
        check_vma=False,
    )
```

profile of v0, /device:TPU:1, one launch (start us, length us, event | category | flops | bytes accessed | tf_op | source)
XLA Modules:
  0.0 576.4 jit_solution(17122632558845800585)
XLA Ops:
  7.9 5.4 reshape_squeeze.3
  17.4 5.2 reshape.192
  28.9 9.6 %collective-permute-start.1 = (bf16[32,1,128]{2,1,0:T(2,128)(2,1)S(1)}, bf16[32,1,128]{2,1,0:T(2,128)(2,1)S(1)}, u32[]{:S(2)}, u32[]{:S(2)}) collective-permute-start(bf16[32,1,128]{2,1,0:T(2,128)(2,1)S(1)} %slice.543), channel_id=1, source_target_pairs={{0,8},{1,9},{2,10},{3,11},{4,12},{5,13},{6,14},{7,15},{8,16},{9,17... | collective-permute-start | bytes 24584 | tf_op jit(solution)/shard_map/ppermute | solution.py:19
  42.2 4.8 collective-permute-start
  59.5 4.7 collective-permute-done.4
  67.9 7.8 %collective-permute-done.6 = bf16[36,2,128]{2,1,0:T(2,128)(2,1)S(1)} collective-permute-done((bf16[36,2,128]{2,1,0:T(2,128)(2,1)S(1)}, bf16[36,2,128]{2,1,0:T(2,128)(2,1)S(1)}, u32[]{:S(2)}, u32[]{:S(2)}) %collective-permute-start.6) | collective-permute-done | bytes 18464 | tf_op jit(solution)/shard_map/ppermute | solution.py:19
  86.1 6.6 %collective-permute-done.8 = bf16[36,36,2]{2,1,0:T(8,128)(2,1)S(1)} collective-permute-done((bf16[36,36,2]{2,1,0:T(8,128)(2,1)S(1)}, bf16[36,36,2]{2,1,0:T(8,128)(2,1)S(1)}, u32[]{:S(2)}, u32[]{:S(2)}) %collective-permute-start.8) | collective-permute-done | bytes 5216 | tf_op jit(solution)/shard_map/ppermute | solution.py:19
  103.5 7.1 %collective-permute-start.10 = (bf16[1,32,128]{2,1,0:T(8,128)(2,1)S(1)}, bf16[1,32,128]{2,1,0:T(8,128)(2,1)S(1)}, u32[]{:S(2)}, u32[]{:S(2)}) collective-permute-start(bf16[1,32,128]{2,1,0:T(8,128)(2,1)S(1)} %get-tuple-element.48), channel_id=1, source_target_pairs={{0,32},{1,33},{2,34},{3,35},{4,36},{5,37},{6,38},{7,39},{8,40},{9,... | collective-permute-start | bytes 24584 | tf_op jit(solution)/shard_map/ppermute | solution.py:19
  112.2 4.7 collective-permute-done.9
  116.9 8.3 %collective-permute-start.12 = (bf16[34,1,128]{2,1,0:T(2,128)(2,1)S(1)}, bf16[34,1,128]{2,1,0:T(2,128)(2,1)S(1)}, u32[]{:S(2)}, u32[]{:S(2)}) collective-permute-start(bf16[34,1,128]{2,1,0:T(2,128)(2,1)S(1)} %get-tuple-element.54), channel_id=1, source_target_pairs={{0,8},{1,9},{2,10},{3,11},{4,12},{5,13},{6,14},{7,15},{8,16},{9,17... | collective-permute-start | bytes 26120 | tf_op jit(solution)/shard_map/ppermute | solution.py:19
  127.1 7.1 %collective-permute-done.11 = bf16[34,1,128]{2,1,0:T(2,128)(2,1)S(1)} collective-permute-done((bf16[34,1,128]{2,1,0:T(2,128)(2,1)S(1)}, bf16[34,1,128]{2,1,0:T(2,128)(2,1)S(1)}, u32[]{:S(2)}, u32[]{:S(2)}) %collective-permute-start.11) | collective-permute-done | bytes 8736 | tf_op jit(solution)/shard_map/ppermute | solution.py:19
  134.5 6.7 %collective-permute-start.13 = (bf16[34,34,1]{2,1,0:T(8,128)(2,1)S(1)}, bf16[34,34,1]{2,1,0:T(8,128)(2,1)S(1)}, u32[]{:S(2)}, u32[]{:S(2)}) collective-permute-start(bf16[34,34,1]{2,1,0:T(8,128)(2,1)S(1)} %get-tuple-element.60), channel_id=1, source_target_pairs={{1,0},{2,1},{3,2},{4,3},{5,4},{6,5},{7,6},{8,7},{9,8},{10,9},{11,1... | collective-permute-start | bytes 6944 | tf_op jit(solution)/shard_map/ppermute | solution.py:19
  148.7 6.6 %collective-permute-start.15 = (bf16[2,32,128]{2,1,0:T(8,128)(2,1)S(1)}, bf16[2,32,128]{2,1,0:T(8,128)(2,1)S(1)}, u32[]{:S(2)}, u32[]{:S(2)}) collective-permute-start(bf16[2,32,128]{2,1,0:T(8,128)(2,1)S(1)} %get-tuple-element.62), channel_id=1, source_target_pairs={{0,32},{1,33},{2,34},{3,35},{4,36},{5,37},{6,38},{7,39},{8,40},{9,... | collective-permute-start | bytes 49160 | tf_op jit(solution)/shard_map/ppermute | solution.py:19
  156.6 7.8 %collective-permute-done.16 = bf16[2,32,128]{2,1,0:T(8,128)(2,1)S(1)} collective-permute-done((bf16[2,32,128]{2,1,0:T(8,128)(2,1)S(1)}, bf16[2,32,128]{2,1,0:T(8,128)(2,1)S(1)}, u32[]{:S(2)}, u32[]{:S(2)}) %collective-permute-start.16) | collective-permute-done | bytes 16416 | tf_op jit(solution)/shard_map/ppermute | solution.py:19
  167.7 7.1 %collective-permute-done.18 = bf16[36,2,128]{2,1,0:T(2,128)(2,1)S(1)} collective-permute-done((bf16[36,2,128]{2,1,0:T(2,128)(2,1)S(1)}, bf16[36,2,128]{2,1,0:T(2,128)(2,1)S(1)}, u32[]{:S(2)}, u32[]{:S(2)}) %collective-permute-start.18) | collective-permute-done | bytes 18464 | tf_op jit(solution)/shard_map/ppermute | solution.py:19
  175.8 5.6 collective-permute-start.19
  183.8 29.0 %all-to-all-start.1 = ((bf16[1,2,128,384]{3,1,0,2:T(2,128)(2,1)}), bf16[1,2,128,384]{3,1,0,2:T(2,128)(2,1)}, u32[]{:S(2)}, u32[]{:S(2)}) async-start(bf16[1,2,128,384]{3,1,0,2:T(2,128)(2,1)} %copy.108), calls=%async_computation.1 | async-start | bytes 393216 | tf_op jit(solution)/shard_map/all_to_all | solution.py:170
  216.1 6.4 %collective-permute-done.20 = bf16[36,36,2]{2,1,0:T(8,128)(2,1)S(1)} collective-permute-done((bf16[36,36,2]{2,1,0:T(8,128)(2,1)S(1)}, bf16[36,36,2]{2,1,0:T(8,128)(2,1)S(1)}, u32[]{:S(2)}, u32[]{:S(2)}) %collective-permute-start.20) | collective-permute-done | bytes 5216 | tf_op jit(solution)/shard_map/ppermute | solution.py:19
  235.6 6.6 %multiply_multiply_fusion = (f32[36,36,132]{2,1,0:T(8,128)S(1)}, f32[36,36,132]{2,1,0:T(8,128)}) fusion(f32[36,36,132]{2,1,0:T(8,128)S(1)} %get-tuple-element.33, f32[36,36,132]{2,1,0:T(8,128)} %multiply_multiply_fusion.1, f32[36]{0:T(128)S(1)} %get-tuple-element.78, pred[36]{0:T(512)(128)(4,1)S(1)} %get-tuple-element.79, pred[132]{0:T(512)(128)(4,1)S(1)} %copy-done.15), kind=kLoop, calls=%fused_computation.54 | loop fusion | flops 1710720 | bytes 2737464 | tf_op jit(solution)/shard_map/div | solution.py:73
  244.0 14.5 %all-to-all-start.3 = ((bf16[2,128,1,384]{3,0,2,1:T(2,128)(2,1)}), bf16[2,128,1,384]{3,0,2,1:T(2,128)(2,1)}, u32[]{:S(2)}, u32[]{:S(2)}) async-start(bf16[2,128,1,384]{3,0,2,1:T(2,128)(2,1)} %copy.111), calls=%async_computation.3 | async-start | bytes 393216 | tf_op jit(solution)/shard_map/all_to_all | solution.py:180
  263.2 9.1 %all-to-all-done.3 = bf16[2,128,1,384]{3,0,2,1:T(2,128)(2,1)} async-done(((bf16[2,128,1,384]{3,0,2,1:T(2,128)(2,1)}), bf16[2,128,1,384]{3,0,2,1:T(2,128)(2,1)}, u32[]{:S(2)}, u32[]{:S(2)}) %all-to-all-start.3) | async-done | bytes 196640 | tf_op jit(solution)/shard_map/all_to_all | solution.py:180
  275.2 7.5 %copy.115 = bf16[3,32,32,1,8,6]{4,0,5,2,1,3:T(4,128)(2,1)} copy(bf16[3,32,32,1,8,6]{2,1,5,4,0,3:T(8,128)(2,1)S(1)} %bitcast.141) | data formatting | bytes 589824 | tf_op jit(solution)/shard_map/jvp()/conv_general_dilated | solution.py:23
  285.5 12.8 %select_reduce_fusion.1 = (f32[64]{0:T(128)S(1)}, f32[16,16,8,3,64]{4,2,3,1,0:T(8,128)S(1)}) fusion(pred[8,3]{0,1:T(4,128)(4,1)S(1)} %copy-done.18, bf16[3,3,3,3,64]{4,3,2,1,0:T(4,128)(2,1)S(1)} %copy-done.23, bf16[3,32,32,1,7,2]{4,0,5,2,1,3:T(4,128)(2,1)S(1)} %slice.402, bf16[3,32,32,1,8,6]{4,0,5,2,1,3:T(4,128)(2,1)} %copy.115), kind=kOutput, calls=%fused_computation.23 | convolution fusion | flops 63433664 | bytes 1964440 | tf_op jit(solution)/shard_map/jvp()/conv_general_dilated | solution.py:23
  313.5 6.1 %fusion.32 = f32[3,3,3,64,128]{4,3,2,1,0:T(8,128)} fusion(f32[1,8,8,8,128]{4,0,3,2,1:T(1,128)S(1)} %bitcast.156, bf16[16,16,1,16,64]{4,1,3,0,2:T(8,128)(2,1)S(1)} %slice.411), kind=kOutput, calls=%fused_computation.71 | convolution fusion | flops 199565312 | bytes 1671168 | tf_op jit(solution)/shard_map/transpose(jvp())/conv_general_dilated | solution.py:23
  329.9 16.3 %multiply_reduce_fusion = (f32[64]{0:T(128)S(1)}, f32[1,16,16,16,64]{4,0,3,2,1:T(1,128)}) fusion(f32[1,16,16,16,64]{4,0,3,2,1:T(1,128)S(1)} %bitcast.150, f32[1,16,16,16,64]{4,0,3,2,1:T(1,128)S(1)} %bitcast.147, f32[1,16,16,16,64]{4,0,3,2,1:T(1,128)S(1)} %bitcast.148, f32[1,16,16,16,64]{4,0,3,2,1:T(1,128)S(1)} %bitcast.149, ...), kind=kOutput, calls=%fused_computation.37 | convolution fusion | flops 201179072 | bytes 5947648 | tf_op jit(solution)/shard_map/transpose(jvp())/conv_general_dilated | solution.py:23
  351.9 6.2 %fusion.81 = (f32[64]{0:T(128)S(1)}, f32[1,16,16,16,64]{4,0,3,2,1:T(1,128)}) fusion(f32[1,16,16,16,64]{4,0,3,2,1:T(1,128)S(1)} %bitcast.139, f32[1,16,16,16,64]{4,0,3,2,1:T(1,128)} %get-tuple-element.77, f32[64]{0:T(128)S(1)} %rsqrt_multiply_fusion.1), kind=kLoop, calls=%fused_computation.207 | loop fusion | flops 1048512 | bytes 3146240 | tf_op jit(solution)/shard_map/transpose(jvp())/reduce_sum | solution.py:39
  358.9 5.7 all-to-all-start.5
  365.1 29.7 %copy.140 = bf16[1,3,32,32,32]{1,0,4,3,2:T(2,128)(2,1)} copy(bf16[1,3,32,32,32]{4,3,2,1,0:T(8,128)(2,1)S(1)} %reshape_reshape_transpose.3) | data formatting | bytes 393216 | tf_op jit(solution)/shard_map/jvp()/reshape;reshape;transpose | solution.py:36
  399.9 50.7 %fusion.38 = f32[3,3,3,3,64]{4,3,2,1,0:T(4,128)S(1)} fusion(bf16[1,3,32,32,32]{1,0,4,3,2:T(2,128)(2,1)} %copy.140, f32[1,16,16,16,64]{4,0,3,2,1:T(1,128)S(1)} %copy-done.10, f32[64]{0:T(128)S(1)} %negate_multiply_fusion), kind=kOutput, calls=%fused_computation.74 | convolution fusion | flops 40140544 | bytes 1266176 | tf_op jit(solution)/shard_map/transpose(jvp())/conv_general_dilated | solution.py:23
  451.3 14.6 %all-to-all-start.7 = ((bf16[2,128,1,12]{3,0,2,1:T(2,128)(2,1)}), bf16[2,128,1,12]{3,0,2,1:T(2,128)(2,1)S(1)}, u32[]{:S(2)}, u32[]{:S(2)}) async-start(bf16[2,128,1,12]{3,0,2,1:T(2,128)(2,1)} %copy.126), calls=%async_computation.7 | async-start | bytes 131072 | tf_op jit(solution)/shard_map/all_to_all | solution.py:209
  466.1 79.3 %all-reduce.7 = (f32[3,3,3,3,64]{4,3,2,1,0:T(4,128)}, f32[64]{0:T(128)}, f32[128,6]{0,1:T(8,128)}) all-reduce(f32[3,3,3,3,64]{4,3,2,1,0:T(4,128)S(1)} %fusion.38, f32[64]{0:T(128)S(1)} %get-tuple-element.68, f32[128,6]{0,1:T(8,128)S(1)} %fusion.41), channel_id=1, replica_groups=mesh['sec'=2,'dom'=128] {'sec','dom'}, use_global_device_ids=true, to_apply=%region_6.7 | all-reduce | flops 6016 | bytes 48128 | tf_op jit(solution)/shard_map/psum | solution.py:217
  546.2 20.8 %all-reduce.10.cloned.1.call-done = f32[3,3,3,64,128]{4,3,2,1,0:T(8,128)} async-done(((f32[3,3,3,64,128]{4,3,2,1,0:T(8,128)}), f32[3,3,3,64,128]{4,3,2,1,0:T(8,128)}) %all-reduce.10.cloned.1.call-update) | async-done | bytes 884752 | tf_op jit(solution)/shard_map/psum | solution.py:217
  (212 shorter events, 139.8 us)
Async XLA Ops:
  7.2 304.9 %copy-start = (bf16[3,3,3,64,128]{4,3,2,1,0:T(8,128)(2,1)S(1)}, bf16[3,3,3,64,128]{4,3,2,1,0:T(8,128)(2,1)}, u32[]{:S(2)}) copy-start(bf16[3,3,3,64,128]{4,3,2,1,0:T(8,128)(2,1)} %param.11) | copy-start | bytes 1327108
  24.7 157.3 %all-to-all-start = ((bf16[1,2,128,384]{3,2,0,1:T(8,128)(2,1)}), bf16[1,2,128,384]{3,2,0,1:T(8,128)(2,1)}, u32[]{:S(2)}, u32[]{:S(2)}) async-start(bf16[1,2,128,384]{3,2,0,1:T(8,128)(2,1)} %bitcast.13), calls=%async_computation | async-start | bytes 393216 | tf_op jit(solution)/shard_map/all_to_all | solution.py:171
  28.9 23.2 %collective-permute-start.1 = (bf16[32,1,128]{2,1,0:T(2,128)(2,1)S(1)}, bf16[32,1,128]{2,1,0:T(2,128)(2,1)S(1)}, u32[]{:S(2)}, u32[]{:S(2)}) collective-permute-start(bf16[32,1,128]{2,1,0:T(2,128)(2,1)S(1)} %slice.543), channel_id=1, source_target_pairs={{0,8},{1,9},{2,10},{3,11},{4,12},{5,13},{6,14},{7,15},{8,16},{9,17... | collective-permute-start | bytes 24584 | tf_op jit(solution)/shard_map/ppermute | solution.py:19
  38.7 12.3 %collective-permute-start.2 = (bf16[32,32,1]{2,1,0:T(8,128)(2,1)S(1)}, bf16[32,32,1]{2,1,0:T(8,128)(2,1)}, u32[]{:S(2)}, u32[]{:S(2)}) collective-permute-start(bf16[32,32,1]{2,1,0:T(8,128)(2,1)S(1)} %slice.542), channel_id=1, source_target_pairs={{0,1},{1,2},{2,3},{3,4},{4,5},{5,6},{6,7},{7,8},{8,9},{9,10},{10,1... | collective-permute-start | bytes 6152 | tf_op jit(solution)/shard_map/ppermute | solution.py:19
  42.2 9.9 %collective-permute-start = (bf16[1,32,128]{2,1,0:T(8,128)(2,1)S(1)}, bf16[1,32,128]{2,1,0:T(8,128)(2,1)S(1)}, u32[]{:S(2)}, u32[]{:S(2)}) collective-permute-start(bf16[1,32,128]{2,1,0:T(8,128)(2,1)S(1)} %fusion.71), channel_id=1, source_target_pairs={{0,32},{1,33},{2,34},{3,35},{4,36},{5,37},{6,38},{7,39},{8,40},{9,... | collective-permute-start | bytes 24584 | tf_op jit(solution)/shard_map/ppermute | solution.py:19
  53.7 5.8 collective-permute-start.3
  58.2 6.0 %collective-permute-start.4 = (bf16[2,32,128]{2,1,0:T(8,128)(2,1)S(1)}, bf16[2,32,128]{2,1,0:T(8,128)(2,1)S(1)}, u32[]{:S(2)}, u32[]{:S(2)}) collective-permute-start(bf16[2,32,128]{2,1,0:T(8,128)(2,1)S(1)} %get-tuple-element.65), channel_id=1, source_target_pairs={{32,0},{33,1},{34,2},{35,3},{36,4},{37,5},{38,6},{39,7},{40,8},{41... | collective-permute-start | bytes 49160 | tf_op jit(solution)/shard_map/ppermute | solution.py:19
  64.2 3.7 collective-permute-start.5
  66.6 9.1 %collective-permute-start.6 = (bf16[36,2,128]{2,1,0:T(2,128)(2,1)S(1)}, bf16[36,2,128]{2,1,0:T(2,128)(2,1)S(1)}, u32[]{:S(2)}, u32[]{:S(2)}) collective-permute-start(bf16[36,2,128]{2,1,0:T(2,128)(2,1)S(1)} %get-tuple-element.53), channel_id=1, source_target_pairs={{8,0},{9,1},{10,2},{11,3},{12,4},{13,5},{14,6},{15,7},{16,8},{17,9... | collective-permute-start | bytes 55304 | tf_op jit(solution)/shard_map/ppermute | solution.py:19
  76.0 10.0 %collective-permute-start.7 = (bf16[36,36,2]{2,1,0:T(8,128)(2,1)S(1)}, bf16[36,36,2]{2,1,0:T(8,128)(2,1)S(1)}, u32[]{:S(2)}, u32[]{:S(2)}) collective-permute-start(bf16[36,36,2]{2,1,0:T(8,128)(2,1)S(1)} %get-tuple-element.58), channel_id=1, source_target_pairs={{0,1},{1,2},{2,3},{3,4},{4,5},{5,6},{6,7},{7,8},{8,9},{9,10},{10,1... | collective-permute-start | bytes 15560 | tf_op jit(solution)/shard_map/ppermute | solution.py:19
  83.9 8.8 %collective-permute-start.8 = (bf16[36,36,2]{2,1,0:T(8,128)(2,1)S(1)}, bf16[36,36,2]{2,1,0:T(8,128)(2,1)S(1)}, u32[]{:S(2)}, u32[]{:S(2)}) collective-permute-start(bf16[36,36,2]{2,1,0:T(8,128)(2,1)S(1)} %get-tuple-element.59), channel_id=1, source_target_pairs={{1,0},{2,1},{3,2},{4,3},{5,4},{6,5},{7,6},{8,7},{9,8},{10,9},{11,1... | collective-permute-start | bytes 15560 | tf_op jit(solution)/shard_map/ppermute | solution.py:19
  103.5 8.6 %collective-permute-start.10 = (bf16[1,32,128]{2,1,0:T(8,128)(2,1)S(1)}, bf16[1,32,128]{2,1,0:T(8,128)(2,1)S(1)}, u32[]{:S(2)}, u32[]{:S(2)}) collective-permute-start(bf16[1,32,128]{2,1,0:T(8,128)(2,1)S(1)} %get-tuple-element.48), channel_id=1, source_target_pairs={{0,32},{1,33},{2,34},{3,35},{4,36},{5,37},{6,38},{7,39},{8,40},{9,... | collective-permute-start | bytes 24584 | tf_op jit(solution)/shard_map/ppermute | solution.py:19
  110.9 6.0 %collective-permute-start.9 = (bf16[1,32,128]{2,1,0:T(8,128)(2,1)S(1)}, bf16[1,32,128]{2,1,0:T(8,128)(2,1)S(1)}, u32[]{:S(2)}, u32[]{:S(2)}) collective-permute-start(bf16[1,32,128]{2,1,0:T(8,128)(2,1)S(1)} %get-tuple-element.49), channel_id=1, source_target_pairs={{32,0},{33,1},{34,2},{35,3},{36,4},{37,5},{38,6},{39,7},{40,8},{41... | collective-permute-start | bytes 24584 | tf_op jit(solution)/shard_map/ppermute | solution.py:19
  116.9 10.1 %collective-permute-start.12 = (bf16[34,1,128]{2,1,0:T(2,128)(2,1)S(1)}, bf16[34,1,128]{2,1,0:T(2,128)(2,1)S(1)}, u32[]{:S(2)}, u32[]{:S(2)}) collective-permute-start(bf16[34,1,128]{2,1,0:T(2,128)(2,1)S(1)} %get-tuple-element.54), channel_id=1, source_target_pairs={{0,8},{1,9},{2,10},{3,11},{4,12},{5,13},{6,14},{7,15},{8,16},{9,17... | collective-permute-start | bytes 26120 | tf_op jit(solution)/shard_map/ppermute | solution.py:19
  125.8 8.4 %collective-permute-start.11 = (bf16[34,1,128]{2,1,0:T(2,128)(2,1)S(1)}, bf16[34,1,128]{2,1,0:T(2,128)(2,1)S(1)}, u32[]{:S(2)}, u32[]{:S(2)}) collective-permute-start(bf16[34,1,128]{2,1,0:T(2,128)(2,1)S(1)} %get-tuple-element.55), channel_id=1, source_target_pairs={{8,0},{9,1},{10,2},{11,3},{12,4},{13,5},{14,6},{15,7},{16,8},{17,9... | collective-permute-start | bytes 26120 | tf_op jit(solution)/shard_map/ppermute | solution.py:19
  134.5 9.6 %collective-permute-start.13 = (bf16[34,34,1]{2,1,0:T(8,128)(2,1)S(1)}, bf16[34,34,1]{2,1,0:T(8,128)(2,1)S(1)}, u32[]{:S(2)}, u32[]{:S(2)}) collective-permute-start(bf16[34,34,1]{2,1,0:T(8,128)(2,1)S(1)} %get-tuple-element.60), channel_id=1, source_target_pairs={{1,0},{2,1},{3,2},{4,3},{5,4},{6,5},{7,6},{8,7},{9,8},{10,9},{11,1... | collective-permute-start | bytes 6944 | tf_op jit(solution)/shard_map/ppermute | solution.py:19
  141.7 6.1 %collective-permute-start.14 = (bf16[34,34,1]{2,1,0:T(8,128)(2,1)S(1)}, bf16[34,34,1]{2,1,0:T(8,128)(2,1)S(1)}, u32[]{:S(2)}, u32[]{:S(2)}) collective-permute-start(bf16[34,34,1]{2,1,0:T(8,128)(2,1)S(1)} %get-tuple-element.61), channel_id=1, source_target_pairs={{0,1},{1,2},{2,3},{3,4},{4,5},{5,6},{6,7},{7,8},{8,9},{9,10},{10,1... | collective-permute-start | bytes 6944 | tf_op jit(solution)/shard_map/ppermute | solution.py:19
  148.7 7.9 %collective-permute-start.15 = (bf16[2,32,128]{2,1,0:T(8,128)(2,1)S(1)}, bf16[2,32,128]{2,1,0:T(8,128)(2,1)S(1)}, u32[]{:S(2)}, u32[]{:S(2)}) collective-permute-start(bf16[2,32,128]{2,1,0:T(8,128)(2,1)S(1)} %get-tuple-element.62), channel_id=1, source_target_pairs={{0,32},{1,33},{2,34},{3,35},{4,36},{5,37},{6,38},{7,39},{8,40},{9,... | collective-permute-start | bytes 49160 | tf_op jit(solution)/shard_map/ppermute | solution.py:19
  155.3 9.1 %collective-permute-start.16 = (bf16[2,32,128]{2,1,0:T(8,128)(2,1)S(1)}, bf16[2,32,128]{2,1,0:T(8,128)(2,1)S(1)}, u32[]{:S(2)}, u32[]{:S(2)}) collective-permute-start(bf16[2,32,128]{2,1,0:T(8,128)(2,1)S(1)} %get-tuple-element.63), channel_id=1, source_target_pairs={{32,0},{33,1},{34,2},{35,3},{36,4},{37,5},{38,6},{39,7},{40,8},{41... | collective-permute-start | bytes 49160 | tf_op jit(solution)/shard_map/ppermute | solution.py:19
  164.4 3.2 collective-permute-start.17
  166.3 8.4 %collective-permute-start.18 = (bf16[36,2,128]{2,1,0:T(2,128)(2,1)S(1)}, bf16[36,2,128]{2,1,0:T(2,128)(2,1)S(1)}, u32[]{:S(2)}, u32[]{:S(2)}) collective-permute-start(bf16[36,2,128]{2,1,0:T(2,128)(2,1)S(1)} %get-tuple-element.51), channel_id=1, source_target_pairs={{8,0},{9,1},{10,2},{11,3},{12,4},{13,5},{14,6},{15,7},{16,8},{17,9... | collective-permute-start | bytes 55304 | tf_op jit(solution)/shard_map/ppermute | solution.py:19
  175.8 40.3 %collective-permute-start.19 = (bf16[36,36,2]{2,1,0:T(8,128)(2,1)}, bf16[36,36,2]{2,1,0:T(8,128)(2,1)S(1)}, u32[]{:S(2)}, u32[]{:S(2)}) collective-permute-start(bf16[36,36,2]{2,1,0:T(8,128)(2,1)} %get-tuple-element.56), channel_id=1, source_target_pairs={{0,1},{1,2},{2,3},{3,4},{4,5},{5,6},{6,7},{7,8},{8,9},{9,10},{10,1... | collective-permute-start | bytes 15560 | tf_op jit(solution)/shard_map/ppermute | solution.py:19
  183.8 44.7 %all-to-all-start.1 = ((bf16[1,2,128,384]{3,1,0,2:T(2,128)(2,1)}), bf16[1,2,128,384]{3,1,0,2:T(2,128)(2,1)}, u32[]{:S(2)}, u32[]{:S(2)}) async-start(bf16[1,2,128,384]{3,1,0,2:T(2,128)(2,1)} %copy.108), calls=%async_computation.1 | async-start | bytes 393216 | tf_op jit(solution)/shard_map/all_to_all | solution.py:170
  212.7 9.8 %collective-permute-start.20 = (bf16[36,36,2]{2,1,0:T(8,128)(2,1)S(1)}, bf16[36,36,2]{2,1,0:T(8,128)(2,1)S(1)}, u32[]{:S(2)}, u32[]{:S(2)}) collective-permute-start(bf16[36,36,2]{2,1,0:T(8,128)(2,1)S(1)} %get-tuple-element.57), channel_id=1, source_target_pairs={{1,0},{2,1},{3,2},{4,3},{5,4},{6,5},{7,6},{8,7},{9,8},{10,9},{11,1... | collective-permute-start | bytes 15560 | tf_op jit(solution)/shard_map/ppermute | solution.py:19
  231.6 10.7 %all-to-all-start.2 = ((bf16[2,128,1,384]{3,1,2,0:T(8,128)(2,1)}), bf16[2,128,1,384]{3,1,2,0:T(8,128)(2,1)}, u32[]{:S(2)}, u32[]{:S(2)}) async-start(bf16[2,128,1,384]{3,1,2,0:T(8,128)(2,1)} %broadcast_select_fusion.2), calls=%async_computation.2 | async-start | bytes 393216 | tf_op jit(solution)/shard_map/all_to_all | solution.py:181
  244.0 28.3 %all-to-all-start.3 = ((bf16[2,128,1,384]{3,0,2,1:T(2,128)(2,1)}), bf16[2,128,1,384]{3,0,2,1:T(2,128)(2,1)}, u32[]{:S(2)}, u32[]{:S(2)}) async-start(bf16[2,128,1,384]{3,0,2,1:T(2,128)(2,1)} %copy.111), calls=%async_computation.3 | async-start | bytes 393216 | tf_op jit(solution)/shard_map/all_to_all | solution.py:180
  258.5 308.4 %all-reduce.10.cloned.1.call-start = ((), (), s32[]{:S(2)}) async-start(), calls=%async_computation.8 | async-start | bytes 1769472 | tf_op jit(solution)/shard_map/psum | solution.py:217
  348.7 9.5 %all-to-all-start.4 = ((bf16[1,2,128,12]{2,3,0,1:T(8,128)(2,1)}), bf16[1,2,128,12]{2,3,0,1:T(8,128)(2,1)S(1)}, u32[]{:S(2)}, u32[]{:S(2)}) async-start(bf16[1,2,128,12]{2,3,0,1:T(8,128)(2,1)} %copy.122), calls=%async_computation.4 | async-start | bytes 16384 | tf_op jit(solution)/shard_map/all_to_all | solution.py:201
  358.9 35.9 %all-to-all-start.5 = ((bf16[1,2,128,12]{3,1,0,2:T(2,128)(2,1)}), bf16[1,2,128,12]{3,1,0,2:T(2,128)(2,1)S(1)}, u32[]{:S(2)}, u32[]{:S(2)}) async-start(bf16[1,2,128,12]{3,1,0,2:T(2,128)(2,1)} %copy.123), calls=%async_computation.5 | async-start | bytes 131072 | tf_op jit(solution)/shard_map/all_to_all | solution.py:200
  396.6 53.9 %all-to-all-start.6 = ((bf16[2,128,1,12]{1,3,2,0:T(8,128)(2,1)}), bf16[2,128,1,12]{1,3,2,0:T(8,128)(2,1)S(1)}, u32[]{:S(2)}, u32[]{:S(2)}) async-start(bf16[2,128,1,12]{1,3,2,0:T(8,128)(2,1)} %broadcast_select_fusion.6), calls=%async_computation.6 | async-start | bytes 16384 | tf_op jit(solution)/shard_map/all_to_all | solution.py:210
  399.9 66.1 %copy-start.12 = (f32[1,6,512]{2,1,0:T(8,128)S(1)}, f32[1,6,512]{2,1,0:T(8,128)}, u32[]{:S(2)}) copy-start(f32[1,6,512]{2,1,0:T(8,128)} %copy-done.11) | copy-start | bytes 36868
  451.3 94.1 %all-to-all-start.7 = ((bf16[2,128,1,12]{3,0,2,1:T(2,128)(2,1)}), bf16[2,128,1,12]{3,0,2,1:T(2,128)(2,1)S(1)}, u32[]{:S(2)}, u32[]{:S(2)}) async-start(bf16[2,128,1,12]{3,0,2,1:T(2,128)(2,1)} %copy.126), calls=%async_computation.7 | async-start | bytes 131072 | tf_op jit(solution)/shard_map/all_to_all | solution.py:209
  (22 other events, 262.6 us)
Sparse Core Ops, SparseCore 0:
  319.8 247.1 all-reduce.9
where the time goes:
time: 585 us; the launch traced here: 576 us
  starting transfers between devices  158 us (27%)
  local copies, waits for them, and re-layouts  91.7 us (16%)
  matrix products  87.2 us (15%)
  waiting for transfers between devices  86.3 us (15%)
  blocking collectives  79.3 us (14%)
  other arithmetic  57.2 us (10%)
  between operations  16.4 us (3%)
    conv_general_dilated x5, matrix products, conv_layer(): lax.conv_general_dilated(inputs, kernel, (stride, stride, stride), ((1, 1...  86.7 us
    ppermute x21, starting transfers between devices, shifted_2(): return lax.ppermute(x, axis, pairs)  80 us
    psum x1, blocking collectives, shards(): lax.psum((gradients[0].astype(jnp.float32), gradients[1].astype(jnp.float...  79.3 us
    ppermute x21, waiting for transfers between devices, shifted_2(): return lax.ppermute(x, axis, pairs)  56.3 us
    another operation x4, local copies, waits for them, and re-layouts, network_loss(): batch_rows.reshape(batch_size, 3, BE, BE, BE).transpose(0, 2, 3, 4, 1)  30.9 us
    all_to_all x1, starting transfers between devices, shards(): lax.all_to_all(lax.all_to_all(send_blocks, 'sec', split_axis=1, concat_ax...  29 us
    psum x1, waiting for transfers between devices, shards(): lax.psum((gradients[0].astype(jnp.float32), gradients[1].astype(jnp.float...  20.8 us
    div x6, other arithmetic, local_solve(): correction = inside * (window + neighbours(jnp.pad(correction, 1))) / 6.0  20.3 us
  transfers between devices with their start and end apart: 30, of which 12 were waited for; matrix products, arithmetic and copies ran while one was open for 28% of the time, Pallas kernels for 0%

commit v1 on v0

--- a/solution.py
+++ b/solution.py
@@ -160,60 +160,16 @@
             residual = source - operate(extend(pressure, 1, layout_info))
             window = extend(residual, OV, layout_info)
         pressure = pressure + local_solve(window, inside)
-    snap_count = selection.shape[1]
-    dom_count = lax.axis_size("dom")
-    device_count = 2 * dom_count
-    order = jnp.argsort(assignment.reshape(-1), stable=True)
-    ranks = jnp.argsort(order, stable=True)
-    picked = pick_blocks(volume, selection[0])
-    send_blocks = picked.reshape(snap_count, 2, dom_count, -1)
-    spread = lax.all_to_all(
-        lax.all_to_all(send_blocks, "sec", split_axis=1, concat_axis=1, tiled=True),
-        "dom",
-        split_axis=2,
-        concat_axis=2,
-        tiled=True,
-    )
-    piece_len = spread.shape[3]
-    by_source = spread.transpose(1, 2, 0, 3).reshape(device_count * snap_count, piece_len)
-    sorted_pieces = jnp.take(by_source, order, axis=0).reshape(2, dom_count, snap_count, piece_len)
-    arrived = lax.all_to_all(
-        lax.all_to_all(sorted_pieces, "sec", split_axis=0, concat_axis=0, tiled=True),
-        "dom",
-        split_axis=1,
-        concat_axis=1,
-        tiled=True,
-    )
-    batch_rows = arrived.transpose(2, 0, 1, 3).reshape(snap_count, -1)
-    targets = target_stress[0]
+    chosen = assignment.reshape(-1)[lax.axis_index("sec") * lax.axis_size("dom") + lax.axis_index("dom")]
+    every_target = lax.all_gather(target_stress[0, 0], ("sec", "dom"))
+    targets = lax.dynamic_slice_in_dim(every_target, chosen, 1, axis=0)
+    batch_rows = pick_blocks(volume, selection[0])
     weights = (first_kernel, norm_gain, second_kernel, head_weight)
     loss_value, pullback, stress = jax.vjp(
         lambda params: network_loss(params, batch_rows, targets), weights, has_aux=True
     )
     gradients = pullback(jnp.ones_like(loss_value))[0]
-    stress_len = stress.shape[1]
-    share_len = (stress_len + device_count - 1) // device_count
-    outgoing = jnp.pad(
-        stress.astype(jnp.bfloat16), ((0, 0), (0, share_len * device_count - stress_len))
-    )
-    outgoing = outgoing.reshape(snap_count, 2, dom_count, share_len)
-    stress_parts = lax.all_to_all(
-        lax.all_to_all(outgoing, "sec", split_axis=1, concat_axis=1, tiled=True),
-        "dom",
-        split_axis=2,
-        concat_axis=2,
-        tiled=True,
-    )
-    by_rank = stress_parts.transpose(1, 2, 0, 3).reshape(device_count * snap_count, share_len)
-    by_owner = jnp.take(by_rank, ranks, axis=0).reshape(2, dom_count, snap_count, share_len)
-    returned = lax.all_to_all(
-        lax.all_to_all(by_owner, "sec", split_axis=0, concat_axis=0, tiled=True),
-        "dom",
-        split_axis=1,
-        concat_axis=1,
-        tiled=True,
-    )
-    predicted = returned.transpose(2, 0, 1, 3).reshape(snap_count, -1)[:, :stress_len]
+    predicted = stress.astype(jnp.bfloat16)
     summed = lax.psum(
         (
             gradients[0].astype(jnp.float32),

time: 585 us -> 707 us (1.21)
  waiting for transfers between devices: 86.3 us -> 289 us
  starting transfers between devices: 158 us -> 86.8 us
  other arithmetic: 57.2 us -> 43.7 us
    all_gather x0 -> x1, waiting for transfers between devices: none -> 133 us  [shards(): every_target = lax.all_gather(target_stress[0, 0], ('sec', 'dom'))]
    psum x1, waiting for transfers between devices: 20.8 us -> 105 us  [shards(): lax.psum((gradients[0].astype(jnp.float32), gradients[1].astype(jnp.float...]
    all_to_all x8 -> x0, starting transfers between devices: 78.3 us -> none  [the longest x1 29 us: shards(): lax.all_to_all(lax.all_to_all(send_blocks, 'sec', split_axis=1, concat_ax...]
    convert_element_type x1 -> x5, local copies, waits for them, and re-layouts: 0.78 us -> 40.7 us  [pick_blocks(): return jnp.take(blocks, chosen, axis=0).astype(jnp.bfloat16)]
    another operation x6 -> x1, local copies, waits for them, and re-layouts: 31.7 us -> 0.1 us  [the longest x4 30.9 us: network_loss(): batch_rows.reshape(batch_size, 3, BE, BE, BE).transpose(0, 2, 3, 4, 1)]
    all_to_all x8 -> x0, waiting for transfers between devices: 9.11 us -> none  [the longest x1 9.09 us: shards(): lax.all_to_all(lax.all_to_all(sorted_pieces, 'sec', split_axis=0, concat_...]
    div x6, other arithmetic: 20.3 us -> 12.7 us  [local_solve(): correction = inside * (window + neighbours(jnp.pad(correction, 1))) / 6.0]
    all_to_all x8 -> x0, local copies, waits for them, and re-layouts: 7.08 us -> none  [the longest x1 1.81 us: shards(): lax.all_to_all(sorted_pieces, 'sec', split_axis=0, concat_axis=0, tiled=T...]
  transfers between devices with their start and end apart: 30 -> 23, of which waited for: 12 -> 12; matrix products, arithmetic and copies ran while one was open for 28% -> 31% of each run, Pallas kernels for 0% -> 0%
where the time goes in v1:
time: 707 us; the launch traced here: 696 us
  waiting for transfers between devices  289 us (41%)
  local copies, waits for them, and re-layouts  95.1 us (13%)
  starting transfers between devices  86.8 us (12%)
  matrix products  86.2 us (12%)
  blocking collectives  76.9 us (11%)
  other arithmetic  43.7 us (6%)
  between operations  18 us (3%)
    all_gather x1, waiting for transfers between devices, shards(): every_target = lax.all_gather(target_stress[0, 0], ('sec', 'dom'))  133 us
    psum x1, waiting for transfers between devices, shards(): lax.psum((gradients[0].astype(jnp.float32), gradients[1].astype(jnp.float...  105 us
    ppermute x21, starting transfers between devices, shifted_2(): return lax.ppermute(x, axis, pairs)  86.8 us
    conv_general_dilated x5, matrix products, conv_layer(): lax.conv_general_dilated(inputs, kernel, (stride, stride, stride), ((1, 1...  85.6 us
    psum x1, blocking collectives, shards(): lax.psum((gradients[0].astype(jnp.float32), gradients[1].astype(jnp.float...  76.9 us
    ppermute x21, waiting for transfers between devices, shifted_2(): return lax.ppermute(x, axis, pairs)  50.4 us
    convert_element_type x5, local copies, waits for them, and re-layouts, pick_blocks(): return jnp.take(blocks, chosen, axis=0).astype(jnp.bfloat16)  40.7 us
  transfers between devices with their start and end apart: 23, of which 12 were waited for; matrix products, arithmetic and copies ran while one was open for 31% of the time, Pallas kernels for 0%

profile of v1, /device:TPU:1, one launch (start us, length us, event | category | flops | bytes accessed | tf_op | source)
XLA Modules:
  0.0 695.7 jit_solution(13956518993805165915)
XLA Ops:
  9.3 9.6 %collective-permute-start.1 = (bf16[32,1,128]{2,1,0:T(2,128)(2,1)S(1)}, bf16[32,1,128]{2,1,0:T(2,128)(2,1)S(1)}, u32[]{:S(2)}, u32[]{:S(2)}) collective-permute-start(bf16[32,1,128]{2,1,0:T(2,128)(2,1)S(1)} %slice.539), channel_id=1, source_target_pairs={{0,8},{1,9},{2,10},{3,11},{4,12},{5,13},{6,14},{7,15},{8,16},{9,17... | collective-permute-start | bytes 24584 | tf_op jit(solution)/shard_map/ppermute | solution.py:19
  23.3 4.8 collective-permute-start
  32.8 4.2 copy.108
  36.9 5.0 reshape.128
  47.0 7.4 %copy.72 = bf16[3,32,32,1,8,6]{4,0,5,2,1,3:T(4,128)(2,1)} copy(bf16[3,32,32,1,8,6]{2,1,5,4,0,3:T(8,128)(2,1)S(1)} %bitcast.125) | data formatting | bytes 589824 | tf_op jit(solution)/shard_map/jvp()/conv_general_dilated | solution.py:23
  57.3 13.5 %select_reduce_fusion.1 = (f32[64]{0:T(128)S(1)}, f32[16,16,8,3,64]{4,2,3,1,0:T(8,128)}) fusion(pred[8,3]{0,1:T(4,128)(4,1)S(1)} %copy-done.20, bf16[3,3,3,3,64]{4,3,2,1,0:T(4,128)(2,1)S(1)} %copy-done.22, bf16[3,32,32,1,7,2]{4,0,5,2,1,3:T(4,128)(2,1)S(1)} %slice.398, bf16[3,32,32,1,8,6]{4,0,5,2,1,3:T(4,128)(2,1)} %copy.72), kind=kOutput, calls=%fused_computation.21 | convolution fusion | flops 63433664 | bytes 1964440 | tf_op jit(solution)/shard_map/jvp()/conv_general_dilated | solution.py:23
  70.8 4.4 select_reduce_fusion
  78.0 4.4 collective-permute-start.3
  83.8 4.7 collective-permute-done.4
  92.2 7.7 %collective-permute-done.6 = bf16[36,2,128]{2,1,0:T(2,128)(2,1)S(1)} collective-permute-done((bf16[36,2,128]{2,1,0:T(2,128)(2,1)S(1)}, bf16[36,2,128]{2,1,0:T(2,128)(2,1)S(1)}, u32[]{:S(2)}, u32[]{:S(2)}) %collective-permute-start.6) | collective-permute-done | bytes 18464 | tf_op jit(solution)/shard_map/ppermute | solution.py:19
  100.2 4.8 collective-permute-start.7
  109.7 4.4 collective-permute-done.8
  124.8 7.4 %collective-permute-start.10 = (bf16[1,32,128]{2,1,0:T(8,128)(2,1)S(1)}, bf16[1,32,128]{2,1,0:T(8,128)(2,1)S(1)}, u32[]{:S(2)}, u32[]{:S(2)}) collective-permute-start(bf16[1,32,128]{2,1,0:T(8,128)(2,1)S(1)} %get-tuple-element.44), channel_id=1, source_target_pairs={{0,32},{1,33},{2,34},{3,35},{4,36},{5,37},{6,38},{7,39},{8,40},{9,... | collective-permute-start | bytes 24584 | tf_op jit(solution)/shard_map/ppermute | solution.py:19
  136.3 4.7 collective-permute-done.9
  141.1 8.1 %collective-permute-start.12 = (bf16[34,1,128]{2,1,0:T(2,128)(2,1)S(1)}, bf16[34,1,128]{2,1,0:T(2,128)(2,1)S(1)}, u32[]{:S(2)}, u32[]{:S(2)}) collective-permute-start(bf16[34,1,128]{2,1,0:T(2,128)(2,1)S(1)} %get-tuple-element.50), channel_id=1, source_target_pairs={{0,8},{1,9},{2,10},{3,11},{4,12},{5,13},{6,14},{7,15},{8,16},{9,17... | collective-permute-start | bytes 26120 | tf_op jit(solution)/shard_map/ppermute | solution.py:19
  152.8 7.1 %collective-permute-done.11 = bf16[34,1,128]{2,1,0:T(2,128)(2,1)S(1)} collective-permute-done((bf16[34,1,128]{2,1,0:T(2,128)(2,1)S(1)}, bf16[34,1,128]{2,1,0:T(2,128)(2,1)S(1)}, u32[]{:S(2)}, u32[]{:S(2)}) %collective-permute-start.11) | collective-permute-done | bytes 8736 | tf_op jit(solution)/shard_map/ppermute | solution.py:19
  160.2 5.1 collective-permute-start.13
  170.8 4.3 collective-permute-done.14
  175.9 5.4 collective-permute-start.15
  182.9 7.7 %collective-permute-done.16 = bf16[2,32,128]{2,1,0:T(8,128)(2,1)S(1)} collective-permute-done((bf16[2,32,128]{2,1,0:T(8,128)(2,1)S(1)}, bf16[2,32,128]{2,1,0:T(8,128)(2,1)S(1)}, u32[]{:S(2)}, u32[]{:S(2)}) %collective-permute-start.16) | collective-permute-done | bytes 16416 | tf_op jit(solution)/shard_map/ppermute | solution.py:19
  194.9 7.1 %collective-permute-done.18 = bf16[36,2,128]{2,1,0:T(2,128)(2,1)S(1)} collective-permute-done((bf16[36,2,128]{2,1,0:T(2,128)(2,1)S(1)}, bf16[36,2,128]{2,1,0:T(2,128)(2,1)S(1)}, u32[]{:S(2)}, u32[]{:S(2)}) %collective-permute-start.18) | collective-permute-done | bytes 18464 | tf_op jit(solution)/shard_map/ppermute | solution.py:19
  203.1 5.7 collective-permute-start.19
  210.9 4.3 copy.82
  233.1 35.8 %copy.90 = bf16[1,3,32,32,32]{1,0,4,3,2:T(2,128)(2,1)} copy(bf16[1,3,32,32,32]{4,3,2,1,0:T(8,128)(2,1)} %convert_element_type.217) | data formatting | bytes 393216 | tf_op jit(solution)/shard_map/convert_element_type | solution.py:57
  270.2 12.6 %collective-permute-start.20 = (bf16[36,36,2]{2,1,0:T(8,128)(2,1)S(1)}, bf16[36,36,2]{2,1,0:T(8,128)(2,1)S(1)}, u32[]{:S(2)}, u32[]{:S(2)}) collective-permute-start(bf16[36,36,2]{2,1,0:T(8,128)(2,1)S(1)} %copy-done.17), channel_id=1, source_target_pairs={{1,0},{2,1},{3,2},{4,3},{5,4},{6,5},{7,6},{8,7},{9,8},{10,9},{11,1... | collective-permute-start | bytes 15560 | tf_op jit(solution)/shard_map/ppermute | solution.py:19
  293.0 132.8 %all-gather.3.cloned.1.call-done = bf16[256,1,3072]{2,1,0:T(2,128)(2,1)} async-done(((bf16[1,1,3072]{2,1,0:T(2,128)(2,1)}), bf16[256,1,3072]{2,1,0:T(2,128)(2,1)}) %all-gather.3.cloned.1.call-update) | async-done | bytes 1572880 | tf_op jit(solution)/shard_map/all_gather | solution.py:164
  427.0 7.2 %fusion.32 = f32[3,3,3,64,128]{4,3,2,1,0:T(8,128)} fusion(f32[1,8,8,8,128]{4,0,3,2,1:T(1,128)S(1)} %bitcast.138, bf16[16,16,1,16,64]{4,1,3,0,2:T(8,128)(2,1)} %slice.407), kind=kOutput, calls=%fused_computation.69 | convolution fusion | flops 199565312 | bytes 1671168 | tf_op jit(solution)/shard_map/transpose(jvp())/conv_general_dilated | solution.py:23
  434.3 16.2 %multiply_reduce_fusion = (f32[64]{0:T(128)S(1)}, f32[1,16,16,16,64]{4,0,3,2,1:T(1,128)S(1)}) fusion(f32[1,16,16,16,64]{4,0,3,2,1:T(1,128)} %bitcast.134, f32[1,16,16,16,64]{4,0,3,2,1:T(1,128)S(1)} %bitcast.131, f32[1,16,16,16,64]{4,0,3,2,1:T(1,128)} %bitcast.132, f32[1,16,16,16,64]{4,0,3,2,1:T(1,128)} %bitcast.133, f32[1,8,8,8,128]{4,0,3,2,1:T(1,128)S(1)} %bitcast.139, ...), kind=kOutput, calls=%fused_computation.35 | convolution fusion | flops 201179072 | bytes 5947648 | tf_op jit(solution)/shard_map/transpose(jvp())/conv_general_dilated | solution.py:23
  452.2 4.8 fusion.82
  457.1 47.2 %fusion.38 = f32[3,3,3,3,64]{4,3,2,1,0:T(4,128)S(1)} fusion(bf16[1,3,32,32,32]{1,0,4,3,2:T(2,128)(2,1)S(1)} %bitcast.117, f32[1,16,16,16,64]{4,0,3,2,1:T(1,128)S(1)} %get-tuple-element.21, f32[64]{0:T(128)S(1)} %negate_multiply_fusion), kind=kOutput, calls=%fused_computation.72 | convolution fusion | flops 40140544 | bytes 1266176 | tf_op jit(solution)/shard_map/transpose(jvp())/conv_general_dilated | solution.py:23
  504.4 76.9 %all-reduce.7 = (f32[3,3,3,3,64]{4,3,2,1,0:T(4,128)}, f32[64]{0:T(128)}, f32[128,6]{0,1:T(8,128)}) all-reduce(f32[3,3,3,3,64]{4,3,2,1,0:T(4,128)S(1)} %fusion.38, f32[64]{0:T(128)S(1)} %get-tuple-element.64, f32[128,6]{0,1:T(8,128)S(1)} %fusion.41), channel_id=1, replica_groups=mesh['sec'=2,'dom'=128] {'sec','dom'}, use_global_device_ids=true, to_apply=%region_4.5 | all-reduce | flops 6016 | bytes 48128 | tf_op jit(solution)/shard_map/psum | solution.py:173
  581.3 105.1 %all-reduce.10.cloned.1.call-done = f32[3,3,3,64,128]{4,3,2,1,0:T(8,128)} async-done(((f32[3,3,3,64,128]{4,3,2,1,0:T(8,128)}), f32[3,3,3,64,128]{4,3,2,1,0:T(8,128)}) %all-reduce.10.cloned.1.call-update) | async-done | bytes 884752 | tf_op jit(solution)/shard_map/psum | solution.py:173
  (184 shorter events, 97.3 us)
Async XLA Ops:
  7.2 184.8 %copy-start = (bf16[3,3,3,64,128]{4,3,2,1,0:T(8,128)(2,1)S(1)}, bf16[3,3,3,64,128]{4,3,2,1,0:T(8,128)(2,1)}, u32[]{:S(2)}) copy-start(bf16[3,3,3,64,128]{4,3,2,1,0:T(8,128)(2,1)} %param.11) | copy-start | bytes 1327108
  7.2 418.6 %all-gather.3.cloned.1.call-start = ((), (), s32[]{:S(2)}) async-start(), calls=%async_computation.1 | async-start | bytes 3158016 | tf_op jit(solution)/shard_map/all_gather | solution.py:164
  7.9 678.5 %all-reduce.10.cloned.1.call-start = ((), (), s32[]{:S(2)}) async-start(), calls=%async_computation | async-start | bytes 1769472 | tf_op jit(solution)/shard_map/psum | solution.py:173
  9.3 67.0 %collective-permute-start.1 = (bf16[32,1,128]{2,1,0:T(2,128)(2,1)S(1)}, bf16[32,1,128]{2,1,0:T(2,128)(2,1)S(1)}, u32[]{:S(2)}, u32[]{:S(2)}) collective-permute-start(bf16[32,1,128]{2,1,0:T(2,128)(2,1)S(1)} %slice.539), channel_id=1, source_target_pairs={{0,8},{1,9},{2,10},{3,11},{4,12},{5,13},{6,14},{7,15},{8,16},{9,17... | collective-permute-start | bytes 24584 | tf_op jit(solution)/shard_map/ppermute | solution.py:19
  19.8 55.5 %collective-permute-start.2 = (bf16[32,32,1]{2,1,0:T(8,128)(2,1)}, bf16[32,32,1]{2,1,0:T(8,128)(2,1)}, u32[]{:S(2)}, u32[]{:S(2)}) collective-permute-start(bf16[32,32,1]{2,1,0:T(8,128)(2,1)} %slice.538), channel_id=1, source_target_pairs={{0,1},{1,2},{2,3},{3,4},{4,5},{5,6},{6,7},{7,8},{8,9},{9,10},{10,1... | collective-permute-start | bytes 6152 | tf_op jit(solution)/shard_map/ppermute | solution.py:19
  23.3 53.0 %collective-permute-start = (bf16[1,32,128]{2,1,0:T(8,128)(2,1)S(1)}, bf16[1,32,128]{2,1,0:T(8,128)(2,1)S(1)}, u32[]{:S(2)}, u32[]{:S(2)}) collective-permute-start(bf16[1,32,128]{2,1,0:T(8,128)(2,1)S(1)} %fusion.74), channel_id=1, source_target_pairs={{0,32},{1,33},{2,34},{3,35},{4,36},{5,37},{6,38},{7,39},{8,40},{9,... | collective-permute-start | bytes 24584 | tf_op jit(solution)/shard_map/ppermute | solution.py:19
  78.0 5.8 collective-permute-start.3
  82.5 6.0 collective-permute-start.4
  88.5 3.7 collective-permute-start.5
  90.9 9.0 %collective-permute-start.6 = (bf16[36,2,128]{2,1,0:T(2,128)(2,1)S(1)}, bf16[36,2,128]{2,1,0:T(2,128)(2,1)S(1)}, u32[]{:S(2)}, u32[]{:S(2)}) collective-permute-start(bf16[36,2,128]{2,1,0:T(2,128)(2,1)S(1)} %get-tuple-element.49), channel_id=1, source_target_pairs={{8,0},{9,1},{10,2},{11,3},{12,4},{13,5},{14,6},{15,7},{16,8},{17,9... | collective-permute-start | bytes 55304 | tf_op jit(solution)/shard_map/ppermute | solution.py:19
  100.2 9.4 %collective-permute-start.7 = (bf16[36,36,2]{2,1,0:T(8,128)(2,1)S(1)}, bf16[36,36,2]{2,1,0:T(8,128)(2,1)S(1)}, u32[]{:S(2)}, u32[]{:S(2)}) collective-permute-start(bf16[36,36,2]{2,1,0:T(8,128)(2,1)S(1)} %get-tuple-element.54), channel_id=1, source_target_pairs={{0,1},{1,2},{2,3},{3,4},{4,5},{5,6},{6,7},{7,8},{8,9},{9,10},{10,1... | collective-permute-start | bytes 15560 | tf_op jit(solution)/shard_map/ppermute | solution.py:19
  105.0 9.0 %collective-permute-start.8 = (bf16[36,36,2]{2,1,0:T(8,128)(2,1)S(1)}, bf16[36,36,2]{2,1,0:T(8,128)(2,1)S(1)}, u32[]{:S(2)}, u32[]{:S(2)}) collective-permute-start(bf16[36,36,2]{2,1,0:T(8,128)(2,1)S(1)} %get-tuple-element.55), channel_id=1, source_target_pairs={{1,0},{2,1},{3,2},{4,3},{5,4},{6,5},{7,6},{8,7},{9,8},{10,9},{11,1... | collective-permute-start | bytes 15560 | tf_op jit(solution)/shard_map/ppermute | solution.py:19
  124.8 11.5 %collective-permute-start.10 = (bf16[1,32,128]{2,1,0:T(8,128)(2,1)S(1)}, bf16[1,32,128]{2,1,0:T(8,128)(2,1)S(1)}, u32[]{:S(2)}, u32[]{:S(2)}) collective-permute-start(bf16[1,32,128]{2,1,0:T(8,128)(2,1)S(1)} %get-tuple-element.44), channel_id=1, source_target_pairs={{0,32},{1,33},{2,34},{3,35},{4,36},{5,37},{6,38},{7,39},{8,40},{9,... | collective-permute-start | bytes 24584 | tf_op jit(solution)/shard_map/ppermute | solution.py:19
  134.8 30.5 %copy-start.1 = (f32[16,16,8,3,64]{4,2,3,1,0:T(8,128)}, f32[16,16,8,3,64]{4,2,3,1,0:T(8,128)S(1)}, u32[]{:S(2)}) copy-start(f32[16,16,8,3,64]{4,2,3,1,0:T(8,128)S(1)} %get-tuple-element.23) | copy-start | bytes 4718596
  135.0 6.0 collective-permute-start.9
  141.1 11.7 %collective-permute-start.12 = (bf16[34,1,128]{2,1,0:T(2,128)(2,1)S(1)}, bf16[34,1,128]{2,1,0:T(2,128)(2,1)S(1)}, u32[]{:S(2)}, u32[]{:S(2)}) collective-permute-start(bf16[34,1,128]{2,1,0:T(2,128)(2,1)S(1)} %get-tuple-element.50), channel_id=1, source_target_pairs={{0,8},{1,9},{2,10},{3,11},{4,12},{5,13},{6,14},{7,15},{8,16},{9,17... | collective-permute-start | bytes 26120 | tf_op jit(solution)/shard_map/ppermute | solution.py:19
  151.5 8.4 %collective-permute-start.11 = (bf16[34,1,128]{2,1,0:T(2,128)(2,1)S(1)}, bf16[34,1,128]{2,1,0:T(2,128)(2,1)S(1)}, u32[]{:S(2)}, u32[]{:S(2)}) collective-permute-start(bf16[34,1,128]{2,1,0:T(2,128)(2,1)S(1)} %get-tuple-element.51), channel_id=1, source_target_pairs={{8,0},{9,1},{10,2},{11,3},{12,4},{13,5},{14,6},{15,7},{16,8},{17,9... | collective-permute-start | bytes 26120 | tf_op jit(solution)/shard_map/ppermute | solution.py:19
  160.2 10.6 %collective-permute-start.13 = (bf16[34,34,1]{2,1,0:T(8,128)(2,1)S(1)}, bf16[34,34,1]{2,1,0:T(8,128)(2,1)S(1)}, u32[]{:S(2)}, u32[]{:S(2)}) collective-permute-start(bf16[34,34,1]{2,1,0:T(8,128)(2,1)S(1)} %get-tuple-element.56), channel_id=1, source_target_pairs={{1,0},{2,1},{3,2},{4,3},{5,4},{6,5},{7,6},{8,7},{9,8},{10,9},{11,1... | collective-permute-start | bytes 6944 | tf_op jit(solution)/shard_map/ppermute | solution.py:19
  168.8 6.3 collective-permute-start.14
  175.9 7.0 %collective-permute-start.15 = (bf16[2,32,128]{2,1,0:T(8,128)(2,1)S(1)}, bf16[2,32,128]{2,1,0:T(8,128)(2,1)S(1)}, u32[]{:S(2)}, u32[]{:S(2)}) collective-permute-start(bf16[2,32,128]{2,1,0:T(8,128)(2,1)S(1)} %get-tuple-element.58), channel_id=1, source_target_pairs={{0,32},{1,33},{2,34},{3,35},{4,36},{5,37},{6,38},{7,39},{8,40},{9,... | collective-permute-start | bytes 49160 | tf_op jit(solution)/shard_map/ppermute | solution.py:19
  181.6 9.0 %collective-permute-start.16 = (bf16[2,32,128]{2,1,0:T(8,128)(2,1)S(1)}, bf16[2,32,128]{2,1,0:T(8,128)(2,1)S(1)}, u32[]{:S(2)}, u32[]{:S(2)}) collective-permute-start(bf16[2,32,128]{2,1,0:T(8,128)(2,1)S(1)} %get-tuple-element.59), channel_id=1, source_target_pairs={{32,0},{33,1},{34,2},{35,3},{36,4},{37,5},{38,6},{39,7},{40,8},{41... | collective-permute-start | bytes 49160 | tf_op jit(solution)/shard_map/ppermute | solution.py:19
  190.6 4.3 collective-permute-start.17
  193.5 21.8 %copy-start.15 = (bf16[8,8,8,1,128]{4,2,1,0,3:T(8,128)(2,1)}, bf16[8,8,8,1,128]{4,2,1,0,3:T(8,128)(2,1)S(1)}, u32[]{:S(2)}) copy-start(bf16[8,8,8,1,128]{4,2,1,0,3:T(8,128)(2,1)S(1)} %get-tuple-element.68) | copy-start | bytes 393220
  193.5 8.5 %collective-permute-start.18 = (bf16[36,2,128]{2,1,0:T(2,128)(2,1)S(1)}, bf16[36,2,128]{2,1,0:T(2,128)(2,1)S(1)}, u32[]{:S(2)}, u32[]{:S(2)}) collective-permute-start(bf16[36,2,128]{2,1,0:T(2,128)(2,1)S(1)} %get-tuple-element.47), channel_id=1, source_target_pairs={{8,0},{9,1},{10,2},{11,3},{12,4},{13,5},{14,6},{15,7},{16,8},{17,9... | collective-permute-start | bytes 55304 | tf_op jit(solution)/shard_map/ppermute | solution.py:19
  203.1 79.6 %collective-permute-start.19 = (bf16[36,36,2]{2,1,0:T(8,128)(2,1)}, bf16[36,36,2]{2,1,0:T(8,128)(2,1)}, u32[]{:S(2)}, u32[]{:S(2)}) collective-permute-start(bf16[36,36,2]{2,1,0:T(8,128)(2,1)} %get-tuple-element.52), channel_id=1, source_target_pairs={{0,1},{1,2},{2,3},{3,4},{4,5},{5,6},{6,7},{7,8},{8,9},{9,10},{10,1... | collective-permute-start | bytes 15560 | tf_op jit(solution)/shard_map/ppermute | solution.py:19
  233.1 37.1 %copy-start.17 = (bf16[36,36,2]{2,1,0:T(8,128)(2,1)S(1)}, bf16[36,36,2]{2,1,0:T(8,128)(2,1)}, u32[]{:S(2)}) copy-start(bf16[36,36,2]{2,1,0:T(8,128)(2,1)} %get-tuple-element.53) | copy-start | bytes 15556
  270.2 13.7 %collective-permute-start.20 = (bf16[36,36,2]{2,1,0:T(8,128)(2,1)S(1)}, bf16[36,36,2]{2,1,0:T(8,128)(2,1)S(1)}, u32[]{:S(2)}, u32[]{:S(2)}) collective-permute-start(bf16[36,36,2]{2,1,0:T(8,128)(2,1)S(1)} %copy-done.17), channel_id=1, source_target_pairs={{1,0},{2,1},{3,2},{4,3},{5,4},{6,5},{7,6},{8,7},{9,8},{10,9},{11,1... | collective-permute-start | bytes 15560 | tf_op jit(solution)/shard_map/ppermute | solution.py:19
  289.8 137.0 %copy-start.18 = (f32[8,8,8,1,128]{4,2,3,1,0:T(8,128)S(1)}, f32[8,8,8,1,128]{4,2,3,1,0:T(8,128)}, u32[]{:S(2)}) copy-start(f32[8,8,8,1,128]{4,2,3,1,0:T(8,128)} %get-tuple-element.69) | copy-start | bytes 786436
  434.2 22.8 %slice-start = ((s8[16777216]{0:T(1024)(128)(4,1)}), s8[4194304]{0:T(1024)(128)(4,1)S(1)}, s32[]{:S(2)}) async-start(s8[16777216]{0:T(1024)(128)(4,1)} %bitcast.116), calls=%async_computation.2 | async-start | bytes 8388608
  434.3 22.8 %slice-start.1 = ((s8[16777216]{0:T(1024)(128)(4,1)}), s8[4194304]{0:T(1024)(128)(4,1)S(1)}, s32[]{:S(2)}) async-start(s8[16777216]{0:T(1024)(128)(4,1)} %bitcast.116), calls=%async_computation.3 | async-start | bytes 8388608
  434.3 22.8 %slice-start.2 = ((s8[16777216]{0:T(1024)(128)(4,1)}), s8[4194304]{0:T(1024)(128)(4,1)S(1)}, s32[]{:S(2)}) async-start(s8[16777216]{0:T(1024)(128)(4,1)} %bitcast.116), calls=%async_computation.4 | async-start | bytes 8388608
  457.0 47.2 %copy-start.16 = (bf16[8,8,8,1,128]{4,2,1,0,3:T(8,128)(2,1)S(1)}, bf16[8,8,8,1,128]{4,2,1,0,3:T(8,128)(2,1)}, u32[]{:S(2)}) copy-start(bf16[8,8,8,1,128]{4,2,1,0,3:T(8,128)(2,1)} %copy-done.15) | copy-start | bytes 393220
  (19 other events, 149.5 us)
Sparse Core Ops, SparseCore 0:
  9.9 415.8 all-gather.2
  434.3 252.0 all-reduce.9

commit v2 on v1

v2 whole, which is shorter than its diff:
```python
import functools

import jax
import jax.numpy as jnp
from jax import lax
from jax.experimental import pallas as pl
from jax.experimental.pallas import tpu as pltpu
from jax.sharding import PartitionSpec as P

F32 = jnp.float32
BF16 = jnp.bfloat16
NORM_EPS = 1e-05
MESH = pl.DeviceIdType.MESH
RANKS = 16
BIG = 112
SMALL = 8
PIECE = 128


def iota(shape, dim):
    return lax.broadcasted_iota(jnp.int32, shape, dim)


def dot(left, right, cl, cr):
    return lax.dot_general(
        left, right, (((cl,), (cr,)), ((), ())), preferred_element_type=F32
    )


def lanes(t, width=128):
    return slice(t * width, (t + 1) * width)


def build_first_weights(sel, w1_ref, wg, table):
    for kx in range(3):
        for kz in range(3):
            rows = []
            for ky in range(3):
                w = w1_ref[kx, ky, kz].astype(F32)
                rows.append(jnp.concatenate([w, w], axis=1))
            for g in range(4):
                mixed = jnp.zeros((3, 128), F32)
                for ky in range(3):
                    mixed = jnp.where(lax.rem(sel + ky, 4) == g, rows[ky], mixed)
                for i in range(3):
                    wg[(kx * 3 + i) * 4 + g, kz : kz + 1, :] = mixed[i : i + 1]
    row = iota((32, 128), 0)
    upper = (iota((32, 128), 1) >= 64).astype(jnp.int32)
    for t in range(8):
        tap = row - 2 * (2 * t + upper) + 1
        masks = [(tap == k).astype(F32) for k in range(3)]

        def fill(c, carry):
            w = wg[c]
            block = masks[0] * w[0:1] + masks[1] * w[1:2] + masks[2] * w[2:3]
            table[pl.ds(pl.multiple_of(c * 32, 32), 32), lanes(t)] = block.astype(BF16)
            return carry

        lax.fori_loop(0, 36, fill, 0)


def build_second_weights(w2_ref, wp):
    for kx in range(3):
        for ky in range(3):
            k = kx * 3 + ky
            wp[k, 0:64, :] = jnp.zeros((64, 128), BF16)
            for kz in range(3):
                wp[k, 64 + kz * 64 : 128 + kz * 64, :] = w2_ref[kx, ky, kz]


def build_rows(sel, vel_ref, mx):
    keep = lax.shift_right_logical(iota((8, 128), 1), 5) == sel
    top = iota((8, 128), 0) == 0
    for i in range(3):
        mx[i, 0, 0] = jnp.zeros((16, 128), BF16)

        def one(x):
            d = [
                jnp.where(keep, vel_ref[0, i, x, pl.ds(o, 8, stride=4), :], 0.0)
                for o in range(4)
            ]
            before = jnp.where(top, 0.0, pltpu.roll(d[3], 1, 0))
            even = before + pltpu.roll(d[0], 32, 1) + pltpu.roll(d[1], 64, 1)
            odd = d[1] + pltpu.roll(d[2], 32, 1) + pltpu.roll(d[3], 64, 1)
            return jnp.concatenate([even, odd], axis=0).astype(BF16)

        def pair(m, carry):
            mx[i, m, 1] = one(2 * m)
            mx[i, m + 1, 0] = one(2 * m + 1)
            return carry

        lax.fori_loop(0, 16, pair, 0)


def first_rows(mx, kx, i):
    if kx == 0:
        part = mx[i, 0:16, 0]
    elif kx == 1:
        part = mx[i, 0:16, 1]
    else:
        part = mx[i, 1:17, 0]
    return part.reshape(256, 128)


def fold_channels(row):
    total = row[:, lanes(0)]
    for t in range(1, 8):
        total = total + row[:, lanes(t)]
    return total + pltpu.roll(total, 64, 1)


def first_layer(mx, table, cen):
    left = jnp.concatenate(
        [first_rows(mx, kx, i) for kx in range(3) for i in range(3)], axis=1
    )
    for t in range(4):
        cen[:, lanes(t, 256)] = dot(left, table[:, lanes(t, 256)], 1, 0)


def normalise(cen, gain_ref):
    total = fold_channels(jnp.sum(cen[...], axis=0, keepdims=True))
    mean = total * (1.0 / 4096.0)
    square = jnp.zeros((1, 128), F32)
    for t in range(8):
        c = cen[:, lanes(t)] - mean
        cen[:, lanes(t)] = c
        square = square + jnp.sum(c * c, axis=0, keepdims=True)
    var = (square + pltpu.roll(square, 64, 1)) * (1.0 / 4096.0)
    gain = gain_ref[0:1, :]
    gain = jnp.concatenate([gain, gain], axis=1)
    return gain, lax.rsqrt(var + NORM_EPS)


def hidden_rows(cen, scale, lhs):
    top = iota((16, 8, 128), 1) == 0
    for k in range(9):
        lhs[k, :, 0:128] = jnp.zeros((64, 128), BF16)
    for t in range(8):
        n = cen[:, lanes(t)] * scale
        h = (n * jax.nn.sigmoid(n)).reshape(16, 2, 8, 128)
        even, odd = h[:, 0], h[:, 1]
        before = jnp.where(top, 0.0, pltpu.roll(odd, 1, 1))
        for ky, plane in ((0, before), (1, even), (2, odd)):
            plane = plane.reshape(8, 2, 8, 128)
            low, high = plane[:, 0], plane[:, 1]
            shifted = jnp.concatenate([jnp.zeros((1, 8, 128), F32), high[:7]], axis=0)
            for kx, part in ((0, shifted), (1, low), (2, high)):
                lhs[kx * 3 + ky, :, lanes(t + 1)] = part.reshape(64, 128).astype(BF16)


def second_rows(lhs, k):
    return jnp.concatenate(
        [lhs[k, :, p * 128 : p * 128 + 256] for p in range(8)], axis=0
    )


def second_layer(lhs, wp):
    out = jnp.zeros((512, 128), F32)
    for k in range(9):
        out = out + dot(second_rows(lhs, k), wp[k], 1, 0)
    return out


def cell_order():
    r, c = iota((512, 512), 0), iota((512, 512), 1)
    same = (lax.shift_right_logical(c, 3) == lax.bitwise_and(r, 63)) & (
        lax.bitwise_and(c, 7) == lax.shift_right_logical(r, 6)
    )
    return same.astype(F32).astype(BF16)


def target_rows(pieces):
    row = iota((512, 16), 0)
    which = lax.shift_right_logical(lax.bitwise_and(row, 63), 2)
    pick = (which == iota((512, 16), 1)).astype(F32).astype(BF16)
    spread = dot(pick, pieces.astype(BF16), 1, 0)
    row, lane = iota((512, 256), 0), iota((512, 256), 1)
    cell = lax.bitwise_and(row, 3) * 8 + lax.shift_right_logical(row, 6)
    kept = jnp.where(lax.bitwise_and(lane, 31) == cell, spread, 0.0).astype(BF16)
    r, c = iota((256, 128), 0), iota((256, 128), 1)
    collect = (lax.shift_right_logical(r, 5) == c).astype(F32).astype(BF16)
    return dot(kept, collect, 1, 0)


def second_gradient(lhs, dout, gb):
    for k in range(9):
        grad = dot(second_rows(lhs, k), dout, 0, 0)
        gb[k * 192 : (k + 1) * 192, :] = grad[64:256].astype(BF16)


def hidden_gradient(dout, wp, back):
    for k in range(9):
        back[k] = dot(dout, wp[k], 1, 1).astype(F32)


def norm_backward(back, cen, gain, rstd, dn):
    scale = gain * rstd
    bottom = iota((8, 8, 128), 1) == 7
    sums = jnp.zeros((1, 128), F32)
    products = jnp.zeros((1, 128), F32)
    for t in range(8):
        planes = []
        for k in range(9):
            part = back[k, t * 64 : (t + 1) * 64, 128:256]
            if t < 7:
                part = part + back[k, (t + 1) * 64 : (t + 2) * 64, 0:128]
            planes.append(part.reshape(8, 8, 128))
        by_kx = []
        for kx in range(3):
            before = jnp.where(bottom, 0.0, pltpu.roll(planes[kx * 3], 7, 1))
            by_kx.append((planes[kx * 3 + 1], planes[kx * 3 + 2] + before))
        parts = []
        for q in range(2):
            moved = jnp.concatenate(
                [by_kx[0][q][1:], jnp.zeros((1, 8, 128), F32)], axis=0
            )
            parts.append((by_kx[1][q], by_kx[2][q] + moved))
        dh = jnp.stack(
            [
                jnp.stack([parts[0][0], parts[1][0]], axis=1),
                jnp.stack([parts[0][1], parts[1][1]], axis=1),
            ],
            axis=1,
        ).reshape(256, 128)
        dh = dh.astype(BF16).astype(F32)
        c = cen[:, lanes(t)]
        n = c * scale
        s = jax.nn.sigmoid(n)
        d = dh * (s * (1.0 + n * (1.0 - s)))
        dn[:, lanes(t)] = d
        sums = sums + jnp.sum(d, axis=0, keepdims=True)
        products = products + jnp.sum(d * c, axis=0, keepdims=True)
    sums = (sums + pltpu.roll(sums, 64, 1)) * (1.0 / 4096.0)
    products = products + pltpu.roll(products, 64, 1)
    slope = products * (rstd * rstd * (1.0 / 4096.0))
    for t in range(8):
        d = dn[:, lanes(t)]
        dn[:, lanes(t)] = scale * (d - sums - cen[:, lanes(t)] * slope)
    return products * rstd


def first_gradient(sel, mx, dn, gs):
    right = dn[...].astype(BF16)
    row = iota((128, 128), 0)
    z = lax.bitwise_and(row, 31)
    upper = (iota((128, 128), 1) >= 64).astype(jnp.int32)
    for kx in range(3):
        for i in range(3):
            full = dot(first_rows(mx, kx, i), right, 0, 0)
            for kz in range(3):
                total = jnp.zeros((128, 128), F32)
                for t in range(8):
                    tap = z - 2 * (2 * t + upper) + 1
                    total = total + jnp.where(tap == kz, full[:, lanes(t)], 0.0)
                total = jnp.sum(total.reshape(4, 32, 128), axis=1)
                total = total + pltpu.roll(total, 64, 1)
                for ky in range(3):
                    value = jnp.zeros((1, 128), F32)
                    for g in range(4):
                        value = jnp.where(
                            lax.rem(sel + ky, 4) == g, total[g : g + 1], value
                        )
                    at = ((kx * 3 + ky) * 3 + kz) * 3 + i
                    gs[at : at + 1, :] = value


def cell_masks(coords):
    _, by, bz = coords
    y, z = iota((40, 256), 0), iota((40, 256), 1)
    in_y = (y < 32) | ((y < 34) & (by < 3)) | ((y >= 38) & (by > 0))
    in_z = (z < 128) | ((z < 130) & (bz < 7)) | ((z >= 254) & (bz > 0))
    return jnp.where(in_y & in_z, 1.0 / 6.0, 0.0).astype(F32)


def divergence(vel_ref, rim_x, rim_y, rim_z, flags, window):
    first_row = iota((32, 128), 0) == 0
    first_lane = iota((32, 128), 1) == 0

    def layer(x, before):
        ux, uy, uz = vel_ref[0, 0, x], vel_ref[0, 1, x], vel_ref[0, 2, x]
        y_rim = rim_y[pl.ds(x, 1), :] * flags[2]
        y_before = jnp.where(first_row, y_rim, pltpu.roll(uy, 1, 0))
        z_rim = pltpu.roll(rim_z[...], 128 - x if not isinstance(x, int) else 0, 1) * flags[4]
        z_before = jnp.where(first_lane, z_rim, pltpu.roll(uz, 1, 1))
        total = (ux - before) + (uy - y_before) + (uz - z_before)
        window[x + 2, 0:32, 0:128] = -total

    layer(0, rim_x[...] * flags[0])

    def step(x, carry):
        layer(x, vel_ref[0, 0, x - 1])
        return carry

    lax.fori_loop(1, 32, step, 0)


def pack_rim_z(vel_ref, send):
    lane = iota((32, 128), 1)
    packed = jnp.zeros((32, 128), F32)
    for x in range(32):
        moved = pltpu.roll(vel_ref[0, 2, x], (x + 1) % 128, 1)
        packed = jnp.where(lane == x, moved, packed)
    send[...] = packed


def pack_y(field, count, h, w, send):
    sub = iota((8, 128), 0)
    per = 8 // w
    for m in range(count // per):
        high = jnp.zeros((8, 128), F32)
        low = jnp.zeros((8, 128), F32)
        for j in range(per):
            x = m * per + j
            here = (sub >= j * w) & (sub < j * w + w)
            top = pltpu.roll(field[x, 24:32, 0:128], (j * w - (8 - h)) % 8, 0)
            bottom = field[x, 0:8, 0:128]
            if j:
                bottom = pltpu.roll(bottom, j * w, 0)
            high = jnp.where(here, top, high)
            low = jnp.where(here, bottom, low)
        send[0, m] = high
        send[1, m] = low


def unpack_y(field, count, h, w, got, flags):
    sub = iota((8, 128), 0)
    per = 8 // w
    for m in range(count // per):
        below, above = got[0, m] * flags[2], got[1, m] * flags[3]
        for j in range(per):
            lower = pltpu.roll(below, (8 - h - j * w) % 8, 0)
            upper = pltpu.roll(above, (-j * w) % 8, 0) if j else above
            field[m * per + j, 32:40, 0:128] = jnp.where(
                sub < h, upper, jnp.where(sub >= 8 - h, lower, 0.0)
            )


def pack_z(field, count, h, send):
    lane = iota((40, 128), 1)
    high = jnp.zeros((40, 128), F32)
    low = jnp.zeros((40, 128), F32)
    for x in range(count):
        here = (lane >= x * h) & (lane < x * h + h)
        own = field[x, :, 0:128]
        high = jnp.where(here, pltpu.roll(own, (x * h + h) % 128, 1), high)
        low = jnp.where(here, pltpu.roll(own, x * h, 1) if x else own, low)
    send[0] = high
    send[1] = low


def unpack_z(field, count, h, got, flags):
    lane = iota((40, 128), 1)
    below, above = got[0] * flags[4], got[1] * flags[5]
    for x in range(count):
        lower = pltpu.roll(below, (128 - h - x * h) % 128, 1)
        upper = pltpu.roll(above, (-x * h) % 128, 1) if x else above
        field[x, :, 128:256] = jnp.where(
            lane < h, upper, jnp.where(lane >= 128 - h, lower, 0.0)
        )


def neighbours(field, at):
    own = field[at]
    across = field[at - 1] + field[at + 1]
    along = pltpu.roll(own, 1, 0) + pltpu.roll(own, 39, 0)
    return own, across + along + pltpu.roll(own, 1, 1) + pltpu.roll(own, 255, 1)


def local_solve(window, mask, za, zb, flags, pressure, emit):
    def inside(xi):
        return jnp.where(xi < 2, flags[0], jnp.where(xi > 33, flags[1], 1.0))

    for z in (za, zb):
        z[0] = jnp.zeros((40, 256), F32)
        z[37] = jnp.zeros((40, 256), F32)

    def first(xi, carry):
        w = window[xi]
        if pressure is not None:
            own, around = neighbours(pressure, xi + 1)
            w = w - (6.0 * own - around)
            window[xi] = w
        za[xi + 1] = w * (mask[...] * inside(xi))
        return carry

    def sweep(source, target):
        def step(xi, carry):
            _, around = neighbours(source, xi + 1)
            target[xi + 1] = (window[xi] + around) * (mask[...] * inside(xi))
            return carry

        return step

    def last(xi, carry):
        _, around = neighbours(za, xi + 1)
        z = (window[xi] + around) * mask[...]
        emit(xi, z[0:32, 0:128])
        return carry

    lax.fori_loop(0, 36, first, 0)
    lax.fori_loop(0, 36, sweep(za, zb), 0)
    lax.fori_loop(1, 35, sweep(zb, za), 0)
    lax.fori_loop(2, 34, last, 0)


SCRATCH = dict(
    wg=((36, 8, 128), F32),
    table=((1152, 1024), BF16),
    mx=((3, 17, 2, 16, 128), BF16),
    cen=((256, 1024), F32),
    lhs=((9, 64, 1152), BF16),
    wp=((9, 256, 128), BF16),
    hp=((128, 128), BF16),
    back=((9, 512, 256), F32),
    dn=((256, 1024), F32),
    order=((512, 512), BF16),
    t1=((RANKS, 1, 256), F32),
    t2=((RANKS, RANKS, 1, 256), F32),
    stage=((RANKS, 1, 256), F32),
    t3=((RANKS, 1, 256), F32),
    pieces=((RANKS, 256), F32),
    gb=((RANKS * BIG, 128), BF16),
    gs=((RANKS * SMALL, 128), F32),
    r1=((RANKS, BIG, 128), BF16),
    r1s=((RANKS, SMALL, 128), F32),
    part=((RANKS, 8, 128), F32),
    r2=((RANKS, 8, 128), F32),
    whole=((RANKS, 8, 128), F32),
    gathered=((RANKS, PIECE, 128), BF16),
    rim_x=((32, 128), F32),
    rim_y=((32, 128), F32),
    rim_z=((32, 128), F32),
    rim_ys=((32, 128), F32),
    rim_zs=((32, 128), F32),
    window=((36, 40, 256), F32),
    press=((38, 40, 256), F32),
    za=((38, 40, 256), F32),
    zb=((38, 40, 256), F32),
    mask=((40, 256), F32),
    wys=((2, 9, 8, 128), F32),
    wyr=((2, 9, 8, 128), F32),
    wzs=((2, 40, 128), F32),
    wzr=((2, 40, 128), F32),
    pys=((2, 19, 8, 128), F32),
    pyr=((2, 19, 8, 128), F32),
    pzs=((2, 40, 128), F32),
    pzr=((2, 40, 128), F32),
)
GROUP_STEPS = ("t1", "t2", "t3", "g1", "g1s", "g2", "g3", "g4")
HALO_STEPS = ("rim", "wx", "wy", "wz", "px", "py", "pz")
SEMAPHORES = 16 * len(GROUP_STEPS) + 3 * len(HALO_STEPS)


def kernel(*refs):
    (sel_ref, asg_ref, vel_ref, w1_ref, gain_ref, w2_ref, head_ref, target_ref) = refs[:8]
    pressure_ref, pred_ref, grad_ref = refs[8:11]
    s = dict(zip(SCRATCH, refs[11 : 11 + len(SCRATCH)]))
    send_sem, recv_sem = refs[11 + len(SCRATCH) :]

    me = lax.axis_index("sec") * 128 + lax.axis_index("dom")
    a, b = lax.div(me, 16), lax.rem(me, 16)
    coords = (lax.div(me, 32), lax.rem(lax.div(me, 8), 4), lax.rem(me, 8))
    bx, by, bz = coords
    flags = [
        jnp.where(cond, 1.0, 0.0).astype(F32)
        for cond in (bx > 0, bx < 7, by > 0, by < 3, bz > 0, bz < 7)
    ]

    def device(f):
        return (lax.div(f, 128), lax.rem(f, 128))

    def box(x, y, z):
        return device(lax.rem(x + 8, 8) * 32 + lax.rem(y + 4, 4) * 8 + lax.rem(z + 8, 8))

    above = [box(bx + 1, by, bz), box(bx, by + 1, bz), box(bx, by, bz + 1)]
    below = [box(bx - 1, by, bz), box(bx, by - 1, bz), box(bx, by, bz - 1)]
    a_ranks = [None] + [lax.rem(a + j, RANKS) for j in range(1, RANKS)]
    b_ranks = [None] + [lax.rem(b + j, RANKS) for j in range(1, RANKS)]
    a_peers = [None] + [device(a_ranks[j] * 16 + b) for j in range(1, RANKS)]
    b_peers = [None] + [device(a * 16 + b_ranks[j]) for j in range(1, RANKS)]

    barrier = pltpu.get_barrier_semaphore()
    everyone = a_peers[1:] + b_peers[1:] + above + below
    for other in everyone:
        pl.semaphore_signal(barrier, inc=1, device_id=other, device_id_type=MESH)

    started = []
    flights = {}

    def start(step, at, source, target, other):
        base = (
            GROUP_STEPS.index(step) * 16
            if step in GROUP_STEPS
            else 16 * len(GROUP_STEPS) + 3 * HALO_STEPS.index(step)
        )
        copy = pltpu.make_async_remote_copy(
            src_ref=source,
            dst_ref=target,
            send_sem=send_sem.at[base + at],
            recv_sem=recv_sem.at[base + at],
            device_id=other,
            device_id_type=MESH,
        )
        copy.start()
        started.append(copy)
        flights.setdefault(step, []).append(copy)

    def arrive(step, sent=False):
        for copy in flights[step]:
            copy.wait_recv()
            if sent:
                copy.wait_send()
                started[:] = [other for other in started if other is not copy]

    sel = sel_ref[0, 0]
    build_first_weights(sel, w1_ref, s["wg"], s["table"])
    build_second_weights(w2_ref, s["wp"])
    s["hp"][...] = jnp.zeros((128, 128), BF16)
    s["hp"][:, 0:6] = head_ref[...]
    s["mask"][...] = cell_masks(coords)
    pack_rim_z(vel_ref, s["rim_zs"])
    s["rim_ys"][...] = vel_ref[0, 1, :, 31, :]

    pl.semaphore_wait(barrier, len(everyone))

    for j in range(1, RANKS):
        start("t1", j, target_ref.at[a_ranks[j]], s["t1"].at[a], a_peers[j])
    start("rim", 0, vel_ref.at[0, 0, 31], s["rim_x"], above[0])
    start("rim", 1, s["rim_ys"], s["rim_y"], above[1])
    start("rim", 2, s["rim_zs"], s["rim_z"], above[2])
    s["t1"][a] = target_ref[a]

    build_rows(sel, vel_ref, s["mx"])
    arrive("t1")
    for j in range(1, RANKS):
        start("t2", j, s["t1"], s["t2"].at[b], b_peers[j])
    s["t2"][b] = s["t1"][...]
    first_layer(s["mx"], s["table"], s["cen"])
    arrive("rim")
    window = s["window"]
    divergence(vel_ref, s["rim_x"], s["rim_y"], s["rim_z"], flags, window)
    own = (slice(0, 32), slice(0, 128))
    start("wx", 0, window.at[32:34, 0:32, 0:128], window.at[0:2, 0:32, 0:128], above[0])
    start("wx", 1, window.at[2:4, 0:32, 0:128], window.at[34:36, 0:32, 0:128], below[0])
    gain, rstd = normalise(s["cen"], gain_ref)
    arrive("t2")
    for q in range(RANKS):
        wanted = asg_ref[q * 16 + b]
        s["stage"][q] = s["t2"][lax.rem(wanted, 16), lax.div(wanted, 16)]
    for j in range(1, RANKS):
        start("t3", j, s["stage"].at[a_ranks[j]], s["t3"].at[a], a_peers[j])
    s["t3"][a] = s["stage"][a]
    hidden_rows(s["cen"], gain * rstd, s["lhs"])
    arrive("wx", True)
    pack_y(window, 36, 2, 2, s["wys"])
    start("wy", 0, s["wys"].at[0], s["wyr"].at[0], above[1])
    start("wy", 1, s["wys"].at[1], s["wyr"].at[1], below[1])

    out = second_layer(s["lhs"], s["wp"])
    sig = jax.nn.sigmoid(out)
    deep = (out * sig).astype(BF16)
    slope = sig * (1.0 + out * (1.0 - sig))
    stress = dot(deep, s["hp"][...], 1, 0)
    arrive("t3")
    for q in range(RANKS):
        s["pieces"][q : q + 1, :] = s["t3"][q]
    error = (stress - target_rows(s["pieces"][...])).astype(BF16)
    dout = dot(error, s["hp"][...], 1, 1).astype(BF16).astype(F32) * slope
    dout = dout.astype(BF16)

    s["gb"][1728:1792, :] = jnp.zeros((64, 128), BF16)
    second_gradient(s["lhs"], dout, s["gb"])
    for j in range(1, RANKS):
        rows = pl.ds(pl.multiple_of(a_ranks[j] * BIG, 16), BIG)
        start("g1", j, s["gb"].at[rows], s["r1"].at[j], a_peers[j])

    arrive("wy")
    unpack_y(window, 36, 2, 2, s["wyr"], flags)
    pack_z(window, 36, 2, s["wzs"])
    start("wz", 0, s["wzs"].at[0], s["wzr"].at[0], above[2])
    start("wz", 1, s["wzs"].at[1], s["wzr"].at[1], below[2])

    gs = s["gs"]
    gs[...] = jnp.zeros((128, 128), F32)
    gs[82:88, :] = dot(error, deep, 0, 0)[0:6]
    hidden_gradient(dout, s["wp"], s["back"])
    gs[81:82, :] = norm_backward(s["back"], s["cen"], gain, rstd, s["dn"])
    first_gradient(sel, s["mx"], s["dn"], gs)
    for j in range(1, RANKS):
        rows = pl.ds(pl.multiple_of(a_ranks[j] * SMALL, 8), SMALL)
        start("g1s", j, gs.at[rows], s["r1s"].at[j], a_peers[j])
    pred_ref[...] = dot(stress.astype(BF16), cell_order(), 0, 0)[0:8]

    arrive("wz")
    unpack_z(window, 36, 2, s["wzr"], flags)
    press = s["press"]

    def keep(xi, z):
        press[xi + 1, 0:32, 0:128] = z

    local_solve(window, s["mask"], s["za"], s["zb"], flags, None, keep)
    start("px", 0, press.at[32:35, 0:32, 0:128], press.at[0:3, 0:32, 0:128], above[0])
    start("px", 1, press.at[3:6, 0:32, 0:128], press.at[35:38, 0:32, 0:128], below[0])

    arrive("g1")
    arrive("g1s")
    rows = pl.ds(pl.multiple_of(a * BIG, 16), BIG)
    big = s["gb"][rows, :].astype(F32)
    small = gs[pl.ds(pl.multiple_of(a * SMALL, 8), SMALL), :]
    for j in range(1, RANKS):
        big = big + s["r1"][j].astype(F32)
        small = small + s["r1s"][j]
    part = s["part"]
    part[0:14] = big.reshape(14, 8, 128)
    part[14] = small
    part[15] = jnp.zeros((8, 128), F32)
    for j in range(1, RANKS):
        start("g2", j, part.at[b_ranks[j]], s["r2"].at[j], b_peers[j])

    arrive("px", True)
    press[0:3, 0:32, 0:128] = press[0:3, 0:32, 0:128] * flags[0]
    press[35:38, 0:32, 0:128] = press[35:38, 0:32, 0:128] * flags[1]
    pack_y(press, 38, 3, 4, s["pys"])
    start("py", 0, s["pys"].at[0], s["pyr"].at[0], above[1])
    start("py", 1, s["pys"].at[1], s["pyr"].at[1], below[1])

    arrive("g2")
    total = part[b]
    for j in range(1, RANKS):
        total = total + s["r2"][j]
    s["whole"][b] = total
    for j in range(1, RANKS):
        start("g3", j, s["whole"].at[b], s["whole"].at[b], b_peers[j])

    arrive("py")
    unpack_y(press, 38, 3, 4, s["pyr"], flags)
    pack_z(press, 38, 3, s["pzs"])
    start("pz", 0, s["pzs"].at[0], s["pzr"].at[0], above[2])
    start("pz", 1, s["pzs"].at[1], s["pzr"].at[1], below[2])

    arrive("g3")
    gathered = s["gathered"]
    gathered[a] = s["whole"][...].reshape(PIECE, 128).astype(BF16)
    for j in range(1, RANKS):
        start("g4", j, gathered.at[a], gathered.at[a], a_peers[j])

    arrive("pz")
    unpack_z(press, 38, 3, s["pzr"], flags)

    def finish(xi, z):
        pressure_ref[xi - 2] = press[xi + 1, 0:32, 0:128] + z

    local_solve(window, s["mask"], s["za"], s["zb"], flags, press, finish)
    arrive("g4")
    grad_ref[...] = gathered[...]
    for copy in started:
        copy.wait_send()


def shards(
    velocity,
    first_kernel,
    norm_gain,
    second_kernel,
    head_weight,
    selection,
    assignment,
    target_stress,
):
    pieces = target_stress.reshape(6, 16, 32).transpose(1, 0, 2).reshape(16, 192)
    pieces = jnp.pad(pieces.astype(F32), ((0, 0), (0, 64))).reshape(16, 1, 256)
    vmem = pl.BlockSpec(memory_space=pltpu.VMEM)
    smem = pl.BlockSpec(memory_space=pltpu.SMEM)
    pressure, stress, grads = pl.pallas_call(
        kernel,
        out_shape=[
            jax.ShapeDtypeStruct((32, 32, 128), F32),
            jax.ShapeDtypeStruct((8, 512), F32),
            jax.ShapeDtypeStruct((RANKS, PIECE, 128), BF16),
        ],
        in_specs=[smem, smem] + [vmem] * 6,
        out_specs=[vmem] * 3,
        scratch_shapes=[pltpu.VMEM(shape, kind) for shape, kind in SCRATCH.values()]
        + [pltpu.SemaphoreType.DMA((SEMAPHORES,))] * 2,
        compiler_params=pltpu.CompilerParams(
            collective_id=0, has_side_effects=True, vmem_limit_bytes=56 << 20
        ),
    )(
        selection,
        assignment.reshape(-1),
        velocity,
        first_kernel,
        norm_gain.reshape(1, 64),
        second_kernel,
        head_weight,
        pieces,
    )
    predicted = stress[:6].astype(BF16).reshape(1, 1, 3072)
    second = grads[:, :BIG].reshape(RANKS * BIG, 128)[:1728].astype(F32)
    rest = grads[:, BIG : BIG + SMALL].reshape(RANKS * SMALL, 128).astype(F32)
    return (
        pressure[None],
        predicted,
        rest[:81, :64].reshape(3, 3, 3, 3, 64),
        rest[81, :64],
        second.reshape(3, 3, 3, 64, 128),
        rest[82:88].T,
    )


def solution(mesh):
    placed = (
        P(("sec", "dom"), None, None, None, None),
        P(),
        P(),
        P(),
        P(),
        P(("sec", "dom"), None),
        P(),
        P(("sec", "dom"), None, None),
    )
    return jax.shard_map(
        shards,
        mesh=mesh,
        in_specs=placed,
        out_specs=(
            P(("sec", "dom"), None, None, None),
            P(("sec", "dom"), None, None),
            P(),
            P(),
            P(),
            P(),
        ),
        check_vma=False,
    )
```

time: 707 us -> 95.4 us (0.13); the launches traced: 696 us -> 95 us
  waiting for transfers between devices: 289 us -> 0 us
  local copies, waits for them, and re-layouts: 95.1 us -> 7.25 us
  starting transfers between devices: 86.8 us -> 0 us
  matrix products: 86.2 us -> 0 us
  Pallas kernels: 0 us -> 83.9 us
  blocking collectives: 76.9 us -> 0 us
  other arithmetic: 43.7 us -> 2.53 us
  between operations: 18 us -> 1.31 us
    all_gather x1 -> x0, waiting for transfers between devices: 133 us -> none  [shards(): every_target = lax.all_gather(target_stress[0, 0], ('sec', 'dom'))]
    psum x1 -> x0, waiting for transfers between devices: 105 us -> none  [shards(): lax.psum((gradients[0].astype(jnp.float32), gradients[1].astype(jnp.float...]
    ppermute x21 -> x0, starting transfers between devices: 86.8 us -> none  [shifted_2(): return lax.ppermute(x, axis, pairs)]
    conv_general_dilated x5 -> x0, matrix products: 85.6 us -> none  [conv_layer(): lax.conv_general_dilated(inputs, kernel, (stride, stride, stride), ((1, 1...]
    pallas_call x0 -> x1, Pallas kernels: none -> 83.9 us  [shards(): pl.pallas_call(kernel, out_shape=[jax.ShapeDtypeStruct((32, 32, 128), F32...]
    psum x1 -> x0, blocking collectives: 76.9 us -> none  [shards(): lax.psum((gradients[0].astype(jnp.float32), gradients[1].astype(jnp.float...]
    ppermute x21 -> x0, waiting for transfers between devices: 50.4 us -> none  [shifted_2(): return lax.ppermute(x, axis, pairs)]
    convert_element_type x13 -> x3, local copies, waits for them, and re-layouts: 45.7 us -> 0.19 us  [shards(): pieces = jnp.pad(pieces.astype(F32), ((0, 0), (0, 64))).reshape(16, 1, 256)]
  transfers between devices with their start and end apart: 23 -> 0, of which waited for: 12 -> 0; matrix products, arithmetic and copies ran while one was open for 31% -> 0% of each run, Pallas kernels for 0% -> 0%
where the time goes in v2:
time: 95.4 us; the launch traced here: 95 us
  Pallas kernels  83.9 us (88%)
  local copies, waits for them, and re-layouts  7.25 us (8%)
  other arithmetic  2.53 us (3%)
  between operations  1.31 us (1%)
    pallas_call x1, Pallas kernels, shards(): pl.pallas_call(kernel, out_shape=[jax.ShapeDtypeStruct((32, 32, 128), F32...  83.9 us
    unnamed x4, local copies, waits for them, and re-layouts  2.21 us

profile of v2, /device:TPU:1, one launch (start us, length us, event | category | flops | bytes accessed | tf_op | source)
XLA Modules:
  0.0 95.0 jit_solution(6847212837112847886)
XLA Ops:
  1.3 0.7 reduce
  2.0 0.1 convert_element_type.20
  2.1 0.1 convert_element_type.22
  2.2 0.6 reshape.57.refs_7_
  2.9 1.4 %copy.17.refs_6_ = bf16[128,6]{1,0:T(8,128)(2,1)} copy(bf16[128,6]{0,1:T(8,128)(2,1)} %param.12) | data formatting | bytes 3072 | tf_op args[4]
  4.3 83.9 %shard_map.127 = (f32[32,32,128]{2,1,0:T(8,128)}, f32[8,512]{1,0:T(8,128)}, bf16[16,128,128]{2,1,0:T(8,128)(2,1)}) custom-call(s32[1,1]{1,0:T(1,128)S(6)} %copy.21.refs_0_, s32[256]{0:T(256)} %bitcast.20, f32[1,3,32,32,128]{4,3,2,1,0:T(8,128)} %refs_2_.1, bf16[3,3,3,3,64]{4,3,2,1,0:T(4,128)(2,1)} %refs_3_.1, f32[1,64]{1,0:T(1,128)} %bitcast.21, ...), custom_call_target="tpu_custom_call" | custom-call | tf_op jit(solution)/shard_map/pallas_call | solution.py:674
  88.2 0.7 slice.38
  88.9 0.6 reshape.51
  89.6 0.8 bitcast_convert_fusion
  90.3 0.0 copy-start
  90.3 1.1 %slice.26 = bf16[16,112,128]{2,1,0:T(8,128)(2,1)S(1)} slice(bf16[16,128,128]{2,1,0:T(8,128)(2,1)} %get-tuple-element.11), slice={[0:16], [0:112], [0:128]} | slice | bytes 917504 | tf_op jit(solution)/shard_map/slice | solution.py:699
  91.5 0.5 slice_bitcast_fusion.1
  92.0 0.6 slice_bitcast_fusion
  92.6 0.6 reshape.52
  93.2 1.0 %convert.13 = f32[3,3,3,64,128]{4,3,2,1,0:T(8,128)} convert(bf16[3,3,3,64,128]{4,3,2,1,0:T(8,128)(2,1)S(1)} %bitcast.17) | non-fusion elementwise | flops 221184 | bytes 1327104 | tf_op jit(solution)/shard_map/reshape | solution.py:706
  94.2 0.0 copy-done
  94.2 0.8 copy.22
  (4 shorter events, 0.1 us)
Async XLA Ops:
  90.3 3.9 %copy-start = (f32[32,32,128]{2,1,0:T(8,128)S(1)}, f32[32,32,128]{2,1,0:T(8,128)}, u32[]{:S(2)}) copy-start(f32[32,32,128]{2,1,0:T(8,128)} %get-tuple-element.9) | copy-start | bytes 1572868

commit v3 on v2

--- a/solution.py
+++ b/solution.py
@@ -1,5 +1,3 @@
-import functools
-
 import jax
 import jax.numpy as jnp
 from jax import lax
@@ -14,7 +12,6 @@
 RANKS = 16
 BIG = 112
 SMALL = 8
-PIECE = 128
 
 
 def iota(shape, dim):
@@ -50,13 +47,10 @@
         tap = row - 2 * (2 * t + upper) + 1
         masks = [(tap == k).astype(F32) for k in range(3)]
 
-        def fill(c, carry):
-            w = wg[c]
-            block = masks[0] * w[0:1] + masks[1] * w[1:2] + masks[2] * w[2:3]
-            table[pl.ds(pl.multiple_of(c * 32, 32), 32), lanes(t)] = block.astype(BF16)
-            return carry
-
-        lax.fori_loop(0, 36, fill, 0)
+        for c in range(0, 36, 12):
+            w = wg[c : c + 12]
+            block = sum(masks[k][None] * w[:, k : k + 1, :] for k in range(3))
+            table[c : c + 12, :, lanes(t)] = block.astype(BF16)
 
 
 def build_second_weights(w2_ref, wp):
@@ -69,27 +63,22 @@
 
 
 def build_rows(sel, vel_ref, mx):
-    keep = lax.shift_right_logical(iota((8, 128), 1), 5) == sel
-    top = iota((8, 128), 0) == 0
+    keep = lax.shift_right_logical(iota((8, 8, 128), 2), 5) == sel
+    top = iota((8, 8, 128), 1) == 0
     for i in range(3):
         mx[i, 0, 0] = jnp.zeros((16, 128), BF16)
-
-        def one(x):
-            d = [
-                jnp.where(keep, vel_ref[0, i, x, pl.ds(o, 8, stride=4), :], 0.0)
-                for o in range(4)
-            ]
-            before = jnp.where(top, 0.0, pltpu.roll(d[3], 1, 0))
-            even = before + pltpu.roll(d[0], 32, 1) + pltpu.roll(d[1], 64, 1)
-            odd = d[1] + pltpu.roll(d[2], 32, 1) + pltpu.roll(d[3], 64, 1)
-            return jnp.concatenate([even, odd], axis=0).astype(BF16)
-
-        def pair(m, carry):
-            mx[i, m, 1] = one(2 * m)
-            mx[i, m + 1, 0] = one(2 * m + 1)
-            return carry
-
-        lax.fori_loop(0, 16, pair, 0)
+        for m in range(0, 16, 4):
+            d = []
+            for o in range(4):
+                rows = vel_ref[0, i, 2 * m : 2 * m + 8, pl.ds(o, 8, stride=4), :]
+                d.append(jnp.where(keep, rows, 0.0))
+            before = jnp.where(top, 0.0, pltpu.roll(d[3], 1, 1))
+            even = before + pltpu.roll(d[0], 32, 2) + pltpu.roll(d[1], 64, 2)
+            odd = d[1] + pltpu.roll(d[2], 32, 2) + pltpu.roll(d[3], 64, 2)
+            both = jnp.concatenate([even, odd], axis=1).astype(BF16)
+            both = both.reshape(4, 2, 16, 128)
+            mx[i, m : m + 4, 1] = both[:, 0]
+            mx[i, m + 1 : m + 5, 0] = both[:, 1]
 
 
 def first_rows(mx, kx, i):
@@ -114,7 +103,8 @@
         [first_rows(mx, kx, i) for kx in range(3) for i in range(3)], axis=1
     )
     for t in range(4):
-        cen[:, lanes(t, 256)] = dot(left, table[:, lanes(t, 256)], 1, 0)
+        right = table[:, :, lanes(t, 256)].reshape(1152, 256)
+        cen[:, lanes(t, 256)] = dot(left, right, 1, 0)
 
 
 def normalise(cen, gain_ref):
@@ -169,16 +159,23 @@
     return same.astype(F32).astype(BF16)
 
 
-def target_rows(pieces):
-    row = iota((512, 16), 0)
-    which = lax.shift_right_logical(lax.bitwise_and(row, 63), 2)
-    pick = (which == iota((512, 16), 1)).astype(F32).astype(BF16)
-    spread = dot(pick, pieces.astype(BF16), 1, 0)
-    row, lane = iota((512, 256), 0), iota((512, 256), 1)
-    cell = lax.bitwise_and(row, 3) * 8 + lax.shift_right_logical(row, 6)
-    kept = jnp.where(lax.bitwise_and(lane, 31) == cell, spread, 0.0).astype(BF16)
-    r, c = iota((256, 128), 0), iota((256, 128), 1)
-    collect = (lax.shift_right_logical(r, 5) == c).astype(F32).astype(BF16)
+def target_rows(flat, wide):
+    wide[...] = jnp.zeros((8, 768), F32)
+    for k in range(6):
+        wide[0:4, lanes(k)] = flat[4 * k : 4 * k + 4]
+    row = iota((512, 8), 0)
+    which = lax.bitwise_and(lax.shift_right_logical(row, 4), 3)
+    pick = (which == iota((512, 8), 1)).astype(F32).astype(BF16)
+    spread = dot(pick, wide[...].astype(BF16), 1, 0)
+    row, lane = iota((512, 768), 0), iota((512, 768), 1)
+    cell = (
+        lax.bitwise_and(lax.shift_right_logical(row, 3), 1) * 64
+        + lax.bitwise_and(row, 7) * 8
+        + lax.shift_right_logical(row, 6)
+    )
+    kept = jnp.where(lax.bitwise_and(lane, 127) == cell, spread, 0.0).astype(BF16)
+    r, c = iota((768, 128), 0), iota((768, 128), 1)
+    collect = (lax.shift_right_logical(r, 7) == c).astype(F32).astype(BF16)
     return dot(kept, collect, 1, 0)
 
 
@@ -278,20 +275,17 @@
 
     def layer(x, before):
         ux, uy, uz = vel_ref[0, 0, x], vel_ref[0, 1, x], vel_ref[0, 2, x]
-        y_rim = rim_y[pl.ds(x, 1), :] * flags[2]
+        y_rim = rim_y[x : x + 1, :] * flags[2]
         y_before = jnp.where(first_row, y_rim, pltpu.roll(uy, 1, 0))
-        z_rim = pltpu.roll(rim_z[...], 128 - x if not isinstance(x, int) else 0, 1) * flags[4]
+        z_rim = pltpu.roll(rim_z[...], (128 - x) % 128, 1) * flags[4]
         z_before = jnp.where(first_lane, z_rim, pltpu.roll(uz, 1, 1))
         total = (ux - before) + (uy - y_before) + (uz - z_before)
         window[x + 2, 0:32, 0:128] = -total
 
     layer(0, rim_x[...] * flags[0])
 
-    def step(x, carry):
+    for x in range(1, 32):
         layer(x, vel_ref[0, 0, x - 1])
-        return carry
-
-    lax.fori_loop(1, 32, step, 0)
 
 
 def pack_rim_z(vel_ref, send):
@@ -303,36 +297,27 @@
     send[...] = packed
 
 
-def pack_y(field, count, h, w, send):
-    sub = iota((8, 128), 0)
-    per = 8 // w
-    for m in range(count // per):
-        high = jnp.zeros((8, 128), F32)
-        low = jnp.zeros((8, 128), F32)
-        for j in range(per):
-            x = m * per + j
-            here = (sub >= j * w) & (sub < j * w + w)
-            top = pltpu.roll(field[x, 24:32, 0:128], (j * w - (8 - h)) % 8, 0)
-            bottom = field[x, 0:8, 0:128]
-            if j:
-                bottom = pltpu.roll(bottom, j * w, 0)
-            high = jnp.where(here, top, high)
-            low = jnp.where(here, bottom, low)
-        send[0, m] = high
-        send[1, m] = low
-
-
-def unpack_y(field, count, h, w, got, flags):
-    sub = iota((8, 128), 0)
-    per = 8 // w
-    for m in range(count // per):
-        below, above = got[0, m] * flags[2], got[1, m] * flags[3]
-        for j in range(per):
-            lower = pltpu.roll(below, (8 - h - j * w) % 8, 0)
-            upper = pltpu.roll(above, (-j * w) % 8, 0) if j else above
-            field[m * per + j, 32:40, 0:128] = jnp.where(
-                sub < h, upper, jnp.where(sub >= 8 - h, lower, 0.0)
-            )
+def pack_y(field, h, send):
+    for r in range(h):
+        send[0, r] = field[h : h + 32, 32 - h + r, 0:128]
+        send[1, r] = field[h : h + 32, r, 0:128]
+
+
+def unpack_xy(field, h, got, edges, flags):
+    if flags is not None:
+        field[0:h, 0:32, 0:128] = field[0:h, 0:32, 0:128] * flags[0]
+        field[h + 32 :, 0:32, 0:128] = field[h + 32 :, 0:32, 0:128] * flags[1]
+    else:
+        flags = [1.0] * 6
+    for side, at in ((0, 40 - h), (1, 32)):
+        for r in range(h):
+            row = at + r
+            field[h : h + 32, row, 0:128] = got[side, r] * flags[2 + side]
+            for end, low, take in ((0, 0, 8 - h), (1, h + 32, 0)):
+                both = flags[2 + side] * flags[end]
+                strip = edges[end * 2 + side, r] * both
+                for k in range(h):
+                    field[low + k, row : row + 1, 0:128] = strip[take + k : take + k + 1]
 
 
 def pack_z(field, count, h, send):
@@ -368,44 +353,53 @@
 
 def local_solve(window, mask, za, zb, flags, pressure, emit):
     def inside(xi):
+        if isinstance(xi, int):
+            return flags[0] if xi < 2 else flags[1] if xi > 33 else 1.0
         return jnp.where(xi < 2, flags[0], jnp.where(xi > 33, flags[1], 1.0))
 
     for z in (za, zb):
         z[0] = jnp.zeros((40, 256), F32)
         z[37] = jnp.zeros((40, 256), F32)
 
-    def first(xi, carry):
+    def first(xi):
         w = window[xi]
         if pressure is not None:
             own, around = neighbours(pressure, xi + 1)
             w = w - (6.0 * own - around)
             window[xi] = w
         za[xi + 1] = w * (mask[...] * inside(xi))
-        return carry
 
     def sweep(source, target):
-        def step(xi, carry):
+        def step(xi):
             _, around = neighbours(source, xi + 1)
             target[xi + 1] = (window[xi] + around) * (mask[...] * inside(xi))
-            return carry
 
         return step
 
-    def last(xi, carry):
+    def last(xi):
         _, around = neighbours(za, xi + 1)
         z = (window[xi] + around) * mask[...]
         emit(xi, z[0:32, 0:128])
-        return carry
-
-    lax.fori_loop(0, 36, first, 0)
-    lax.fori_loop(0, 36, sweep(za, zb), 0)
-    lax.fori_loop(1, 35, sweep(zb, za), 0)
-    lax.fori_loop(2, 34, last, 0)
+
+    def over(low, high, body):
+        half = (high - low) // 2
+
+        def both(m, carry):
+            for k in range(half):
+                body(low + m * half + k)
+            return carry
+
+        lax.fori_loop(0, 2, both, 0)
+
+    over(0, 36, first)
+    over(0, 36, sweep(za, zb))
+    over(1, 35, sweep(zb, za))
+    over(2, 34, last)
 
 
 SCRATCH = dict(
     wg=((36, 8, 128), F32),
-    table=((1152, 1024), BF16),
+    table=((36, 32, 1024), BF16),
     mx=((3, 17, 2, 16, 128), BF16),
     cen=((256, 1024), F32),
     lhs=((9, 64, 1152), BF16),
@@ -413,20 +407,22 @@
     hp=((128, 128), BF16),
     back=((9, 512, 256), F32),
     dn=((256, 1024), F32),
-    order=((512, 512), BF16),
-    t1=((RANKS, 1, 256), F32),
-    t2=((RANKS, RANKS, 1, 256), F32),
-    stage=((RANKS, 1, 256), F32),
-    t3=((RANKS, 1, 256), F32),
-    pieces=((RANKS, 256), F32),
+    wide=((8, 768), F32),
+    rows=((32, 128), F32),
+    t0=((32, 128), BF16),
+    t1=((RANKS, 32, 128), BF16),
+    stage=((RANKS, 32, 128), BF16),
+    t2=((RANKS, 32, 128), BF16),
     gb=((RANKS * BIG, 128), BF16),
-    gs=((RANKS * SMALL, 128), F32),
     r1=((RANKS, BIG, 128), BF16),
-    r1s=((RANKS, SMALL, 128), F32),
     part=((RANKS, 8, 128), F32),
     r2=((RANKS, 8, 128), F32),
     whole=((RANKS, 8, 128), F32),
-    gathered=((RANKS, PIECE, 128), BF16),
+    gathered=((RANKS, BIG, 128), BF16),
+    gs=((RANKS * SMALL, 128), F32),
+    r1s=((RANKS, SMALL, 128), F32),
+    r2s=((RANKS, SMALL, 128), F32),
+    gathered_s=((RANKS, SMALL, 128), F32),
     rim_x=((32, 128), F32),
     rim_y=((32, 128), F32),
     rim_z=((32, 128), F32),
@@ -437,25 +433,25 @@
     za=((38, 40, 256), F32),
     zb=((38, 40, 256), F32),
     mask=((40, 256), F32),
-    wys=((2, 9, 8, 128), F32),
-    wyr=((2, 9, 8, 128), F32),
+    wys=((2, 2, 32, 128), F32),
+    wyr=((2, 2, 32, 128), F32),
+    wer=((4, 2, 8, 128), F32),
     wzs=((2, 40, 128), F32),
     wzr=((2, 40, 128), F32),
-    pys=((2, 19, 8, 128), F32),
-    pyr=((2, 19, 8, 128), F32),
+    pys=((2, 3, 32, 128), F32),
+    pyr=((2, 3, 32, 128), F32),
+    per=((4, 3, 8, 128), F32),
     pzs=((2, 40, 128), F32),
     pzr=((2, 40, 128), F32),
 )
-GROUP_STEPS = ("t1", "t2", "t3", "g1", "g1s", "g2", "g3", "g4")
-HALO_STEPS = ("rim", "wx", "wy", "wz", "px", "py", "pz")
-SEMAPHORES = 16 * len(GROUP_STEPS) + 3 * len(HALO_STEPS)
+STEPS = ("t1", "t2", "g1", "g2", "g3", "g4", "s1", "s2", "s3", "rim", "wxy", "wz", "pxy", "pz")
 
 
 def kernel(*refs):
     (sel_ref, asg_ref, vel_ref, w1_ref, gain_ref, w2_ref, head_ref, target_ref) = refs[:8]
-    pressure_ref, pred_ref, grad_ref = refs[8:11]
-    s = dict(zip(SCRATCH, refs[11 : 11 + len(SCRATCH)]))
-    send_sem, recv_sem = refs[11 + len(SCRATCH) :]
+    pressure_ref, pred_ref, grad_ref, small_ref = refs[8:12]
+    s = dict(zip(SCRATCH, refs[12 : 12 + len(SCRATCH)]))
+    send_sem, recv_sem = refs[12 + len(SCRATCH) :]
 
     me = lax.axis_index("sec") * 128 + lax.axis_index("dom")
     a, b = lax.div(me, 16), lax.rem(me, 16)
@@ -470,17 +466,20 @@
         return (lax.div(f, 128), lax.rem(f, 128))
 
     def box(x, y, z):
-        return device(lax.rem(x + 8, 8) * 32 + lax.rem(y + 4, 4) * 8 + lax.rem(z + 8, 8))
-
-    above = [box(bx + 1, by, bz), box(bx, by + 1, bz), box(bx, by, bz + 1)]
-    below = [box(bx - 1, by, bz), box(bx, by - 1, bz), box(bx, by, bz - 1)]
+        return device(
+            lax.rem(bx + x + 8, 8) * 32 + lax.rem(by + y + 4, 4) * 8 + lax.rem(bz + z + 8, 8)
+        )
+
+    above = [box(1, 0, 0), box(0, 1, 0), box(0, 0, 1)]
+    below = [box(-1, 0, 0), box(0, -1, 0), box(0, 0, -1)]
+    corners = [box(1, 1, 0), box(1, -1, 0), box(-1, 1, 0), box(-1, -1, 0)]
     a_ranks = [None] + [lax.rem(a + j, RANKS) for j in range(1, RANKS)]
     b_ranks = [None] + [lax.rem(b + j, RANKS) for j in range(1, RANKS)]
     a_peers = [None] + [device(a_ranks[j] * 16 + b) for j in range(1, RANKS)]
     b_peers = [None] + [device(a * 16 + b_ranks[j]) for j in range(1, RANKS)]
 
     barrier = pltpu.get_barrier_semaphore()
-    everyone = a_peers[1:] + b_peers[1:] + above + below
+    everyone = a_peers[1:] + b_peers[1:] + above + below + corners
     for other in everyone:
         pl.semaphore_signal(barrier, inc=1, device_id=other, device_id_type=MESH)
 
@@ -488,16 +487,12 @@
     flights = {}
 
     def start(step, at, source, target, other):
-        base = (
-            GROUP_STEPS.index(step) * 16
-            if step in GROUP_STEPS
-            else 16 * len(GROUP_STEPS) + 3 * HALO_STEPS.index(step)
-        )
+        index = STEPS.index(step) * 16 + at
         copy = pltpu.make_async_remote_copy(
             src_ref=source,
             dst_ref=target,
-            send_sem=send_sem.at[base + at],
-            recv_sem=recv_sem.at[base + at],
+            send_sem=send_sem.at[index],
+            recv_sem=recv_sem.at[index],
             device_id=other,
             device_id_type=MESH,
         )
@@ -512,73 +507,94 @@
                 copy.wait_send()
                 started[:] = [other for other in started if other is not copy]
 
+    def start_xy(step, field, h, send, got, edges):
+        low, high = slice(0, 32), slice(0, 128)
+        start(step, 0, field.at[32 : 32 + h, low, high], field.at[0:h, low, high], above[0])
+        start(
+            step, 1, field.at[h : 2 * h, low, high], field.at[32 + h : 32 + 2 * h, low, high], below[0]
+        )
+        pack_y(field, h, send)
+        start(step, 2, send.at[0], got.at[0], above[1])
+        start(step, 3, send.at[1], got.at[1], below[1])
+        for k, (side, at) in enumerate(((0, 24), (1, 24), (0, 0), (1, 0))):
+            start(step, 4 + k, send.at[side, :, at : at + 8, :], edges.at[k], corners[k])
+
+    def start_z(step, send, got):
+        start(step, 0, send.at[0], got.at[0], above[2])
+        start(step, 1, send.at[1], got.at[1], below[2])
+
     sel = sel_ref[0, 0]
-    build_first_weights(sel, w1_ref, s["wg"], s["table"])
-    build_second_weights(w2_ref, s["wp"])
-    s["hp"][...] = jnp.zeros((128, 128), BF16)
-    s["hp"][:, 0:6] = head_ref[...]
-    s["mask"][...] = cell_masks(coords)
+    window, press = s["window"], s["press"]
+    flat = target_ref[0].astype(F32)
+    s["rows"][...] = jnp.zeros((32, 128), F32)
+    for r in range(24):
+        s["rows"][r : r + 1, :] = flat[:, lanes(r)]
+    s["t0"][...] = s["rows"][...].astype(BF16)
+    s["t1"][a] = s["t0"][...]
     pack_rim_z(vel_ref, s["rim_zs"])
     s["rim_ys"][...] = vel_ref[0, 1, :, 31, :]
+    build_first_weights(sel, w1_ref, s["wg"], s["table"])
 
     pl.semaphore_wait(barrier, len(everyone))
 
     for j in range(1, RANKS):
-        start("t1", j, target_ref.at[a_ranks[j]], s["t1"].at[a], a_peers[j])
+        start("t1", j, s["t0"], s["t1"].at[a], a_peers[j])
     start("rim", 0, vel_ref.at[0, 0, 31], s["rim_x"], above[0])
     start("rim", 1, s["rim_ys"], s["rim_y"], above[1])
     start("rim", 2, s["rim_zs"], s["rim_z"], above[2])
-    s["t1"][a] = target_ref[a]
 
     build_rows(sel, vel_ref, s["mx"])
+    first_layer(s["mx"], s["table"], s["cen"])
+    s["mask"][...] = cell_masks(coords)
+    window[:, 32:40, 0:128] = jnp.zeros((36, 8, 128), F32)
+    press[:, 32:40, 0:128] = jnp.zeros((38, 8, 128), F32)
+    s["hp"][...] = jnp.zeros((128, 128), BF16)
+    s["hp"][0:6, :] = head_ref[...]
+    build_second_weights(w2_ref, s["wp"])
+
     arrive("t1")
-    for j in range(1, RANKS):
-        start("t2", j, s["t1"], s["t2"].at[b], b_peers[j])
-    s["t2"][b] = s["t1"][...]
-    first_layer(s["mx"], s["table"], s["cen"])
+    for q in range(RANKS):
+        s["stage"][q] = s["t1"][lax.div(asg_ref[a * 16 + q], 16)]
+    for j in range(1, RANKS):
+        start("t2", j, s["stage"].at[b_ranks[j]], s["t2"].at[b], b_peers[j])
+    s["t2"][b] = s["stage"][b]
     arrive("rim")
-    window = s["window"]
     divergence(vel_ref, s["rim_x"], s["rim_y"], s["rim_z"], flags, window)
-    own = (slice(0, 32), slice(0, 128))
-    start("wx", 0, window.at[32:34, 0:32, 0:128], window.at[0:2, 0:32, 0:128], above[0])
-    start("wx", 1, window.at[2:4, 0:32, 0:128], window.at[34:36, 0:32, 0:128], below[0])
+    start_xy("wxy", window, 2, s["wys"], s["wyr"], s["wer"])
+
     gain, rstd = normalise(s["cen"], gain_ref)
-    arrive("t2")
-    for q in range(RANKS):
-        wanted = asg_ref[q * 16 + b]
-        s["stage"][q] = s["t2"][lax.rem(wanted, 16), lax.div(wanted, 16)]
-    for j in range(1, RANKS):
-        start("t3", j, s["stage"].at[a_ranks[j]], s["t3"].at[a], a_peers[j])
-    s["t3"][a] = s["stage"][a]
     hidden_rows(s["cen"], gain * rstd, s["lhs"])
-    arrive("wx", True)
-    pack_y(window, 36, 2, 2, s["wys"])
-    start("wy", 0, s["wys"].at[0], s["wyr"].at[0], above[1])
-    start("wy", 1, s["wys"].at[1], s["wyr"].at[1], below[1])
-
     out = second_layer(s["lhs"], s["wp"])
     sig = jax.nn.sigmoid(out)
     deep = (out * sig).astype(BF16)
     slope = sig * (1.0 + out * (1.0 - sig))
-    stress = dot(deep, s["hp"][...], 1, 0)
-    arrive("t3")
-    for q in range(RANKS):
-        s["pieces"][q : q + 1, :] = s["t3"][q]
-    error = (stress - target_rows(s["pieces"][...])).astype(BF16)
-    dout = dot(error, s["hp"][...], 1, 1).astype(BF16).astype(F32) * slope
+    stress = dot(deep, s["hp"][...], 1, 1)
+    pred_ref[...] = dot(stress.astype(BF16), cell_order(), 0, 0)[0:8]
+
+    arrive("wxy", True)
+    unpack_xy(window, 2, s["wyr"], s["wer"], None)
+    pack_z(window, 36, 2, s["wzs"])
+    start_z("wz", s["wzs"], s["wzr"])
+
+    arrive("t2")
+    target = s["t2"][lax.rem(asg_ref[me], 16)].astype(F32)
+    error = (stress - target_rows(target, s["wide"])).astype(BF16)
+    dout = dot(error, s["hp"][...], 1, 0).astype(BF16).astype(F32) * slope
     dout = dout.astype(BF16)
-
     s["gb"][1728:1792, :] = jnp.zeros((64, 128), BF16)
     second_gradient(s["lhs"], dout, s["gb"])
     for j in range(1, RANKS):
         rows = pl.ds(pl.multiple_of(a_ranks[j] * BIG, 16), BIG)
         start("g1", j, s["gb"].at[rows], s["r1"].at[j], a_peers[j])
 
-    arrive("wy")
-    unpack_y(window, 36, 2, 2, s["wyr"], flags)
-    pack_z(window, 36, 2, s["wzs"])
-    start("wz", 0, s["wzs"].at[0], s["wzr"].at[0], above[2])
-    start("wz", 1, s["wzs"].at[1], s["wzr"].at[1], below[2])
+    arrive("wz")
+    unpack_z(window, 36, 2, s["wzr"], flags)
+
+    def keep(xi, z):
+        press[xi + 1, 0:32, 0:128] = z
+
+    local_solve(window, s["mask"], s["za"], s["zb"], flags, None, keep)
+    start_xy("pxy", press, 3, s["pys"], s["pyr"], s["per"])
 
     gs = s["gs"]
     gs[...] = jnp.zeros((128, 128), F32)
@@ -588,41 +604,30 @@
     first_gradient(sel, s["mx"], s["dn"], gs)
     for j in range(1, RANKS):
         rows = pl.ds(pl.multiple_of(a_ranks[j] * SMALL, 8), SMALL)
-        start("g1s", j, gs.at[rows], s["r1s"].at[j], a_peers[j])
-    pred_ref[...] = dot(stress.astype(BF16), cell_order(), 0, 0)[0:8]
-
-    arrive("wz")
-    unpack_z(window, 36, 2, s["wzr"], flags)
-    press = s["press"]
-
-    def keep(xi, z):
-        press[xi + 1, 0:32, 0:128] = z
-
-    local_solve(window, s["mask"], s["za"], s["zb"], flags, None, keep)
-    start("px", 0, press.at[32:35, 0:32, 0:128], press.at[0:3, 0:32, 0:128], above[0])
-    start("px", 1, press.at[3:6, 0:32, 0:128], press.at[35:38, 0:32, 0:128], below[0])
+        start("s1", j, gs.at[rows], s["r1s"].at[j], a_peers[j])
 
     arrive("g1")
-    arrive("g1s")
-    rows = pl.ds(pl.multiple_of(a * BIG, 16), BIG)
-    big = s["gb"][rows, :].astype(F32)
-    small = gs[pl.ds(pl.multiple_of(a * SMALL, 8), SMALL), :]
+    big = s["gb"][pl.ds(pl.multiple_of(a * BIG, 16), BIG), :].astype(F32)
     for j in range(1, RANKS):
         big = big + s["r1"][j].astype(F32)
-        small = small + s["r1s"][j]
     part = s["part"]
     part[0:14] = big.reshape(14, 8, 128)
-    part[14] = small
-    part[15] = jnp.zeros((8, 128), F32)
+    part[14:16] = jnp.zeros((2, 8, 128), F32)
     for j in range(1, RANKS):
         start("g2", j, part.at[b_ranks[j]], s["r2"].at[j], b_peers[j])
 
-    arrive("px", True)
-    press[0:3, 0:32, 0:128] = press[0:3, 0:32, 0:128] * flags[0]
-    press[35:38, 0:32, 0:128] = press[35:38, 0:32, 0:128] * flags[1]
-    pack_y(press, 38, 3, 4, s["pys"])
-    start("py", 0, s["pys"].at[0], s["pyr"].at[0], above[1])
-    start("py", 1, s["pys"].at[1], s["pyr"].at[1], below[1])
+    arrive("pxy", True)
+    unpack_xy(press, 3, s["pyr"], s["per"], flags)
+    pack_z(press, 38, 3, s["pzs"])
+    start_z("pz", s["pzs"], s["pzr"])
+
+    arrive("s1")
+    small = gs[pl.ds(pl.multiple_of(a * SMALL, 8), SMALL), :]
+    for j in range(1, RANKS):
+        small = small + s["r1s"][j]
+    s["r2s"][b] = small
+    for j in range(1, RANKS):
+        start("s2", j, s["r2s"].at[b], s["r2s"].at[b], b_peers[j])
 
     arrive("g2")
     total = part[b]
@@ -632,29 +637,50 @@
     for j in range(1, RANKS):
         start("g3", j, s["whole"].at[b], s["whole"].at[b], b_peers[j])
 
-    arrive("py")
-    unpack_y(press, 38, 3, 4, s["pyr"], flags)
-    pack_z(press, 38, 3, s["pzs"])
-    start("pz", 0, s["pzs"].at[0], s["pzr"].at[0], above[2])
-    start("pz", 1, s["pzs"].at[1], s["pzr"].at[1], below[2])
+    arrive("pz")
+    unpack_z(press, 38, 3, s["pzr"], flags)
+
+    def finish(xi, z):
+        pressure_ref[xi - 2] = press[xi + 1, 0:32, 0:128] + z
+
+    local_solve(window, s["mask"], s["za"], s["zb"], flags, press, finish)
+
+    arrive("s2")
+    small = s["r2s"][0]
+    for q in range(1, RANKS):
+        small = small + s["r2s"][q]
+    s["gathered_s"][a] = small
+    for j in range(1, RANKS):
+        start("s3", j, s["gathered_s"].at[a], s["gathered_s"].at[a], a_peers[j])
 
     arrive("g3")
     gathered = s["gathered"]
-    gathered[a] = s["whole"][...].reshape(PIECE, 128).astype(BF16)
+    gathered[a] = s["whole"][0:14].reshape(BIG, 128).astype(BF16)
     for j in range(1, RANKS):
         start("g4", j, gathered.at[a], gathered.at[a], a_peers[j])
-
-    arrive("pz")
-    unpack_z(press, 38, 3, s["pzr"], flags)
-
-    def finish(xi, z):
-        pressure_ref[xi - 2] = press[xi + 1, 0:32, 0:128] + z
-
-    local_solve(window, s["mask"], s["za"], s["zb"], flags, press, finish)
+    arrive("s3")
+    small_ref[...] = s["gathered_s"][...].reshape(RANKS * SMALL, 128)
     arrive("g4")
     grad_ref[...] = gathered[...]
     for copy in started:
         copy.wait_send()
+
+
+def finish_kernel(
+    pressure_in, pred_in, grad_in, small_in, pressure_out, pred_out, first, gain, second, head
+):
+    pressure_out[0] = pressure_in[...]
+    for k in range(6):
+        pred_out[0, :, lanes(k, 512)] = pred_in[k : k + 1, :].astype(BF16)
+    flat = grad_in[...].reshape(RANKS * BIG, 128)
+    for kx in range(3):
+        for ky in range(3):
+            for kz in range(3):
+                k = (kx * 3 + ky) * 3 + kz
+                second[kx, ky, kz] = flat[k * 64 : (k + 1) * 64].astype(F32)
+                first[kx, ky, kz] = small_in[k * 3 : k * 3 + 3, 0:64]
+    gain[...] = small_in[81:82, 0:64]
+    head[...] = small_in[82:88, :]
 
 
 def shards(
@@ -667,21 +693,21 @@
     assignment,
     target_stress,
 ):
-    pieces = target_stress.reshape(6, 16, 32).transpose(1, 0, 2).reshape(16, 192)
-    pieces = jnp.pad(pieces.astype(F32), ((0, 0), (0, 64))).reshape(16, 1, 256)
     vmem = pl.BlockSpec(memory_space=pltpu.VMEM)
     smem = pl.BlockSpec(memory_space=pltpu.SMEM)
-    pressure, stress, grads = pl.pallas_call(
+    semaphores = 16 * len(STEPS)
+    pressure, stress, grads, small = pl.pallas_call(
         kernel,
         out_shape=[
             jax.ShapeDtypeStruct((32, 32, 128), F32),
             jax.ShapeDtypeStruct((8, 512), F32),
-            jax.ShapeDtypeStruct((RANKS, PIECE, 128), BF16),
+            jax.ShapeDtypeStruct((RANKS, BIG, 128), BF16),
+            jax.ShapeDtypeStruct((RANKS * SMALL, 128), F32),
         ],
         in_specs=[smem, smem] + [vmem] * 6,
-        out_specs=[vmem] * 3,
+        out_specs=[vmem] * 4,
         scratch_shapes=[pltpu.VMEM(shape, kind) for shape, kind in SCRATCH.values()]
-        + [pltpu.SemaphoreType.DMA((SEMAPHORES,))] * 2,
+        + [pltpu.SemaphoreType.DMA((semaphores,))] * 2,
         compiler_params=pltpu.CompilerParams(
             collective_id=0, has_side_effects=True, vmem_limit_bytes=56 << 20
         ),
@@ -692,20 +718,23 @@
         first_kernel,
         norm_gain.reshape(1, 64),
         second_kernel,
-        head_weight,
-        pieces,
+        head_weight.T,
+        target_stress,
     )
-    predicted = stress[:6].astype(BF16).reshape(1, 1, 3072)
-    second = grads[:, :BIG].reshape(RANKS * BIG, 128)[:1728].astype(F32)
-    rest = grads[:, BIG : BIG + SMALL].reshape(RANKS * SMALL, 128).astype(F32)
-    return (
-        pressure[None],
-        predicted,
-        rest[:81, :64].reshape(3, 3, 3, 3, 64),
-        rest[81, :64],
-        second.reshape(3, 3, 3, 64, 128),
-        rest[82:88].T,
-    )
+    pressure, predicted, first, gain, second, head = pl.pallas_call(
+        finish_kernel,
+        out_shape=[
+            jax.ShapeDtypeStruct((1, 32, 32, 128), F32),
+            jax.ShapeDtypeStruct((1, 1, 3072), BF16),
+            jax.ShapeDtypeStruct((3, 3, 3, 3, 64), F32),
+            jax.ShapeDtypeStruct((1, 64), F32),
+            jax.ShapeDtypeStruct((3, 3, 3, 64, 128), F32),
+            jax.ShapeDtypeStruct((6, 128), F32),
+        ],
+        in_specs=[vmem] * 4,
+        out_specs=[vmem] * 6,
+    )(pressure, stress, grads, small)
+    return (pressure, predicted, first, gain.reshape(64), second, head.T)
 
 
 def solution(mesh):

time: 95.4 us -> 73.8 us (0.77)
  Pallas kernels: 83.9 us -> 72.4 us
  local copies, waits for them, and re-layouts: 7.25 us -> 0 us
  other arithmetic: 2.53 us -> 0 us
    pallas_call x1, Pallas kernels: 83.9 us -> 70 us  [shards(): pl.pallas_call(kernel, out_shape=[jax.ShapeDtypeStruct((32, 32, 128), F32...]
    pallas_call x0 -> x1, Pallas kernels: none -> 2.35 us  [shards(): pl.pallas_call(finish_kernel, out_shape=[jax.ShapeDtypeStruct((1, 32, 32,...]
    unnamed x4 -> x0, local copies, waits for them, and re-layouts: 2.21 us -> none
    reshape x3 -> x0, local copies, waits for them, and re-layouts: 1.88 us -> none  [the longest x1 0.64 us: shards(): rest[:81, :64].reshape(3, 3, 3, 3, 64)]
    slice x4 -> x0, local copies, waits for them, and re-layouts: 1.86 us -> none  [the longest x2 1.14 us: shards(): second = grads[:, :BIG].reshape(RANKS * BIG, 128)[:1728].astype(F32)]
    reshape x2 -> x0, other arithmetic: 1.01 us -> none  [the longest x1 1.01 us: shards(): second.reshape(3, 3, 3, 64, 128)]
where the time goes in v3:
time: 73.8 us; the launch traced here: 73.7 us
  Pallas kernels  72.4 us (98%)
  between operations  1.29 us (2%)
    pallas_call x1, Pallas kernels, shards(): pl.pallas_call(kernel, out_shape=[jax.ShapeDtypeStruct((32, 32, 128), F32...  70 us
    pallas_call x1, Pallas kernels, shards(): pl.pallas_call(finish_kernel, out_shape=[jax.ShapeDtypeStruct((1, 32, 32,...  2.35 us

profile of v3, /device:TPU:1, one launch (start us, length us, event | category | flops | bytes accessed | tf_op | source)
XLA Modules:
  0.0 73.7 jit_solution(3270480471994303889)
XLA Ops:
  1.3 70.0 %shard_map.127 = (f32[32,32,128]{2,1,0:T(8,128)}, f32[8,512]{1,0:T(8,128)}, bf16[16,112,128]{2,1,0:T(8,128)(2,1)}, f32[128,128]{1,0:T(8,128)}) custom-call(s32[1,1]{1,0:T(1,128)S(6)} %copy.14.refs_0_, s32[256]{0:T(256)} %bitcast.6, f32[1,3,32,32,128]{4,3,2,1,0:T(8,128)} %refs_2_.1, bf16[3,3,3,3,64]{4,3,2,1,0:T(4,128)(2,1)} %refs_3_.1, f32[1,64]{1,0:T(1,128)} %bitcast.7, ...), custom_call_target="tpu_custom_call" | custom-call | tf_op jit(solution)/shard_map/pallas_call | solution.py:699
  71.3 2.4 %shard_map.128 = (f32[1,32,32,128]{3,2,1,0:T(8,128)}, bf16[1,1,3072]{2,1,0:T(2,128)(2,1)}, f32[3,3,3,3,64]{4,3,2,1,0:T(4,128)}, f32[1,64]{1,0:T(1,128)}, f32[3,3...) custom-call(f32[32,32,128]{2,1,0:T(8,128)} %get-tuple-element.16.pressure_in, f32[8,512]{1,0:T(8,128)} %get-tuple-element.17.pred_in, ...), custom_call_target="tpu_custom_call" | custom-call | tf_op jit(solution)/shard_map/pallas_call | solution.py:724

commit v4 on v3

--- a/solution.py
+++ b/solution.py
@@ -10,7 +10,9 @@
 NORM_EPS = 1e-05
 MESH = pl.DeviceIdType.MESH
 RANKS = 16
-BIG = 112
+OWNERS = 32
+TAPS = 27
+BIG = 64
 SMALL = 8
 
 
@@ -53,15 +55,6 @@
             table[c : c + 12, :, lanes(t)] = block.astype(BF16)
 
 
-def build_second_weights(w2_ref, wp):
-    for kx in range(3):
-        for ky in range(3):
-            k = kx * 3 + ky
-            wp[k, 0:64, :] = jnp.zeros((64, 128), BF16)
-            for kz in range(3):
-                wp[k, 64 + kz * 64 : 128 + kz * 64, :] = w2_ref[kx, ky, kz]
-
-
 def build_rows(sel, vel_ref, mx):
     keep = lax.shift_right_logical(iota((8, 8, 128), 2), 5) == sel
     top = iota((8, 8, 128), 1) == 0
@@ -70,7 +63,7 @@
         for m in range(0, 16, 4):
             d = []
             for o in range(4):
-                rows = vel_ref[0, i, 2 * m : 2 * m + 8, pl.ds(o, 8, stride=4), :]
+                rows = vel_ref[i, 2 * m : 2 * m + 8, pl.ds(o, 8, stride=4), :]
                 d.append(jnp.where(keep, rows, 0.0))
             before = jnp.where(top, 0.0, pltpu.roll(d[3], 1, 1))
             even = before + pltpu.roll(d[0], 32, 2) + pltpu.roll(d[1], 64, 2)
@@ -147,7 +140,7 @@
 def second_layer(lhs, wp):
     out = jnp.zeros((512, 128), F32)
     for k in range(9):
-        out = out + dot(second_rows(lhs, k), wp[k], 1, 0)
+        out = out + dot(second_rows(lhs, k), wp[k // 3, k % 3].reshape(256, 128), 1, 0)
     return out
 
 
@@ -187,7 +180,7 @@
 
 def hidden_gradient(dout, wp, back):
     for k in range(9):
-        back[k] = dot(dout, wp[k], 1, 1).astype(F32)
+        back[k] = dot(dout, wp[k // 3, k % 3].reshape(256, 128), 1, 1)
 
 
 def norm_backward(back, cen, gain, rstd, dn):
@@ -274,7 +267,7 @@
     first_lane = iota((32, 128), 1) == 0
 
     def layer(x, before):
-        ux, uy, uz = vel_ref[0, 0, x], vel_ref[0, 1, x], vel_ref[0, 2, x]
+        ux, uy, uz = vel_ref[0, x], vel_ref[1, x], vel_ref[2, x]
         y_rim = rim_y[x : x + 1, :] * flags[2]
         y_before = jnp.where(first_row, y_rim, pltpu.roll(uy, 1, 0))
         z_rim = pltpu.roll(rim_z[...], (128 - x) % 128, 1) * flags[4]
@@ -285,14 +278,14 @@
     layer(0, rim_x[...] * flags[0])
 
     for x in range(1, 32):
-        layer(x, vel_ref[0, 0, x - 1])
+        layer(x, vel_ref[0, x - 1])
 
 
 def pack_rim_z(vel_ref, send):
     lane = iota((32, 128), 1)
     packed = jnp.zeros((32, 128), F32)
     for x in range(32):
-        moved = pltpu.roll(vel_ref[0, 2, x], (x + 1) % 128, 1)
+        moved = pltpu.roll(vel_ref[2, x], (x + 1) % 128, 1)
         packed = jnp.where(lane == x, moved, packed)
     send[...] = packed
 
@@ -403,7 +396,9 @@
     mx=((3, 17, 2, 16, 128), BF16),
     cen=((256, 1024), F32),
     lhs=((9, 64, 1152), BF16),
-    wp=((9, 256, 128), BF16),
+    wp=((3, 3, 4, 64, 128), BF16),
+    vel=((3, 32, 32, 128), F32),
+    done=((32, 32, 128), F32),
     hp=((128, 128), BF16),
     back=((9, 512, 256), F32),
     dn=((256, 1024), F32),
@@ -413,12 +408,10 @@
     t1=((RANKS, 32, 128), BF16),
     stage=((RANKS, 32, 128), BF16),
     t2=((RANKS, 32, 128), BF16),
-    gb=((RANKS * BIG, 128), BF16),
-    r1=((RANKS, BIG, 128), BF16),
-    part=((RANKS, 8, 128), F32),
-    r2=((RANKS, 8, 128), F32),
-    whole=((RANKS, 8, 128), F32),
-    gathered=((RANKS, BIG, 128), BF16),
+    gb=((OWNERS * BIG, 128), BF16),
+    r1=((OWNERS, BIG, 128), BF16),
+    parts=((8, BIG, 128), BF16),
+    gathered=((OWNERS, BIG, 128), BF16),
     gs=((RANKS * SMALL, 128), F32),
     r1s=((RANKS, SMALL, 128), F32),
     r2s=((RANKS, SMALL, 128), F32),
@@ -444,17 +437,26 @@
     pzs=((2, 40, 128), F32),
     pzr=((2, 40, 128), F32),
 )
-STEPS = ("t1", "t2", "g1", "g2", "g3", "g4", "s1", "s2", "s3", "rim", "wxy", "wz", "pxy", "pz")
+GROUP_STEPS = ("t1", "t2", "g1", "g2", "g3", "s1", "s2", "s3")
+HALO_STEPS = ("rim", "wxy", "wz", "pxy", "pz")
+SEMAPHORES = len(GROUP_STEPS) + 8 * len(HALO_STEPS)
 
 
 def kernel(*refs):
-    (sel_ref, asg_ref, vel_ref, w1_ref, gain_ref, w2_ref, head_ref, target_ref) = refs[:8]
+    (sel_ref, asg_ref, vel_hbm, w1_ref, gain_ref, w2_hbm, head_ref, target_ref) = refs[:8]
     pressure_ref, pred_ref, grad_ref, small_ref = refs[8:12]
     s = dict(zip(SCRATCH, refs[12 : 12 + len(SCRATCH)]))
-    send_sem, recv_sem = refs[12 + len(SCRATCH) :]
+    send_sem, recv_sem, local_sem = refs[12 + len(SCRATCH) :]
+    vel_ref = s["vel"]
+    load_velocity = pltpu.make_async_copy(vel_hbm.at[0], vel_ref, local_sem.at[0])
+    load_velocity.start()
+    load_second = pltpu.make_async_copy(w2_hbm, s["wp"].at[:, :, 1:4], local_sem.at[1])
+    load_second.start()
 
     me = lax.axis_index("sec") * 128 + lax.axis_index("dom")
     a, b = lax.div(me, 16), lax.rem(me, 16)
+    z, core = lax.div(b, 2), lax.rem(b, 2)
+    c = a * 2 + core
     coords = (lax.div(me, 32), lax.rem(lax.div(me, 8), 4), lax.rem(me, 8))
     bx, by, bz = coords
     flags = [
@@ -478,17 +480,23 @@
     a_peers = [None] + [device(a_ranks[j] * 16 + b) for j in range(1, RANKS)]
     b_peers = [None] + [device(a * 16 + b_ranks[j]) for j in range(1, RANKS)]
 
+    c_ranks = [None] + [lax.rem(c + j, OWNERS) for j in range(1, OWNERS)]
+    c_peers = [None] + [
+        device(lax.div(r, 2) * 16 + z * 2 + lax.rem(r, 2)) for r in c_ranks[1:]
+    ]
+    z_peers = [None] + [
+        device(a * 16 + lax.rem(z + j, 8) * 2 + core) for j in range(1, 8)
+    ]
+
     barrier = pltpu.get_barrier_semaphore()
-    everyone = a_peers[1:] + b_peers[1:] + above + below + corners
+    everyone = c_peers[1:] + b_peers[1:] + above + below + corners
     for other in everyone:
         pl.semaphore_signal(barrier, inc=1, device_id=other, device_id_type=MESH)
 
-    started = []
     flights = {}
 
-    def start(step, at, source, target, other):
-        index = STEPS.index(step) * 16 + at
-        copy = pltpu.make_async_remote_copy(
+    def remote(index, source, target, other):
+        return pltpu.make_async_remote_copy(
             src_ref=source,
             dst_ref=target,
             send_sem=send_sem.at[index],
@@ -496,16 +504,29 @@
             device_id=other,
             device_id_type=MESH,
         )
+
+    def start(step, at, source, target, other):
+        index = len(GROUP_STEPS) + 8 * HALO_STEPS.index(step) + at
+        copy = remote(index, source, target, other)
         copy.start()
-        started.append(copy)
         flights.setdefault(step, []).append(copy)
+
+    def start_group(step, source, target, peers):
+        for j in range(1, len(peers)):
+            remote(GROUP_STEPS.index(step), source(j), target(j), peers[j]).start()
+
+    def arrive_group(step, slots, peers):
+        every = remote(GROUP_STEPS.index(step), slots, slots, peers[1])
+        every.wait_recv()
+        flights[step] = [every]
 
     def arrive(step, sent=False):
         for copy in flights[step]:
             copy.wait_recv()
             if sent:
                 copy.wait_send()
-                started[:] = [other for other in started if other is not copy]
+        if sent:
+            del flights[step]
 
     def start_xy(step, field, h, send, got, edges):
         low, high = slice(0, 32), slice(0, 128)
@@ -531,70 +552,67 @@
         s["rows"][r : r + 1, :] = flat[:, lanes(r)]
     s["t0"][...] = s["rows"][...].astype(BF16)
     s["t1"][a] = s["t0"][...]
+    load_velocity.wait()
     pack_rim_z(vel_ref, s["rim_zs"])
-    s["rim_ys"][...] = vel_ref[0, 1, :, 31, :]
-    build_first_weights(sel, w1_ref, s["wg"], s["table"])
+    s["rim_ys"][...] = vel_ref[1, :, 31, :]
 
     pl.semaphore_wait(barrier, len(everyone))
 
-    for j in range(1, RANKS):
-        start("t1", j, s["t0"], s["t1"].at[a], a_peers[j])
-    start("rim", 0, vel_ref.at[0, 0, 31], s["rim_x"], above[0])
+    start_group("t1", lambda j: s["t0"], lambda j: s["t1"].at[a], a_peers)
+    start("rim", 0, vel_ref.at[0, 31], s["rim_x"], above[0])
     start("rim", 1, s["rim_ys"], s["rim_y"], above[1])
     start("rim", 2, s["rim_zs"], s["rim_z"], above[2])
 
+    build_first_weights(sel, w1_ref, s["wg"], s["table"])
     build_rows(sel, vel_ref, s["mx"])
-    first_layer(s["mx"], s["table"], s["cen"])
     s["mask"][...] = cell_masks(coords)
     window[:, 32:40, 0:128] = jnp.zeros((36, 8, 128), F32)
     press[:, 32:40, 0:128] = jnp.zeros((38, 8, 128), F32)
     s["hp"][...] = jnp.zeros((128, 128), BF16)
     s["hp"][0:6, :] = head_ref[...]
-    build_second_weights(w2_ref, s["wp"])
-
-    arrive("t1")
+    s["wp"][:, :, 0] = jnp.zeros((3, 3, 64, 128), BF16)
+    s["gb"][TAPS * BIG :, :] = jnp.zeros(((OWNERS - TAPS) * BIG, 128), BF16)
+
+    arrive_group("t1", s["t1"].at[0:15], a_peers)
     for q in range(RANKS):
         s["stage"][q] = s["t1"][lax.div(asg_ref[a * 16 + q], 16)]
-    for j in range(1, RANKS):
-        start("t2", j, s["stage"].at[b_ranks[j]], s["t2"].at[b], b_peers[j])
+    start_group("t2", lambda j: s["stage"].at[b_ranks[j]], lambda j: s["t2"].at[b], b_peers)
     s["t2"][b] = s["stage"][b]
     arrive("rim")
     divergence(vel_ref, s["rim_x"], s["rim_y"], s["rim_z"], flags, window)
     start_xy("wxy", window, 2, s["wys"], s["wyr"], s["wer"])
 
+    first_layer(s["mx"], s["table"], s["cen"])
     gain, rstd = normalise(s["cen"], gain_ref)
     hidden_rows(s["cen"], gain * rstd, s["lhs"])
+    load_second.wait()
     out = second_layer(s["lhs"], s["wp"])
     sig = jax.nn.sigmoid(out)
     deep = (out * sig).astype(BF16)
     slope = sig * (1.0 + out * (1.0 - sig))
     stress = dot(deep, s["hp"][...], 1, 1)
-    pred_ref[...] = dot(stress.astype(BF16), cell_order(), 0, 0)[0:8]
+
+    arrive_group("t2", s["t2"].at[0:15], b_peers)
+    target = s["t2"][lax.rem(asg_ref[me], 16)].astype(F32)
+    error = (stress - target_rows(target, s["wide"])).astype(BF16)
+    dout = dot(error, s["hp"][...], 1, 0).astype(BF16).astype(F32) * slope
+    dout = dout.astype(BF16)
+    second_gradient(s["lhs"], dout, s["gb"])
+
+    def tap_rows(rank):
+        return pl.ds(pl.multiple_of(rank * BIG, BIG), BIG)
+
+    def small_rows(rank):
+        return pl.ds(pl.multiple_of(rank * SMALL, SMALL), SMALL)
+
+    start_group(
+        "g1", lambda j: s["gb"].at[tap_rows(c_ranks[j])], lambda j: s["r1"].at[j], c_peers
+    )
 
     arrive("wxy", True)
     unpack_xy(window, 2, s["wyr"], s["wer"], None)
     pack_z(window, 36, 2, s["wzs"])
     start_z("wz", s["wzs"], s["wzr"])
-
-    arrive("t2")
-    target = s["t2"][lax.rem(asg_ref[me], 16)].astype(F32)
-    error = (stress - target_rows(target, s["wide"])).astype(BF16)
-    dout = dot(error, s["hp"][...], 1, 0).astype(BF16).astype(F32) * slope
-    dout = dout.astype(BF16)
-    s["gb"][1728:1792, :] = jnp.zeros((64, 128), BF16)
-    second_gradient(s["lhs"], dout, s["gb"])
-    for j in range(1, RANKS):
-        rows = pl.ds(pl.multiple_of(a_ranks[j] * BIG, 16), BIG)
-        start("g1", j, s["gb"].at[rows], s["r1"].at[j], a_peers[j])
-
-    arrive("wz")
-    unpack_z(window, 36, 2, s["wzr"], flags)
-
-    def keep(xi, z):
-        press[xi + 1, 0:32, 0:128] = z
-
-    local_solve(window, s["mask"], s["za"], s["zb"], flags, None, keep)
-    start_xy("pxy", press, 3, s["pys"], s["pyr"], s["per"])
 
     gs = s["gs"]
     gs[...] = jnp.zeros((128, 128), F32)
@@ -602,68 +620,72 @@
     hidden_gradient(dout, s["wp"], s["back"])
     gs[81:82, :] = norm_backward(s["back"], s["cen"], gain, rstd, s["dn"])
     first_gradient(sel, s["mx"], s["dn"], gs)
+    start_group("s1", lambda j: gs.at[small_rows(a_ranks[j])], lambda j: s["r1s"].at[j], a_peers)
+
+    arrive("wz")
+    unpack_z(window, 36, 2, s["wzr"], flags)
+
+    def keep(xi, z):
+        press[xi + 1, 0:32, 0:128] = z
+
+    local_solve(window, s["mask"], s["za"], s["zb"], flags, None, keep)
+    start_xy("pxy", press, 3, s["pys"], s["pyr"], s["per"])
+
+    arrive_group("g1", s["r1"].at[1:OWNERS], c_peers)
+    total = s["gb"][tap_rows(c), :].astype(F32)
+    for j in range(1, OWNERS):
+        total = total + s["r1"][j].astype(F32)
+    s["parts"][z] = total.astype(BF16)
+    start_group("g2", lambda j: s["parts"].at[z], lambda j: s["parts"].at[z], z_peers)
+
+    arrive_group("s1", s["r1s"].at[1:RANKS], a_peers)
+    small = gs[small_rows(a), :]
     for j in range(1, RANKS):
-        rows = pl.ds(pl.multiple_of(a_ranks[j] * SMALL, 8), SMALL)
-        start("s1", j, gs.at[rows], s["r1s"].at[j], a_peers[j])
-
-    arrive("g1")
-    big = s["gb"][pl.ds(pl.multiple_of(a * BIG, 16), BIG), :].astype(F32)
-    for j in range(1, RANKS):
-        big = big + s["r1"][j].astype(F32)
-    part = s["part"]
-    part[0:14] = big.reshape(14, 8, 128)
-    part[14:16] = jnp.zeros((2, 8, 128), F32)
-    for j in range(1, RANKS):
-        start("g2", j, part.at[b_ranks[j]], s["r2"].at[j], b_peers[j])
+        small = small + s["r1s"][j]
+    s["r2s"][b] = small
+    start_group("s2", lambda j: s["r2s"].at[b], lambda j: s["r2s"].at[b], b_peers)
+    pred_ref[...] = dot(stress.astype(BF16), cell_order(), 0, 0)[0:8]
+
+    arrive_group("g2", s["parts"].at[0:7], z_peers)
+    total = s["parts"][0].astype(F32)
+    for q in range(1, 8):
+        total = total + s["parts"][q].astype(F32)
+    gathered = s["gathered"]
+    gathered[c] = total.astype(BF16)
+    start_group("g3", lambda j: gathered.at[c], lambda j: gathered.at[c], c_peers)
 
     arrive("pxy", True)
     unpack_xy(press, 3, s["pyr"], s["per"], flags)
     pack_z(press, 38, 3, s["pzs"])
     start_z("pz", s["pzs"], s["pzr"])
 
-    arrive("s1")
-    small = gs[pl.ds(pl.multiple_of(a * SMALL, 8), SMALL), :]
-    for j in range(1, RANKS):
-        small = small + s["r1s"][j]
-    s["r2s"][b] = small
-    for j in range(1, RANKS):
-        start("s2", j, s["r2s"].at[b], s["r2s"].at[b], b_peers[j])
-
-    arrive("g2")
-    total = part[b]
-    for j in range(1, RANKS):
-        total = total + s["r2"][j]
-    s["whole"][b] = total
-    for j in range(1, RANKS):
-        start("g3", j, s["whole"].at[b], s["whole"].at[b], b_peers[j])
-
-    arrive("pz")
-    unpack_z(press, 38, 3, s["pzr"], flags)
-
-    def finish(xi, z):
-        pressure_ref[xi - 2] = press[xi + 1, 0:32, 0:128] + z
-
-    local_solve(window, s["mask"], s["za"], s["zb"], flags, press, finish)
-
-    arrive("s2")
+    arrive_group("s2", s["r2s"].at[0:15], b_peers)
     small = s["r2s"][0]
     for q in range(1, RANKS):
         small = small + s["r2s"][q]
     s["gathered_s"][a] = small
-    for j in range(1, RANKS):
-        start("s3", j, s["gathered_s"].at[a], s["gathered_s"].at[a], a_peers[j])
-
-    arrive("g3")
-    gathered = s["gathered"]
-    gathered[a] = s["whole"][0:14].reshape(BIG, 128).astype(BF16)
-    for j in range(1, RANKS):
-        start("g4", j, gathered.at[a], gathered.at[a], a_peers[j])
-    arrive("s3")
+    start_group("s3", lambda j: s["gathered_s"].at[a], lambda j: s["gathered_s"].at[a], a_peers)
+
+    arrive("pz")
+    unpack_z(press, 38, 3, s["pzr"], flags)
+
+    def finish(xi, z):
+        s["done"][xi - 2] = press[xi + 1, 0:32, 0:128] + z
+
+    local_solve(window, s["mask"], s["za"], s["zb"], flags, press, finish)
+    store_pressure = pltpu.make_async_copy(s["done"], pressure_ref, local_sem.at[2])
+    store_pressure.start()
+
+    arrive_group("g3", gathered.at[0 : OWNERS - 1], c_peers)
+    store_gradient = pltpu.make_async_copy(gathered.at[0:TAPS], grad_ref, local_sem.at[3])
+    store_gradient.start()
+    arrive_group("s3", s["gathered_s"].at[0:15], a_peers)
     small_ref[...] = s["gathered_s"][...].reshape(RANKS * SMALL, 128)
-    arrive("g4")
-    grad_ref[...] = gathered[...]
-    for copy in started:
-        copy.wait_send()
+    for copies in flights.values():
+        for copy in copies:
+            copy.wait_send()
+    store_pressure.wait()
+    store_gradient.wait()
 
 
 def finish_kernel(
@@ -672,12 +694,11 @@
     pressure_out[0] = pressure_in[...]
     for k in range(6):
         pred_out[0, :, lanes(k, 512)] = pred_in[k : k + 1, :].astype(BF16)
-    flat = grad_in[...].reshape(RANKS * BIG, 128)
     for kx in range(3):
         for ky in range(3):
             for kz in range(3):
                 k = (kx * 3 + ky) * 3 + kz
-                second[kx, ky, kz] = flat[k * 64 : (k + 1) * 64].astype(F32)
+                second[kx, ky, kz] = grad_in[k].astype(F32)
                 first[kx, ky, kz] = small_in[k * 3 : k * 3 + 3, 0:64]
     gain[...] = small_in[81:82, 0:64]
     head[...] = small_in[82:88, :]
@@ -695,19 +716,19 @@
 ):
     vmem = pl.BlockSpec(memory_space=pltpu.VMEM)
     smem = pl.BlockSpec(memory_space=pltpu.SMEM)
-    semaphores = 16 * len(STEPS)
+    anywhere = pl.BlockSpec(memory_space=pl.ANY)
     pressure, stress, grads, small = pl.pallas_call(
         kernel,
         out_shape=[
             jax.ShapeDtypeStruct((32, 32, 128), F32),
             jax.ShapeDtypeStruct((8, 512), F32),
-            jax.ShapeDtypeStruct((RANKS, BIG, 128), BF16),
+            jax.ShapeDtypeStruct((TAPS, BIG, 128), BF16),
             jax.ShapeDtypeStruct((RANKS * SMALL, 128), F32),
         ],
-        in_specs=[smem, smem] + [vmem] * 6,
-        out_specs=[vmem] * 4,
+        in_specs=[smem, smem, anywhere, vmem, vmem, anywhere, vmem, vmem],
+        out_specs=[anywhere, vmem, anywhere, vmem],
         scratch_shapes=[pltpu.VMEM(shape, kind) for shape, kind in SCRATCH.values()]
-        + [pltpu.SemaphoreType.DMA((semaphores,))] * 2,
+        + [pltpu.SemaphoreType.DMA((n,)) for n in (SEMAPHORES, SEMAPHORES, 4)],
         compiler_params=pltpu.CompilerParams(
             collective_id=0, has_side_effects=True, vmem_limit_bytes=56 << 20
         ),

time: 73.8 us -> 64.9 us (0.88)
  Pallas kernels: 72.4 us -> 63.4 us
    pallas_call x1, Pallas kernels: 70 us -> 61.1 us  [shards(): pl.pallas_call(kernel, out_shape=[jax.ShapeDtypeStruct((32, 32, 128), F32...]
where the time goes in v4:
time: 64.9 us; the launch traced here: 64.7 us
  Pallas kernels  63.4 us (98%)
  between operations  1.29 us (2%)
    pallas_call x1, Pallas kernels, shards(): pl.pallas_call(kernel, out_shape=[jax.ShapeDtypeStruct((32, 32, 128), F32...  61.1 us
    pallas_call x1, Pallas kernels, shards(): pl.pallas_call(finish_kernel, out_shape=[jax.ShapeDtypeStruct((1, 32, 32,...  2.35 us

profile of v4, /device:TPU:1, one launch (start us, length us, event | category | flops | bytes accessed | tf_op | source)
XLA Modules:
  0.0 64.7 jit_solution(14884665601043776700)
XLA Ops:
  1.3 61.1 %shard_map.127 = (f32[32,32,128]{2,1,0:T(8,128)}, f32[8,512]{1,0:T(8,128)}, bf16[27,64,128]{2,1,0:T(8,128)(2,1)}, f32[128,128]{1,0:T(8,128)}) custom-call(s32[1,1]{1,0:T(1,128)S(6)} %copy.14.refs_0_, s32[256]{0:T(256)} %bitcast.6, f32[1,3,32,32,128]{4,3,2,1,0:T(8,128)} %refs_2_.1, bf16[3,3,3,3,64]{4,3,2,1,0:T(4,128)(2,1)} %refs_3_.1, f32[1,64]{1,0:T(1,128)} %bitcast.7, ...), custom_call_target="tpu_custom_call" | custom-call | tf_op jit(solution)/shard_map/pallas_call | solution.py:720
  62.4 2.3 %shard_map.128 = (f32[1,32,32,128]{3,2,1,0:T(8,128)}, bf16[1,1,3072]{2,1,0:T(2,128)(2,1)}, f32[3,3,3,3,64]{4,3,2,1,0:T(4,128)}, f32[1,64]{1,0:T(1,128)}, f32[3,3...) custom-call(f32[32,32,128]{2,1,0:T(8,128)} %get-tuple-element.16.pressure_in, f32[8,512]{1,0:T(8,128)} %get-tuple-element.17.pred_in, ...), custom_call_target="tpu_custom_call" | custom-call | tf_op jit(solution)/shard_map/pallas_call | solution.py:745

commit v5 on v4

--- a/solution.py
+++ b/solution.py
@@ -13,7 +13,7 @@
 OWNERS = 32
 TAPS = 27
 BIG = 64
-SMALL = 8
+SMALL = 2
 
 
 def iota(shape, dim):
@@ -290,25 +290,24 @@
     send[...] = packed
 
 
-def pack_y(field, h, send):
+def pack_xy(field, h, send_x, send_y):
+    send_x[0] = field[32 : 32 + h, 0:32, 0:128].astype(BF16)
+    send_x[1] = field[h : 2 * h, 0:32, 0:128].astype(BF16)
     for r in range(h):
-        send[0, r] = field[h : h + 32, 32 - h + r, 0:128]
-        send[1, r] = field[h : h + 32, r, 0:128]
-
-
-def unpack_xy(field, h, got, edges, flags):
-    if flags is not None:
-        field[0:h, 0:32, 0:128] = field[0:h, 0:32, 0:128] * flags[0]
-        field[h + 32 :, 0:32, 0:128] = field[h + 32 :, 0:32, 0:128] * flags[1]
-    else:
-        flags = [1.0] * 6
+        send_y[0, r] = field[h : h + 32, 32 - h + r, 0:128].astype(BF16)
+        send_y[1, r] = field[h : h + 32, r, 0:128].astype(BF16)
+
+
+def unpack_xy(field, h, got_x, got_y, edges, flags):
+    field[0:h, 0:32, 0:128] = got_x[0].astype(F32) * flags[0]
+    field[h + 32 : h + 32 + h, 0:32, 0:128] = got_x[1].astype(F32) * flags[1]
     for side, at in ((0, 40 - h), (1, 32)):
         for r in range(h):
             row = at + r
-            field[h : h + 32, row, 0:128] = got[side, r] * flags[2 + side]
-            for end, low, take in ((0, 0, 8 - h), (1, h + 32, 0)):
+            field[h : h + 32, row, 0:128] = got_y[side, r].astype(F32) * flags[2 + side]
+            for end, low, take in ((0, 0, 16 - h), (1, h + 32, 0)):
                 both = flags[2 + side] * flags[end]
-                strip = edges[end * 2 + side, r] * both
+                strip = edges[end * 2 + side, r].astype(F32) * both
                 for k in range(h):
                     field[low + k, row : row + 1, 0:128] = strip[take + k : take + k + 1]
 
@@ -322,13 +321,15 @@
         own = field[x, :, 0:128]
         high = jnp.where(here, pltpu.roll(own, (x * h + h) % 128, 1), high)
         low = jnp.where(here, pltpu.roll(own, x * h, 1) if x else own, low)
-    send[0] = high
-    send[1] = low
+    rest = jnp.zeros((8, 128), F32)
+    send[0] = jnp.concatenate([high, rest], axis=0).astype(BF16)
+    send[1] = jnp.concatenate([low, rest], axis=0).astype(BF16)
 
 
 def unpack_z(field, count, h, got, flags):
     lane = iota((40, 128), 1)
-    below, above = got[0] * flags[4], got[1] * flags[5]
+    below = got[0, 0:40].astype(F32) * flags[4]
+    above = got[1, 0:40].astype(F32) * flags[5]
     for x in range(count):
         lower = pltpu.roll(below, (128 - h - x * h) % 128, 1)
         upper = pltpu.roll(above, (-x * h) % 128, 1) if x else above
@@ -412,10 +413,9 @@
     r1=((OWNERS, BIG, 128), BF16),
     parts=((8, BIG, 128), BF16),
     gathered=((OWNERS, BIG, 128), BF16),
-    gs=((RANKS * SMALL, 128), F32),
-    r1s=((RANKS, SMALL, 128), F32),
-    r2s=((RANKS, SMALL, 128), F32),
-    gathered_s=((RANKS, SMALL, 128), F32),
+    gs=((SMALL * BIG, 128), F32),
+    gsb=((SMALL * BIG, 128), BF16),
+    r1s=((OWNERS, BIG, 128), BF16),
     rim_x=((32, 128), F32),
     rim_y=((32, 128), F32),
     rim_z=((32, 128), F32),
@@ -426,27 +426,31 @@
     za=((38, 40, 256), F32),
     zb=((38, 40, 256), F32),
     mask=((40, 256), F32),
-    wys=((2, 2, 32, 128), F32),
-    wyr=((2, 2, 32, 128), F32),
-    wer=((4, 2, 8, 128), F32),
-    wzs=((2, 40, 128), F32),
-    wzr=((2, 40, 128), F32),
-    pys=((2, 3, 32, 128), F32),
-    pyr=((2, 3, 32, 128), F32),
-    per=((4, 3, 8, 128), F32),
-    pzs=((2, 40, 128), F32),
-    pzr=((2, 40, 128), F32),
+    wxs=((2, 2, 32, 128), BF16),
+    wxr=((2, 2, 32, 128), BF16),
+    wys=((2, 2, 32, 128), BF16),
+    wyr=((2, 2, 32, 128), BF16),
+    wer=((4, 2, 16, 128), BF16),
+    wzs=((2, 48, 128), BF16),
+    wzr=((2, 48, 128), BF16),
+    pxs=((2, 3, 32, 128), BF16),
+    pxr=((2, 3, 32, 128), BF16),
+    pys=((2, 3, 32, 128), BF16),
+    pyr=((2, 3, 32, 128), BF16),
+    per=((4, 3, 16, 128), BF16),
+    pzs=((2, 48, 128), BF16),
+    pzr=((2, 48, 128), BF16),
 )
-GROUP_STEPS = ("t1", "t2", "g1", "g2", "g3", "s1", "s2", "s3")
+GROUP_STEPS = ("t1", "t2", "g1", "g2", "g3", "s0", "s1")
 HALO_STEPS = ("rim", "wxy", "wz", "pxy", "pz")
 SEMAPHORES = len(GROUP_STEPS) + 8 * len(HALO_STEPS)
 
 
 def kernel(*refs):
     (sel_ref, asg_ref, vel_hbm, w1_ref, gain_ref, w2_hbm, head_ref, target_ref) = refs[:8]
-    pressure_ref, pred_ref, grad_ref, small_ref = refs[8:12]
-    s = dict(zip(SCRATCH, refs[12 : 12 + len(SCRATCH)]))
-    send_sem, recv_sem, local_sem = refs[12 + len(SCRATCH) :]
+    pressure_ref, pred_ref, grad_ref = refs[8:11]
+    s = dict(zip(SCRATCH, refs[11 : 11 + len(SCRATCH)]))
+    send_sem, recv_sem, local_sem = refs[11 + len(SCRATCH) :]
     vel_ref = s["vel"]
     load_velocity = pltpu.make_async_copy(vel_hbm.at[0], vel_ref, local_sem.at[0])
     load_velocity.start()
@@ -520,25 +524,18 @@
         every.wait_recv()
         flights[step] = [every]
 
-    def arrive(step, sent=False):
+    def arrive(step):
         for copy in flights[step]:
             copy.wait_recv()
-            if sent:
-                copy.wait_send()
-        if sent:
-            del flights[step]
-
-    def start_xy(step, field, h, send, got, edges):
-        low, high = slice(0, 32), slice(0, 128)
-        start(step, 0, field.at[32 : 32 + h, low, high], field.at[0:h, low, high], above[0])
-        start(
-            step, 1, field.at[h : 2 * h, low, high], field.at[32 + h : 32 + 2 * h, low, high], below[0]
-        )
-        pack_y(field, h, send)
-        start(step, 2, send.at[0], got.at[0], above[1])
-        start(step, 3, send.at[1], got.at[1], below[1])
-        for k, (side, at) in enumerate(((0, 24), (1, 24), (0, 0), (1, 0))):
-            start(step, 4 + k, send.at[side, :, at : at + 8, :], edges.at[k], corners[k])
+
+    def start_xy(step, field, h, send_x, got_x, send_y, got_y, edges):
+        pack_xy(field, h, send_x, send_y)
+        for k, (side, at) in enumerate(((0, 16), (1, 16), (0, 0), (1, 0))):
+            start(step, 4 + k, send_y.at[side, :, at : at + 16, :], edges.at[k], corners[k])
+        start(step, 2, send_y.at[0], got_y.at[0], above[1])
+        start(step, 3, send_y.at[1], got_y.at[1], below[1])
+        start(step, 0, send_x.at[0], got_x.at[0], above[0])
+        start(step, 1, send_x.at[1], got_x.at[1], below[0])
 
     def start_z(step, send, got):
         start(step, 0, send.at[0], got.at[0], above[2])
@@ -552,6 +549,7 @@
         s["rows"][r : r + 1, :] = flat[:, lanes(r)]
     s["t0"][...] = s["rows"][...].astype(BF16)
     s["t1"][a] = s["t0"][...]
+    build_first_weights(sel, w1_ref, s["wg"], s["table"])
     load_velocity.wait()
     pack_rim_z(vel_ref, s["rim_zs"])
     s["rim_ys"][...] = vel_ref[1, :, 31, :]
@@ -563,7 +561,6 @@
     start("rim", 1, s["rim_ys"], s["rim_y"], above[1])
     start("rim", 2, s["rim_zs"], s["rim_z"], above[2])
 
-    build_first_weights(sel, w1_ref, s["wg"], s["table"])
     build_rows(sel, vel_ref, s["mx"])
     s["mask"][...] = cell_masks(coords)
     window[:, 32:40, 0:128] = jnp.zeros((36, 8, 128), F32)
@@ -580,7 +577,7 @@
     s["t2"][b] = s["stage"][b]
     arrive("rim")
     divergence(vel_ref, s["rim_x"], s["rim_y"], s["rim_z"], flags, window)
-    start_xy("wxy", window, 2, s["wys"], s["wyr"], s["wer"])
+    start_xy("wxy", window, 2, s["wxs"], s["wxr"], s["wys"], s["wyr"], s["wer"])
 
     first_layer(s["mx"], s["table"], s["cen"])
     gain, rstd = normalise(s["cen"], gain_ref)
@@ -602,17 +599,23 @@
     def tap_rows(rank):
         return pl.ds(pl.multiple_of(rank * BIG, BIG), BIG)
 
-    def small_rows(rank):
-        return pl.ds(pl.multiple_of(rank * SMALL, SMALL), SMALL)
-
     start_group(
         "g1", lambda j: s["gb"].at[tap_rows(c_ranks[j])], lambda j: s["r1"].at[j], c_peers
     )
 
-    arrive("wxy", True)
-    unpack_xy(window, 2, s["wyr"], s["wer"], None)
+    arrive("wxy")
+    unpack_xy(window, 2, s["wxr"], s["wyr"], s["wer"], flags)
     pack_z(window, 36, 2, s["wzs"])
     start_z("wz", s["wzs"], s["wzr"])
+
+    arrive("wz")
+    unpack_z(window, 36, 2, s["wzr"], flags)
+
+    def keep(xi, z):
+        press[xi + 1, 0:32, 0:128] = z
+
+    local_solve(window, s["mask"], s["za"], s["zb"], flags, None, keep)
+    start_xy("pxy", press, 3, s["pxs"], s["pxr"], s["pys"], s["pyr"], s["per"])
 
     gs = s["gs"]
     gs[...] = jnp.zeros((128, 128), F32)
@@ -620,31 +623,51 @@
     hidden_gradient(dout, s["wp"], s["back"])
     gs[81:82, :] = norm_backward(s["back"], s["cen"], gain, rstd, s["dn"])
     first_gradient(sel, s["mx"], s["dn"], gs)
-    start_group("s1", lambda j: gs.at[small_rows(a_ranks[j])], lambda j: s["r1s"].at[j], a_peers)
-
-    arrive("wz")
-    unpack_z(window, 36, 2, s["wzr"], flags)
-
-    def keep(xi, z):
-        press[xi + 1, 0:32, 0:128] = z
-
-    local_solve(window, s["mask"], s["za"], s["zb"], flags, None, keep)
-    start_xy("pxy", press, 3, s["pys"], s["pyr"], s["per"])
+    s["gsb"][...] = gs[...].astype(BF16)
+    small_copies = []
+    for n in range(SMALL):
+        owner = TAPS + n
+        rows = slice(n * BIG, (n + 1) * BIG)
+        copy = pltpu.make_async_remote_copy(
+            src_ref=s["gsb"].at[rows],
+            dst_ref=s["r1s"].at[c],
+            send_sem=send_sem.at[GROUP_STEPS.index("s0") + n],
+            recv_sem=recv_sem.at[GROUP_STEPS.index("s0")],
+            device_id=device(owner // 2 * 16 + z * 2 + owner % 2),
+            device_id_type=MESH,
+        )
+        small_copies.append((owner, copy))
+
+        @pl.when(c != owner)
+        def _(copy=copy):
+            copy.start()
+
+        @pl.when(c == owner)
+        def _(rows=rows):
+            s["r1s"][c] = s["gsb"][rows, :]
 
     arrive_group("g1", s["r1"].at[1:OWNERS], c_peers)
     total = s["gb"][tap_rows(c), :].astype(F32)
     for j in range(1, OWNERS):
         total = total + s["r1"][j].astype(F32)
     s["parts"][z] = total.astype(BF16)
+
+    @pl.when((c == TAPS) | (c == TAPS + 1))
+    def _():
+        slots = s["r1s"].at[0 : OWNERS - 1]
+        remote(GROUP_STEPS.index("s0"), slots, slots, c_peers[1]).wait_recv()
+        total = s["r1s"][0].astype(F32)
+        for q in range(1, OWNERS):
+            total = total + s["r1s"][q].astype(F32)
+        s["parts"][z] = total.astype(BF16)
+
     start_group("g2", lambda j: s["parts"].at[z], lambda j: s["parts"].at[z], z_peers)
-
-    arrive_group("s1", s["r1s"].at[1:RANKS], a_peers)
-    small = gs[small_rows(a), :]
-    for j in range(1, RANKS):
-        small = small + s["r1s"][j]
-    s["r2s"][b] = small
-    start_group("s2", lambda j: s["r2s"].at[b], lambda j: s["r2s"].at[b], b_peers)
     pred_ref[...] = dot(stress.astype(BF16), cell_order(), 0, 0)[0:8]
+
+    arrive("pxy")
+    unpack_xy(press, 3, s["pxr"], s["pyr"], s["per"], flags)
+    pack_z(press, 38, 3, s["pzs"])
+    start_z("pz", s["pzs"], s["pzr"])
 
     arrive_group("g2", s["parts"].at[0:7], z_peers)
     total = s["parts"][0].astype(F32)
@@ -654,18 +677,6 @@
     gathered[c] = total.astype(BF16)
     start_group("g3", lambda j: gathered.at[c], lambda j: gathered.at[c], c_peers)
 
-    arrive("pxy", True)
-    unpack_xy(press, 3, s["pyr"], s["per"], flags)
-    pack_z(press, 38, 3, s["pzs"])
-    start_z("pz", s["pzs"], s["pzr"])
-
-    arrive_group("s2", s["r2s"].at[0:15], b_peers)
-    small = s["r2s"][0]
-    for q in range(1, RANKS):
-        small = small + s["r2s"][q]
-    s["gathered_s"][a] = small
-    start_group("s3", lambda j: s["gathered_s"].at[a], lambda j: s["gathered_s"].at[a], a_peers)
-
     arrive("pz")
     unpack_z(press, 38, 3, s["pzr"], flags)
 
@@ -677,20 +688,27 @@
     store_pressure.start()
 
     arrive_group("g3", gathered.at[0 : OWNERS - 1], c_peers)
-    store_gradient = pltpu.make_async_copy(gathered.at[0:TAPS], grad_ref, local_sem.at[3])
+    store_gradient = pltpu.make_async_copy(
+        gathered.at[0 : TAPS + SMALL], grad_ref, local_sem.at[3]
+    )
     store_gradient.start()
-    arrive_group("s3", s["gathered_s"].at[0:15], a_peers)
-    small_ref[...] = s["gathered_s"][...].reshape(RANKS * SMALL, 128)
     for copies in flights.values():
         for copy in copies:
             copy.wait_send()
+    for owner, copy in small_copies:
+
+        @pl.when(c != owner)
+        def _(copy=copy):
+            copy.wait_send()
+
     store_pressure.wait()
     store_gradient.wait()
 
 
 def finish_kernel(
-    pressure_in, pred_in, grad_in, small_in, pressure_out, pred_out, first, gain, second, head
+    pressure_in, pred_in, grad_in, pressure_out, pred_out, first, gain, second, head, small_in
 ):
+    small_in[...] = grad_in[TAPS : TAPS + SMALL].reshape(SMALL * BIG, 128).astype(F32)
     pressure_out[0] = pressure_in[...]
     for k in range(6):
         pred_out[0, :, lanes(k, 512)] = pred_in[k : k + 1, :].astype(BF16)
@@ -717,16 +735,15 @@
     vmem = pl.BlockSpec(memory_space=pltpu.VMEM)
     smem = pl.BlockSpec(memory_space=pltpu.SMEM)
     anywhere = pl.BlockSpec(memory_space=pl.ANY)
-    pressure, stress, grads, small = pl.pallas_call(
+    pressure, stress, grads = pl.pallas_call(
         kernel,
         out_shape=[
             jax.ShapeDtypeStruct((32, 32, 128), F32),
             jax.ShapeDtypeStruct((8, 512), F32),
-            jax.ShapeDtypeStruct((TAPS, BIG, 128), BF16),
-            jax.ShapeDtypeStruct((RANKS * SMALL, 128), F32),
+            jax.ShapeDtypeStruct((TAPS + SMALL, BIG, 128), BF16),
         ],
         in_specs=[smem, smem, anywhere, vmem, vmem, anywhere, vmem, vmem],
-        out_specs=[anywhere, vmem, anywhere, vmem],
+        out_specs=[anywhere, vmem, anywhere],
         scratch_shapes=[pltpu.VMEM(shape, kind) for shape, kind in SCRATCH.values()]
         + [pltpu.SemaphoreType.DMA((n,)) for n in (SEMAPHORES, SEMAPHORES, 4)],
         compiler_params=pltpu.CompilerParams(
@@ -752,9 +769,10 @@
             jax.ShapeDtypeStruct((3, 3, 3, 64, 128), F32),
             jax.ShapeDtypeStruct((6, 128), F32),
         ],
-        in_specs=[vmem] * 4,
+        in_specs=[vmem] * 3,
         out_specs=[vmem] * 6,
-    )(pressure, stress, grads, small)
+        scratch_shapes=[pltpu.VMEM((SMALL * BIG, 128), F32)],
+    )(pressure, stress, grads)
     return (pressure, predicted, first, gain.reshape(64), second, head.T)
 
 

time: 64.9 us -> 61.5 us (0.948)
  Pallas kernels: 63.4 us -> 60 us
    pallas_call x1, Pallas kernels: 61.1 us -> 57.7 us  [shards(): pl.pallas_call(kernel, out_shape=[jax.ShapeDtypeStruct((32, 32, 128), F32...]
where the time goes in v5:
time: 61.5 us; the launch traced here: 61.3 us
  Pallas kernels  60 us (98%)
  between operations  1.29 us (2%)
    pallas_call x1, Pallas kernels, shards(): pl.pallas_call(kernel, out_shape=[jax.ShapeDtypeStruct((32, 32, 128), F32...  57.7 us
    pallas_call x1, Pallas kernels, shards(): pl.pallas_call(finish_kernel, out_shape=[jax.ShapeDtypeStruct((1, 32, 32,...  2.36 us

profile of v5, /device:TPU:1, one launch (start us, length us, event | category | flops | bytes accessed | tf_op | source)
XLA Modules:
  0.0 61.3 jit_solution(15421785134565222593)
XLA Ops:
  1.3 57.7 %shard_map.127 = (f32[32,32,128]{2,1,0:T(8,128)}, f32[8,512]{1,0:T(8,128)}, bf16[29,64,128]{2,1,0:T(8,128)(2,1)}) custom-call(s32[1,1]{1,0:T(1,128)S(6)} %copy.14.refs_0_, s32[256]{0:T(256)} %bitcast.6, f32[1,3,32,32,128]{4,3,2,1,0:T(8,128)} %refs_2_.1, bf16[3,3,3,3,64]{4,3,2,1,0:T(4,128)(2,1)} %refs_3_.1, f32[1,64]{1,0:T(1,128)} %bitcast.7, ...), custom_call_target="tpu_custom_call" | custom-call | tf_op jit(solution)/shard_map/pallas_call | solution.py:738
  59.0 2.4 %shard_map.128 = (f32[1,32,32,128]{3,2,1,0:T(8,128)}, bf16[1,1,3072]{2,1,0:T(2,128)(2,1)}, f32[3,3,3,3,64]{4,3,2,1,0:T(4,128)}, f32[1,64]{1,0:T(1,128)}, f32[3,3...) custom-call(f32[32,32,128]{2,1,0:T(8,128)} %get-tuple-element.15.pressure_in, f32[8,512]{1,0:T(8,128)} %get-tuple-element.16.pred_in, ...), custom_call_target="tpu_custom_call" | custom-call | tf_op jit(solution)/shard_map/pallas_call | solution.py:762

commit v6 on v5

--- a/solution.py
+++ b/solution.py
@@ -290,7 +290,13 @@
     send[...] = packed
 
 
-def pack_xy(field, h, send_x, send_y):
+def pack_xy(field, h, send_x, send_y, send_e, edge):
+    for k, (x, y) in enumerate(((32, 32 - h), (32, 0), (h, 32 - h), (h, 0))):
+        edge[...] = jnp.zeros((16, 128), F32)
+        for r in range(h):
+            for m in range(h):
+                edge[r * h + m : r * h + m + 1, :] = field[x + m, y + r : y + r + 1, 0:128]
+        send_e[k] = edge[...].astype(BF16)
     send_x[0] = field[32 : 32 + h, 0:32, 0:128].astype(BF16)
     send_x[1] = field[h : 2 * h, 0:32, 0:128].astype(BF16)
     for r in range(h):
@@ -305,11 +311,11 @@
         for r in range(h):
             row = at + r
             field[h : h + 32, row, 0:128] = got_y[side, r].astype(F32) * flags[2 + side]
-            for end, low, take in ((0, 0, 16 - h), (1, h + 32, 0)):
+            for end, low in ((0, 0), (1, h + 32)):
                 both = flags[2 + side] * flags[end]
-                strip = edges[end * 2 + side, r].astype(F32) * both
+                strip = edges[end * 2 + side].astype(F32) * both
                 for k in range(h):
-                    field[low + k, row : row + 1, 0:128] = strip[take + k : take + k + 1]
+                    field[low + k, row : row + 1, 0:128] = strip[r * h + k : r * h + k + 1]
 
 
 def pack_z(field, count, h, send):
@@ -347,9 +353,7 @@
 
 def local_solve(window, mask, za, zb, flags, pressure, emit):
     def inside(xi):
-        if isinstance(xi, int):
-            return flags[0] if xi < 2 else flags[1] if xi > 33 else 1.0
-        return jnp.where(xi < 2, flags[0], jnp.where(xi > 33, flags[1], 1.0))
+        return flags[0] if xi < 2 else flags[1] if xi > 33 else 1.0
 
     for z in (za, zb):
         z[0] = jnp.zeros((40, 256), F32)
@@ -376,14 +380,8 @@
         emit(xi, z[0:32, 0:128])
 
     def over(low, high, body):
-        half = (high - low) // 2
-
-        def both(m, carry):
-            for k in range(half):
-                body(low + m * half + k)
-            return carry
-
-        lax.fori_loop(0, 2, both, 0)
+        for xi in range(low, high):
+            body(xi)
 
     over(0, 36, first)
     over(0, 36, sweep(za, zb))
@@ -426,18 +424,21 @@
     za=((38, 40, 256), F32),
     zb=((38, 40, 256), F32),
     mask=((40, 256), F32),
+    edge=((16, 128), F32),
     wxs=((2, 2, 32, 128), BF16),
     wxr=((2, 2, 32, 128), BF16),
     wys=((2, 2, 32, 128), BF16),
     wyr=((2, 2, 32, 128), BF16),
-    wer=((4, 2, 16, 128), BF16),
+    wes=((4, 16, 128), BF16),
+    wer=((4, 16, 128), BF16),
     wzs=((2, 48, 128), BF16),
     wzr=((2, 48, 128), BF16),
     pxs=((2, 3, 32, 128), BF16),
     pxr=((2, 3, 32, 128), BF16),
     pys=((2, 3, 32, 128), BF16),
     pyr=((2, 3, 32, 128), BF16),
-    per=((4, 3, 16, 128), BF16),
+    pes=((4, 16, 128), BF16),
+    per=((4, 16, 128), BF16),
     pzs=((2, 48, 128), BF16),
     pzr=((2, 48, 128), BF16),
 )
@@ -528,10 +529,10 @@
         for copy in flights[step]:
             copy.wait_recv()
 
-    def start_xy(step, field, h, send_x, got_x, send_y, got_y, edges):
-        pack_xy(field, h, send_x, send_y)
-        for k, (side, at) in enumerate(((0, 16), (1, 16), (0, 0), (1, 0))):
-            start(step, 4 + k, send_y.at[side, :, at : at + 16, :], edges.at[k], corners[k])
+    def start_xy(step, field, h, send_x, got_x, send_y, got_y, send_e, edges):
+        pack_xy(field, h, send_x, send_y, send_e, s["edge"])
+        for k in range(4):
+            start(step, 4 + k, send_e.at[k], edges.at[k], corners[k])
         start(step, 2, send_y.at[0], got_y.at[0], above[1])
         start(step, 3, send_y.at[1], got_y.at[1], below[1])
         start(step, 0, send_x.at[0], got_x.at[0], above[0])
@@ -577,7 +578,9 @@
     s["t2"][b] = s["stage"][b]
     arrive("rim")
     divergence(vel_ref, s["rim_x"], s["rim_y"], s["rim_z"], flags, window)
-    start_xy("wxy", window, 2, s["wxs"], s["wxr"], s["wys"], s["wyr"], s["wer"])
+    start_xy(
+        "wxy", window, 2, s["wxs"], s["wxr"], s["wys"], s["wyr"], s["wes"], s["wer"]
+    )
 
     first_layer(s["mx"], s["table"], s["cen"])
     gain, rstd = normalise(s["cen"], gain_ref)
@@ -615,7 +618,9 @@
         press[xi + 1, 0:32, 0:128] = z
 
     local_solve(window, s["mask"], s["za"], s["zb"], flags, None, keep)
-    start_xy("pxy", press, 3, s["pxs"], s["pxr"], s["pys"], s["pyr"], s["per"])
+    start_xy(
+        "pxy", press, 3, s["pxs"], s["pxr"], s["pys"], s["pyr"], s["pes"], s["per"]
+    )
 
     gs = s["gs"]
     gs[...] = jnp.zeros((128, 128), F32)

time: 61.5 us -> 59.2 us (0.963)
  Pallas kernels: 60 us -> 57.8 us
    pallas_call x1, Pallas kernels: 57.7 us -> 55.4 us  [shards(): pl.pallas_call(kernel, out_shape=[jax.ShapeDtypeStruct((32, 32, 128), F32...]
where the time goes in v6:
time: 59.2 us; the launch traced here: 59.1 us
  Pallas kernels  57.8 us (98%)
  between operations  1.29 us (2%)
    pallas_call x1, Pallas kernels, shards(): pl.pallas_call(kernel, out_shape=[jax.ShapeDtypeStruct((32, 32, 128), F32...  55.4 us
    pallas_call x1, Pallas kernels, shards(): pl.pallas_call(finish_kernel, out_shape=[jax.ShapeDtypeStruct((1, 32, 32,...  2.36 us

profile of v6, /device:TPU:1, one launch (start us, length us, event | category | flops | bytes accessed | tf_op | source)
XLA Modules:
  0.0 59.1 jit_solution(2249758576390992277)
XLA Ops:
  1.3 55.4 %shard_map.127 = (f32[32,32,128]{2,1,0:T(8,128)}, f32[8,512]{1,0:T(8,128)}, bf16[29,64,128]{2,1,0:T(8,128)(2,1)}) custom-call(s32[1,1]{1,0:T(1,128)S(6)} %copy.14.refs_0_, s32[256]{0:T(256)} %bitcast.6, f32[1,3,32,32,128]{4,3,2,1,0:T(8,128)} %refs_2_.1, bf16[3,3,3,3,64]{4,3,2,1,0:T(4,128)(2,1)} %refs_3_.1, f32[1,64]{1,0:T(1,128)} %bitcast.7, ...), custom_call_target="tpu_custom_call" | custom-call | tf_op jit(solution)/shard_map/pallas_call | solution.py:743
  56.7 2.4 %shard_map.128 = (f32[1,32,32,128]{3,2,1,0:T(8,128)}, bf16[1,1,3072]{2,1,0:T(2,128)(2,1)}, f32[3,3,3,3,64]{4,3,2,1,0:T(4,128)}, f32[1,64]{1,0:T(1,128)}, f32[3,3...) custom-call(f32[32,32,128]{2,1,0:T(8,128)} %get-tuple-element.15.pressure_in, f32[8,512]{1,0:T(8,128)} %get-tuple-element.16.pred_in, ...), custom_call_target="tpu_custom_call" | custom-call | tf_op jit(solution)/shard_map/pallas_call | solution.py:767
